TPU v7x, 256 devices: a whole 4x4x8 slice. The times are simulated.
256 devices in a mesh: blk: 16 (over y, x), exc: 8 (over z), row: 2 (over core).
Axes of the slice: x: 4, y: 4, z: 8, core: 2. Of those that a mesh axis runs over, the one named last changes fastest.
Arguments:
- panels: bfloat16 [128, 3072, 128], P('blk', 'row'), may hold values from -6 to 6
- patterns: bfloat16 [128, 128, 256], P('blk', 'row'), may hold values from -6 to 6
- geometry: bfloat16 [32, 3072, 256], P('blk', 'row'), may hold values from -0.109375 to 0.109375
- excitations: bfloat16 [32, 768, 3072], P('blk', 'exc', 'row'), may hold values from -0.109375 to 0.109375
- moved_blocks: int32 [32], replicated, may hold values from 0 to 127, as said below
- partners: int32 [32, 2048], P(None, ('blk', 'exc')), may hold values from 0 to 127, as said below
- translation: float32 [32, 2048, 256], P(None, ('blk', 'exc')), may hold values from -0.375 to 0.375
Outputs:
- couplings: bfloat16 [32, 2048, 128, 128], P(None, ('blk', 'exc'), 'row')
- projections: float32 [32, 768, 128], P('blk', 'exc')
Inputs may be any that keep to these rules, and one draw needn't show every extreme that they name: `moved_blocks`: distinct blocks; at most 3 of them lie among the 8 consecutive blocks of any one group, and exactly 3 in some group. `partners`: the block in column j lies in the group of 8 consecutive blocks numbered j * 128 // 16384.
All inputs are finite; a program needn't handle non-finite values.
Results may differ from a plain program's by a relative error of at most 0.0058.
Values may be sent and summed in bfloat16 or wider, within the bound.
No kernel may reach another device: no remote copies, remote signals or barrier semaphores. Data moves between devices by JAX's collectives and lax.ppermute only.
A program may use at most 128 MiB of HBM per device.

v0:
```python
import jax
import jax.numpy as jnp
from jax import lax
from jax.sharding import PartitionSpec as P

CAP = 3


def on_device(panels, patterns, geometry, excitations, moved_blocks, partners, translation):
    blocks_here = panels.shape[0]
    my_group = lax.axis_index("blk")
    group_total = lax.axis_size("blk")
    moved_total = moved_blocks.shape[0]
    per_group = moved_total // group_total
    owners = moved_blocks // blocks_here
    local_slot = moved_blocks % blocks_here
    positions = jnp.arange(moved_total)
    earlier = (owners[None, :] == owners[:, None]) & (positions[None, :] < positions[:, None])
    rank_among = jnp.sum(earlier.astype(jnp.int32), axis=1)
    slot_ids = jnp.arange(CAP)
    picked = (owners[None, :] == my_group) & (rank_among[None, :] == slot_ids[:, None])
    slot_local = jnp.sum(jnp.where(picked, local_slot[None, :], 0), axis=1)
    filled = jnp.any(picked, axis=1)
    outgoing = jnp.where(filled[:, None, None], panels[slot_local], jnp.zeros((), panels.dtype))
    pooled = lax.all_gather(outgoing, "blk", axis=0, tiled=True)
    wanted = lax.dynamic_slice_in_dim(owners * CAP + rank_among, my_group * per_group, per_group, 0)
    arrived = pooled[wanted]
    basis_width = panels.shape[2]
    exc_share = basis_width // lax.axis_size("exc")
    columns = lax.dynamic_slice_in_dim(arrived, lax.axis_index("exc") * exc_share, exc_share, 2)
    partial_value = jnp.einsum(
        "mrl,mrp->mlp", columns, geometry, preferred_element_type=jnp.float32
    )
    projected = jnp.einsum("mer,mrl->mel", excitations, arrived, preferred_element_type=jnp.float32)
    partial_value, projected = lax.psum((partial_value, projected), "row")
    radiation = partial_value.astype(jnp.bfloat16)
    radiation = lax.all_gather(radiation, "exc", axis=1, tiled=True)
    partner_slot = partners % blocks_here
    weighted = (patterns[partner_slot] * translation[:, :, None, :]).astype(jnp.bfloat16)
    couplings = jnp.einsum(
        "mjkp,mlp->mjkl",
        weighted,
        lax.all_gather(radiation, "blk", axis=0, tiled=True),
        preferred_element_type=jnp.float32,
    ).astype(jnp.bfloat16)
    return (couplings, projected)


def solution(mesh):
    placed = (
        P("blk", "row", None),
        P("blk", "row", None),
        P("blk", "row", None),
        P("blk", "exc", "row"),
        P(),
        P(None, ("blk", "exc")),
        P(None, ("blk", "exc"), None),
    )
    return jax.shard_map(
        on_device,
        mesh=mesh,
        in_specs=placed,
        out_specs=(P(None, ("blk", "exc"), "row", None), P("blk", "exc", None)),
        check_vma=False,
    )
```

profile of v0, /device:TPU:1, one launch (start us, length us, event | category | flops | bytes accessed | tf_op | source)
XLA Modules:
  0.0 274.7 jit_solution(15033024215326220200)
XLA Ops:
  7.2 0.0 copy-start
  7.2 0.0 all-gather.3.cloned.1.call-start
  7.2 0.8 and_select_fusion
  8.0 0.8 broadcast_compare_fusion
  8.8 0.2 convert_reduce_fusion
  9.0 0.1 fusion.13
  9.1 0.1 select_reduce_fusion
  9.2 0.0 copy-done
  9.2 1.8 gather_fusion.1
  11.0 2.4 broadcast_select_fusion
  13.4 0.0 copy-start.2
  13.4 0.0 copy-start.1
  13.4 0.0 all-gather.3.cloned.1.call-update
  13.5 0.0 all-gather.5.cloned.1.call-start
  13.5 0.1 compare_select_fusion.1
  13.6 130.8 %all-gather.3.cloned.1.call-done = bf16[48,1536,128]{2,1,0:T(8,128)(2,1)} async-done(((bf16[3,1536,128]{2,1,0:T(8,128)(2,1)}), bf16[48,1536,128]{2,1,0:T(8,128)(2,1)}) %all-gather.3.cloned.1.call-update) | async-done | bytes 18874384 | tf_op jit(solution)/shard_map/all_gather | solution.py:25
  144.4 7.9 %gather_fusion.2 = bf16[2,1536,128]{2,1,0:T(8,128)(2,1)} fusion(bf16[48,1536,128]{2,1,0:T(8,128)(2,1)} %all-gather.3.cloned.1.call-done, s32[1024]{0:T(1024)S(1)} %pad_clamp_fusion), kind=kCustom, calls=%fused_computation.2 | custom fusion | bytes 1572872 | tf_op jit(solution)/shard_map/gather | solution.py:27
  152.3 2.5 fusion.8
  154.8 3.9 %psum.14 = bf16[2,16,256]{2,1,0:T(8,128)(2,1)S(1)} all-reduce(f32[2,16,256]{2,1,0:T(8,128)S(1)} %fusion.8), channel_id=1, replica_groups=mesh['blk'=16,'exc'=8,'row'=2] {'row'}, use_global_device_ids=true, to_apply=%region_3.4 | all-reduce | flops 8192 | bytes 49152 | tf_op jit(solution)/shard_map/psum | solution.py:35
  158.7 22.0 %all_gather.10 = bf16[2,128,256]{2,1,0:T(8,128)(2,1)} all-gather(bf16[2,16,256]{2,1,0:T(8,128)(2,1)S(1)} %psum.14), channel_id=1, replica_groups=mesh['blk'=16,'exc'=8,'row'=2] {'exc'}, dimensions={1}, use_global_device_ids=true | all-gather | bytes 147456 | tf_op jit(solution)/shard_map/all_gather | solution.py:37
  180.7 0.0 all-gather.5.cloned.1.call-update
  180.8 0.0 all-reduce.2.cloned.1.call-start
  180.8 0.0 copy-done.2
  180.8 0.1 copy.14
  180.9 0.1 reshape.27
  181.0 0.0 copy-done.1
  181.0 13.8 %gather_fusion = bf16[512,64,256]{2,1,0:T(8,128)(2,1)} fusion(bf16[8,64,256]{2,1,0:T(8,128)(2,1)S(1)} %copy-done.1, s32[1024]{0:T(1024)S(1)} %pad_clamp_fusion.2), kind=kCustom, calls=%fused_computation | custom fusion | bytes 33556480 | tf_op jit(solution)/shard_map/gather | solution.py:39
  194.8 2.3 convolution_bitcast_fusion
  197.1 0.0 all-reduce.2.cloned.1.call-update
  197.1 36.8 %all-gather.5.cloned.1.call-done = bf16[32,128,256]{2,1,0:T(8,128)(2,1)} async-done(((bf16[2,128,256]{2,1,0:T(8,128)(2,1)}), bf16[32,128,256]{2,1,0:T(8,128)(2,1)}) %all-gather.5.cloned.1.call-update) | async-done | bytes 2097168 | tf_op jit(solution)/shard_map/all_gather | solution.py:43
  233.9 10.8 %fusion.4 = bf16[32,16,64,128]{3,2,1,0:T(8,128)(2,1)} fusion(bf16[32,16,64,256]{3,2,1,0:T(8,128)(2,1)} %bitcast.16, f32[32,16,256]{2,1,0:T(8,128)} %param.13, bf16[32,128,256]{2,1,0:T(8,128)(2,1)} %all-gather.5.cloned.1.call-done), kind=kOutput, calls=%fused_computation.7 | convolution fusion | flops 2176843776 | bytes 27787264 | tf_op jit(solution)/shard_map/mjkp,mlp->mjkl/dot_general | solution.py:40
  244.7 21.9 %all-reduce.2.cloned.1.call-done = f32[2,96,128]{2,1,0:T(8,128)} async-done(((f32[2,96,128]{2,1,0:T(8,128)}), f32[2,96,128]{2,1,0:T(8,128)}) %all-reduce.2.cloned.1.call-update) | async-done | bytes 98320 | tf_op jit(solution)/shard_map/psum | solution.py:35
  266.6 1.5 copy.19
  (6 shorter events, 0.0 us)
Async XLA Ops:
  7.2 2.1 copy-start
  7.2 137.3 %all-gather.3.cloned.1.call-start = ((), (), s32[]{:S(2)}) async-start(), calls=%async_computation | async-start | bytes 20054016 | tf_op jit(solution)/shard_map/all_gather | solution.py:25
  13.4 167.4 %copy-start.2 = (s32[32,16]{0,1:T(8,128)S(1)}, s32[32,16]{0,1:T(8,128)}, u32[]{:S(2)}) copy-start(s32[32,16]{0,1:T(8,128)} %param.12) | copy-start | bytes 6148
  13.4 167.6 %copy-start.1 = (bf16[8,64,256]{2,1,0:T(8,128)(2,1)S(1)}, bf16[8,64,256]{2,1,0:T(8,128)(2,1)}, u32[]{:S(2)}) copy-start(bf16[8,64,256]{2,1,0:T(8,128)(2,1)} %param.8) | copy-start | bytes 786436
  13.5 220.4 %all-gather.5.cloned.1.call-start = ((), (), s32[]{:S(2)}) async-start(), calls=%async_computation.1 | async-start | bytes 2228224 | tf_op jit(solution)/shard_map/all_gather | solution.py:43
  180.8 85.9 %all-reduce.2.cloned.1.call-start = ((), (), s32[]{:S(2)}) async-start(), calls=%async_computation.2 | async-start | bytes 196608 | tf_op jit(solution)/shard_map/psum | solution.py:35
Sparse Core Ops, SparseCore 0:
  13.6 130.8 all-gather.2
  180.9 52.9 all-gather.4
  237.0 29.5 all-reduce.1
where the time goes:
time: 275 us
  waiting for transfers between devices  190 us (69%)
  blocking collectives  25.9 us (9%)
  local copies, waits for them, and re-layouts  25.1 us (9%)
  matrix products  15.6 us (6%)
  between operations  13.8 us (5%)
  other arithmetic  4.54 us (2%)
    all_gather x1, waiting for transfers between devices, on_device(): pooled = lax.all_gather(outgoing, 'blk', axis=0, tiled=True)  131 us
    all_gather x1, waiting for transfers between devices, on_device(): lax.all_gather(radiation, 'blk', axis=0, tiled=True)  36.8 us
    all_gather x1, blocking collectives, on_device(): radiation = lax.all_gather(radiation, 'exc', axis=1, tiled=True)  22 us
    psum x1, waiting for transfers between devices, on_device(): partial_value, projected = lax.psum((partial_value, projected), 'row')  21.9 us
    gather x1, local copies, waits for them, and re-layouts, on_device(): patterns[partner_slot] * translation[:, :, None, :]  13.8 us
    dot_general x1, matrix products, on_device(): jnp.einsum('mjkp,mlp->mjkl', weighted, lax.all_gather(radiation, 'blk', a...  10.8 us
    gather x1, local copies, waits for them, and re-layouts, on_device(): arrived = pooled[wanted]  7.89 us
  transfers between devices with their start and end apart: 3, of which 3 were waited for; matrix products, arithmetic and copies ran while one was open for 10% of the time, Pallas kernels for 0%

commit v1 on v0

v1 whole, which is shorter than its diff:
```python
import jax
import jax.numpy as jnp
from jax import lax
from jax.experimental import pallas as pl
from jax.experimental.pallas import tpu as pltpu
from jax.sharding import PartitionSpec as P

CAP = 3
SIDE = 4
DEPTH = 8
MOVED = 32
AXES = ("blk", "exc", "row")
NT = (((1,), (1,)), ((), ()))
SMEM = pl.BlockSpec(memory_space=pltpu.SMEM)
VMEM = pl.BlockSpec(memory_space=pltpu.VMEM)


def device_id(y, x, z, core):
    return ((y * SIDE + x) * DEPTH + z) * 2 + core


def plane_perm(shift, first):
    pairs = []
    for y in range(SIDE):
        for x in range(SIDE):
            for z in range(DEPTH):
                for core in range(2):
                    along_x = (core == 0) == first
                    y_to = y if along_x else (y + shift) % SIDE
                    x_to = (x + shift) % SIDE if along_x else x
                    pairs.append((device_id(y, x, z, core), device_id(y_to, x_to, z, core)))
    return pairs


def depth_perm(shift):
    pairs = []
    for y in range(SIDE):
        for x in range(SIDE):
            for z in range(DEPTH):
                for core in range(2):
                    z_to = (z + (shift if core == 0 else -shift)) % DEPTH
                    pairs.append((device_id(y, x, z, core), device_id(y, x, z_to, core)))
    return pairs


def plane_send(value, first):
    return [lax.ppermute(value, AXES, plane_perm(s, first)) for s in range(1, SIDE)]


def core_swap(value):
    return lax.ppermute(value, "row", [(0, 1), (1, 0)])


def pick_kernel(moved, panels, out, slots, buf, sem):
    me = lax.axis_index("blk")
    z = lax.axis_index("exc")
    for s in range(CAP):
        slots[s] = 0
    count = jnp.int32(0)
    for i in range(MOVED):
        block = moved[i]
        mine = (block >> 3) == me

        @pl.when(mine)
        def _():
            slots[count] = block & 7

        count = count + mine.astype(jnp.int32)
    copies = []
    for s in range(CAP):
        copy = pltpu.make_async_copy(panels.at[slots[s]], buf.at[s], sem.at[s])
        copy.start()
        copies.append(copy)
    width = buf.shape[2]
    share = out.shape[1]
    rows = lax.broadcasted_iota(jnp.int32, (share, width), 0)
    cols = lax.broadcasted_iota(jnp.int32, (share, width), 1)
    chosen = jnp.where(cols == rows + z * share, 1.0, 0.0).astype(jnp.bfloat16)
    for s in range(CAP):
        copies[s].wait()
        out[s] = lax.dot_general(chosen, buf[s], NT, preferred_element_type=jnp.float32).astype(jnp.bfloat16)


def pick(moved_blocks, panels):
    blocks, rows, width = panels.shape
    share = width // DEPTH
    return pl.pallas_call(
        pick_kernel,
        out_shape=jax.ShapeDtypeStruct((CAP, share, rows), jnp.bfloat16),
        in_specs=[SMEM, pl.BlockSpec(memory_space=pl.ANY)],
        out_specs=VMEM,
        scratch_shapes=[
            pltpu.SMEM((CAP,), jnp.int32),
            pltpu.VMEM((CAP, rows, width), jnp.bfloat16),
            pltpu.SemaphoreType.DMA((CAP,)),
        ],
        name="pick",
    )(moved_blocks, panels)


def route_kernel(moved, a0, a1, a2, a3, o0, o1, o2, o3, count, rank):
    me = lax.axis_index("blk")
    core = lax.axis_index("row")
    y, x = me >> 2, me & 3
    on_x = core == 0
    here = jnp.where(on_x, x, y)
    across = jnp.where(on_x, y, x)
    for g in range(SIDE * SIDE):
        count[g] = 0
    for i in range(MOVED):
        owner = moved[i] >> 3
        seen = count[owner]
        rank[i] = seen
        count[owner] = seen + 1
    arrivals = (a0, a1, a2, a3)
    for t, out in enumerate((o0, o1, o2, o3)):
        target = (across + t) & 3
        block = jnp.where(on_x, target * SIDE + here, here * SIDE + target)
        for s in range(2):
            index = 2 * block + s
            owner = moved[index] >> 3
            slot = rank[index]
            owner_y, owner_x = owner >> 2, owner & 3
            found = jnp.where(on_x, owner_y, owner_x) == across
            source = (here - jnp.where(on_x, owner_x, owner_y)) & 3
            out[s] = jnp.zeros_like(out[s])
            for k in range(SIDE):

                @pl.when(found & (source == k))
                def _(k=k, s=s, out=out, slot=slot):
                    out[s] = arrivals[k][slot]


def route(moved_blocks, arrivals):
    _, share, rows = arrivals[0].shape
    return pl.pallas_call(
        route_kernel,
        out_shape=[jax.ShapeDtypeStruct((2, share, rows), jnp.bfloat16)] * SIDE,
        in_specs=[SMEM] + [VMEM] * SIDE,
        out_specs=[VMEM] * SIDE,
        scratch_shapes=[pltpu.SMEM((SIDE * SIDE,), jnp.int32), pltpu.SMEM((MOVED,), jnp.int32)],
        name="route",
    )(moved_blocks, *arrivals)


def radiate_kernel(a0, a1, a2, a3, geometry, columns, partial):
    rows = a0.shape[2]
    for s in range(2):
        panel = (a0[s] + a1[s]) + (a2[s] + a3[s])
        columns[s, :, :rows] = panel
        columns[s, :, rows:] = jnp.zeros((panel.shape[0], columns.shape[2] - rows), jnp.bfloat16)
        partial[s] = jnp.dot(panel, geometry[s], preferred_element_type=jnp.float32)


def radiate(arrivals, geometry):
    _, share, rows = arrivals[0].shape
    return pl.pallas_call(
        radiate_kernel,
        out_shape=[
            jax.ShapeDtypeStruct((2, share, rows + rows // 3), jnp.bfloat16),
            jax.ShapeDtypeStruct((2, share, geometry.shape[2]), jnp.float32),
        ],
        in_specs=[VMEM] * 5,
        out_specs=[VMEM] * 2,
        name="radiate",
    )(*arrivals, geometry)


def assemble_kernel(own, r1, r2, r3, w1, w2, w3, far, out):
    z = lax.axis_index("exc")
    core = lax.axis_index("row")
    sign = 1 - 2 * core
    share = own.shape[1]

    def place(source, value):
        start = pl.multiple_of((source & 7) * share, share)
        out[pl.ds(start, share), :] = value

    place(z, own[core])
    for k, (r, w) in enumerate(((r1, w1), (r2, w2), (r3, w3)), start=1):
        place(z - sign * k + DEPTH, r[core])
        place(z + sign * k + DEPTH, w[core])
    place(z + 4, far[...])


def assemble(own, direct, swapped, far):
    _, share, width = own.shape
    return pl.pallas_call(
        assemble_kernel,
        out_shape=jax.ShapeDtypeStruct((DEPTH * share, width), jnp.bfloat16),
        in_specs=[VMEM] * 8,
        out_specs=VMEM,
        name="assemble",
    )(own, *direct, *swapped, far)


def couple(ids, slots, pieces, translation, patterns, so_far=None):
    n = len(pieces)
    moved, columns, width = translation.shape
    _, rows, _ = patterns.shape
    basis = pieces[0].shape[1]
    together = 4

    def kernel(ids_ref, slots_ref, *refs):
        piece_refs = refs[:n]
        trans, patt = refs[n], refs[n + 1]
        out = refs[-1]
        step = pl.program_id(0)
        moved_id = ids_ref[step]
        rad = piece_refs[0][0]
        for p in range(1, n):
            rad = jnp.where(step >= 4 * p, piece_refs[p][0], rad)
        for first in range(0, columns, together):
            parts = []
            for j in range(first, first + together):
                pattern = patt[slots_ref[moved_id, j]].astype(jnp.float32)
                parts.append((pattern * trans[0, j : j + 1, :]).astype(jnp.bfloat16))
            weighted = jnp.concatenate(parts, axis=0)
            block = lax.dot_general(weighted, rad, NT, preferred_element_type=jnp.float32)
            out[0, first : first + together] = block.astype(jnp.bfloat16).reshape(together, rows, basis)

    def piece_spec(p):
        return pl.BlockSpec((1, basis, width), lambda g, ids_ref, slots_ref: (jnp.clip(g - 4 * p, 0, 3), 0, 0))

    in_specs = [piece_spec(p) for p in range(n)]
    in_specs.append(pl.BlockSpec((1, columns, width), lambda g, ids_ref, slots_ref: (ids_ref[g], 0, 0)))
    in_specs.append(pl.BlockSpec(patterns.shape, lambda g, ids_ref, slots_ref: (0, 0, 0)))
    operands = [*pieces, translation, patterns]
    aliases = {}
    if so_far is not None:
        in_specs.append(pl.BlockSpec(memory_space=pl.ANY))
        aliases = {2 + len(operands): 0}
        operands.append(so_far)
    return pl.pallas_call(
        kernel,
        out_shape=jax.ShapeDtypeStruct((moved, columns, rows, basis), jnp.bfloat16),
        grid_spec=pltpu.PrefetchScalarGridSpec(
            num_scalar_prefetch=2,
            grid=(4 * n,),
            in_specs=in_specs,
            out_specs=pl.BlockSpec((1, columns, rows, basis), lambda g, ids_ref, slots_ref: (ids_ref[g], 0, 0, 0)),
        ),
        input_output_aliases=aliases,
        cost_estimate=pl.CostEstimate(
            flops=4 * n * columns * rows * width * basis * 4,
            bytes_accessed=4 * n * columns * rows * basis * 2,
            transcendentals=0,
        ),
        name="couple",
    )(ids, slots, *operands)


def project_kernel(excitations, gathered, out):
    rows = excitations.shape[2]
    for s in range(2):
        panel = gathered[:, s, :, :rows].reshape(-1, rows)
        out[s] = lax.dot_general(excitations[s], panel, NT, preferred_element_type=jnp.float32)


def project(excitations, gathered):
    moved, count, _ = excitations.shape
    basis = gathered.shape[0] * gathered.shape[2]
    return pl.pallas_call(
        project_kernel,
        out_shape=jax.ShapeDtypeStruct((moved, count, basis), jnp.float32),
        in_specs=[VMEM] * 2,
        out_specs=VMEM,
        name="project",
    )(excitations, gathered)


def piece_ids(y, x, core, leg):
    k = jnp.arange(SIDE)
    near = jnp.where(core == 0, x, y)
    far = jnp.where(core == 0, y, x)
    first = (near - k) & 3
    second = (far - leg) & 3
    block = jnp.where(core == 0, second * SIDE + first, first * SIDE + second)
    return 2 * block + core


def on_device(panels, patterns, geometry, excitations, moved_blocks, partners, translation):
    me = lax.axis_index("blk")
    core = lax.axis_index("row")
    y, x = me >> 2, me & 3
    slots = partners & 7

    outgoing = pick(moved_blocks, panels)
    routed = route(moved_blocks, [outgoing, *plane_send(outgoing, True)])
    landed = [lax.ppermute(routed[s], AXES, plane_perm(s, False)) for s in range(1, SIDE)]
    columns, partial = radiate([routed[0], *landed], geometry)
    gathered = lax.all_gather(columns, "exc", axis=0)

    radiation = (partial + core_swap(partial)).astype(jnp.bfloat16)
    half = lax.dynamic_index_in_dim(radiation, core, 0, keepdims=False)
    direct = [lax.ppermute(radiation, AXES, depth_perm(k)) for k in range(1, 4)]
    far = lax.ppermute(half, AXES, depth_perm(4))
    swapped = [core_swap(value) for value in direct]
    mine = assemble(radiation, direct, swapped, far)

    stack = jnp.stack([mine, *plane_send(mine, True)])
    arrived = plane_send(stack, False)
    stack_other = core_swap(stack)
    arrived_other = [core_swap(value) for value in arrived]
    other = 1 - core
    ids_near = jnp.concatenate([piece_ids(y, x, core, 0), piece_ids(y, x, other, 0)])
    ids_own = jnp.concatenate([piece_ids(y, x, core, leg) for leg in range(1, 4)])
    ids_other = jnp.concatenate([piece_ids(y, x, other, leg) for leg in range(1, 4)])
    couplings = couple(ids_near, slots, [stack, stack_other], translation, patterns)
    couplings = couple(ids_own, slots, arrived, translation, patterns, couplings)
    couplings = couple(ids_other, slots, arrived_other, translation, patterns, couplings)

    projected = project(excitations, gathered)
    projected = projected + core_swap(projected)
    return (couplings, projected)


def solution(mesh):
    placed = (
        P("blk", "row", None),
        P("blk", "row", None),
        P("blk", "row", None),
        P("blk", "exc", "row"),
        P(),
        P(None, ("blk", "exc")),
        P(None, ("blk", "exc"), None),
    )
    return jax.shard_map(
        on_device,
        mesh=mesh,
        in_specs=placed,
        out_specs=(P(None, ("blk", "exc"), "row", None), P("blk", "exc", None)),
        check_vma=False,
    )
```

time: 275 us -> 123 us (0.45)
  waiting for transfers between devices: 190 us -> 12.2 us
  starting transfers between devices: 0.12 us -> 45 us
  Pallas kernels: 0 us -> 39.2 us
  blocking collectives: 25.9 us -> 0 us
  local copies, waits for them, and re-layouts: 25.1 us -> 6.08 us
  matrix products: 15.6 us -> 0 us
    all_gather x2 -> x1, waiting for transfers between devices: 168 us -> 0.01 us  [on_device(): gathered = lax.all_gather(columns, 'exc', axis=0)]
    ppermute x0 -> x25, starting transfers between devices: none -> 45 us  [the longest x9 14.7 us: core_swap(): return lax.ppermute(value, 'row', [(0, 1), (1, 0)])]
    pallas_call x0 -> x8, Pallas kernels: none -> 39.2 us  [the longest x3 27.4 us: couple(): pl.pallas_call(kernel, out_shape=jax.ShapeDtypeStruct((moved, columns, ro...]
    gather x3 -> x0, local copies, waits for them, and re-layouts: 23.4 us -> none  [the longest x1 13.8 us: on_device(): patterns[partner_slot] * translation[:, :, None, :]]
    all_gather x1 -> x0, blocking collectives: 22 us -> none  [on_device(): radiation = lax.all_gather(radiation, 'exc', axis=1, tiled=True)]
    psum x1 -> x0, waiting for transfers between devices: 21.9 us -> none  [on_device(): partial_value, projected = lax.psum((partial_value, projected), 'row')]
    dot_general x3 -> x0, matrix products: 15.6 us -> none  [the longest x1 10.8 us: on_device(): jnp.einsum('mjkp,mlp->mjkl', weighted, lax.all_gather(radiation, 'blk', a...]
    ppermute x0 -> x25, waiting for transfers between devices: none -> 12.2 us  [the longest x9 6.66 us: plane_send(): lax.ppermute(value, AXES, plane_perm(s, first))]
  transfers between devices with their start and end apart: 3 -> 26, of which waited for: 3 -> 10; matrix products, arithmetic and copies ran while one was open for 10% -> 4% of each run, Pallas kernels for 0% -> 26%
where the time goes in v1:
time: 123 us; the launch traced here: 122 us
  starting transfers between devices  45 us (37%)
  Pallas kernels  39.2 us (32%)
  between operations  14.2 us (12%)
  waiting for transfers between devices  12.2 us (10%)
  local copies, waits for them, and re-layouts  6.08 us (5%)
  other arithmetic  4.85 us (4%)
    pallas_call x3, Pallas kernels, couple(): pl.pallas_call(kernel, out_shape=jax.ShapeDtypeStruct((moved, columns, ro...  27.4 us
    ppermute x9, starting transfers between devices, core_swap(): return lax.ppermute(value, 'row', [(0, 1), (1, 0)])  14.7 us
    ppermute x9, starting transfers between devices, plane_send(): lax.ppermute(value, AXES, plane_perm(s, first))  14 us
    ppermute x3, starting transfers between devices, on_device(): direct = [lax.ppermute(radiation, AXES, depth_perm(k)) for k in range(1, 4)]  7.27 us
    ppermute x9, waiting for transfers between devices, plane_send(): lax.ppermute(value, AXES, plane_perm(s, first))  6.66 us
    unnamed x47, local copies, waits for them, and re-layouts  6.08 us
    ppermute x3, starting transfers between devices, on_device(): lax.ppermute(routed[s], AXES, plane_perm(s, False))  4.53 us
    ppermute x1, starting transfers between devices, on_device(): far = lax.ppermute(half, AXES, depth_perm(4))  4.48 us
  transfers between devices with their start and end apart: 26, of which 10 were waited for; matrix products, arithmetic and copies ran while one was open for 4% of the time, Pallas kernels for 26%

profile of v1, /device:TPU:1, one launch (start us, length us, event | category | flops | bytes accessed | tf_op | source)
XLA Modules:
  0.0 121.5 jit_solution(16846441380951536795)
XLA Ops:
  7.2 0.0 all-gather.3.cloned.1.call-start
  7.2 3.1 %pick.1.a0 = bf16[3,16,1536]{2,1,0:T(8,128)(2,1)} custom-call(s32[32]{0:T(128)} %moved.3, bf16[8,1536,128]{2,1,0:T(8,128)(2,1)} %panels.1), custom_call_target="tpu_custom_call" | custom-call | tf_op jit(solution)/shard_map/pick/pallas_call | solution.py:87
  10.3 2.2 %collective-permute-start = (bf16[3,16,1536]{2,1,0:T(8,128)(2,1)}, bf16[3,16,1536]{2,1,0:T(8,128)(2,1)S(1)}, u32[]{:S(2)}, u32[]{:S(2)}) collective-permute-start(bf16[3,16,1536]{2,1,0:T(8,128)(2,1)} %pick.1.a0), channel_id=1, source_target_pairs={{0,16},{1,65},{2,18},{3,67},{4,20},{5,69},{6,22},{7,71},{8,24},{9,... | collective-permute-start | bytes 442376 | tf_op jit(solution)/shard_map/ppermute | solution.py:47
  12.5 2.6 %collective-permute-start.1 = (bf16[3,16,1536]{2,1,0:T(8,128)(2,1)}, bf16[3,16,1536]{2,1,0:T(8,128)(2,1)S(1)}, u32[]{:S(2)}, u32[]{:S(2)}) collective-permute-start(bf16[3,16,1536]{2,1,0:T(8,128)(2,1)} %pick.1.a0), channel_id=1, source_target_pairs={{0,32},{1,129},{2,34},{3,131},{4,36},{5,133},{6,38},{7,135},{8,40}... | collective-permute-start | bytes 442376 | tf_op jit(solution)/shard_map/ppermute | solution.py:47
  15.1 1.1 collective-permute-start.2
  16.2 0.5 collective-permute-done.a1
  16.7 3.0 %collective-permute-done.1.a2 = bf16[3,16,1536]{2,1,0:T(8,128)(2,1)S(1)} collective-permute-done((bf16[3,16,1536]{2,1,0:T(8,128)(2,1)}, bf16[3,16,1536]{2,1,0:T(8,128)(2,1)S(1)}, u32[]{:S(2)}, u32[]{:S(2)}) %collective-permute-start.1) | collective-permute-done | bytes 147488 | tf_op jit(solution)/shard_map/ppermute | solution.py:47
  19.7 0.0 collective-permute-done.2.a3
  19.8 0.6 copy-done.10
  20.4 0.7 copy-done.11
  21.1 2.3 %route.1 = (bf16[2,16,1536]{2,1,0:T(8,128)(2,1)}, bf16[2,16,1536]{2,1,0:T(8,128)(2,1)}, bf16[2,16,1536]{2,1,0:T(8,128)(2,1)}, bf16[2,16,1536]{2,1,0:T(8,128)(2,1)}) custom-call(s32[32]{0:T(128)} %moved.3, bf16[3,16,1536]{2,1,0:T(8,128)(2,1)} %pick.1.a0, bf16[3,16,1536]{2,1,0:T(8,128)(2,1)} %copy-done.9, bf16[3,16,1536]{2,1,0:T(8,128)(2,1)} %copy-done.10, ...), custom_call_target="tpu_custom_call" | custom-call | tf_op jit(solution)/shard_map/route/pallas_call | solution.py:136
  23.3 0.9 collective-permute-start.3
  24.2 2.8 %collective-permute-start.4 = (bf16[2,16,1536]{2,1,0:T(8,128)(2,1)}, bf16[2,16,1536]{2,1,0:T(8,128)(2,1)S(1)}, u32[]{:S(2)}, u32[]{:S(2)}) collective-permute-start(bf16[2,16,1536]{2,1,0:T(8,128)(2,1)} %get-tuple-element.10), channel_id=1, source_target_pairs={{0,128},{1,33},{2,130},{3,35},{4,132},{5,37},{6,134},{7,39},{8,136... | collective-permute-start | bytes 294920 | tf_op jit(solution)/shard_map/ppermute | solution.py:290
  27.0 0.9 collective-permute-start.5
  27.8 0.4 collective-permute-done.3.a1
  28.2 2.0 %collective-permute-done.4.a2 = bf16[2,16,1536]{2,1,0:T(8,128)(2,1)S(1)} collective-permute-done((bf16[2,16,1536]{2,1,0:T(8,128)(2,1)}, bf16[2,16,1536]{2,1,0:T(8,128)(2,1)S(1)}, u32[]{:S(2)}, u32[]{:S(2)}) %collective-permute-start.4) | collective-permute-done | bytes 98336 | tf_op jit(solution)/shard_map/ppermute | solution.py:290
  30.3 0.7 collective-permute-done.5.a3
  31.0 0.6 copy-done.15
  31.6 2.5 %radiate.1 = (bf16[2,16,2048]{2,1,0:T(8,128)(2,1)}, f32[2,16,256]{2,1,0:T(8,128)}) custom-call(bf16[2,16,1536]{2,1,0:T(8,128)(2,1)} %get-tuple-element.8.a0, bf16[2,16,1536]{2,1,0:T(8,128)(2,1)} %copy-done.13, bf16[2,16,1536]{2,1,0:T(8,128)(2,1)} %copy-done.14, bf16[2,16,1536]{2,1,0:T(8,128)(2,1)} %copy-done.15, bf16[2,1536,256]{2,1,0:T(8,128)(2,1)} %geometry.1), custom_call_target="tpu_custom_call" | custom-call | tf_op jit(solution)/shard_map/radiate/pallas_call | solution.py:157
  34.1 0.0 all-gather.3.cloned.1.call-update
  34.2 0.8 copy.12
  35.0 0.6 broadcast_and_fusion.slots_ref
  35.6 2.9 %collective-permute-start.6 = (f32[2,16,256]{2,1,0:T(8,128)}, f32[2,16,256]{2,1,0:T(8,128)S(1)}, u32[]{:S(2)}, u32[]{:S(2)}) collective-permute-start(f32[2,16,256]{2,1,0:T(8,128)} %get-tuple-element.12), channel_id=1, source_target_pairs={{0,1},{1,0},{2,3},{3,2},{4,5},{5,4},{6,7},{7,6},{8,9},{9,8},{10,11... | collective-permute-start | bytes 98312 | tf_op jit(solution)/shard_map/ppermute | solution.py:51
  38.5 1.1 collective-permute-done.6
  39.6 0.8 add_convert_fusion.own
  40.3 5.6 %collective-permute-start.7 = (bf16[2,16,256]{2,1,0:T(8,128)(2,1)S(1)}, bf16[2,16,256]{2,1,0:T(8,128)(2,1)S(1)}, u32[]{:S(2)}, u32[]{:S(2)}) collective-permute-start(bf16[2,16,256]{2,1,0:T(8,128)(2,1)S(1)} %add_convert_fusion.own), channel_id=1, source_target_pairs={{0,2},{1,15},{2,4},{3,1},{4,6},{5,3},{6,8},{7,5},{8,10},{9,7},{10,... | collective-permute-start | bytes 49160 | tf_op jit(solution)/shard_map/ppermute | solution.py:296
  46.0 1.2 collective-permute-start.8
  47.2 0.4 collective-permute-start.9
  47.6 4.5 %collective-permute-start.13 = (bf16[16,256]{1,0:T(8,128)(2,1)S(1)}, bf16[16,256]{1,0:T(8,128)(2,1)S(1)}, u32[]{:S(2)}, u32[]{:S(2)}) collective-permute-start(bf16[16,256]{1,0:T(8,128)(2,1)S(1)} %dynamic-slice_bitcast_fusion), channel_id=1, source_target_pairs={{0,8},{1,9},{2,10},{3,11},{4,12},{5,13},{6,14},{7,15},{8,0},{9,1},... | collective-permute-start | bytes 24584 | tf_op jit(solution)/shard_map/ppermute | solution.py:297
  52.1 0.5 collective-permute-start.11
  52.6 0.1 collective-permute-start.12
  52.7 1.3 %collective-permute-done.13.far = bf16[16,256]{1,0:T(8,128)(2,1)S(1)} collective-permute-done((bf16[16,256]{1,0:T(8,128)(2,1)S(1)}, bf16[16,256]{1,0:T(8,128)(2,1)S(1)}, u32[]{:S(2)}, u32[]{:S(2)}) %collective-permute-start.13) | collective-permute-done | bytes 8224 | tf_op jit(solution)/shard_map/ppermute | solution.py:297
  54.1 0.5 copy-done.22
  54.6 0.0 copy-done.19
  54.7 0.0 copy-done.20
  54.7 0.6 copy-done.21
  55.3 1.5 %assemble.1 = bf16[128,256]{1,0:T(8,128)(2,1)} custom-call(bf16[2,16,256]{2,1,0:T(8,128)(2,1)} %copy-done.12, bf16[2,16,256]{2,1,0:T(8,128)(2,1)} %copy-done.16, bf16[2,16,256]{2,1,0:T(8,128)(2,1)} %copy-done.17, bf16[2,16,256]{2,1,0:T(8,128)(2,1)} %copy-done.18, bf16[2,16,256]{2,1,0:T(8,128)(2,1)} %copy-done.19, bf16[2,16,256]{2,1,0:T(8,128)(2,1)} %copy-done.20, ...), custom_call_target="tpu_custom_call" | custom-call | tf_op jit(solution)/shard_map/assemble/pallas_call | solution.py:188
  56.7 0.4 collective-permute-start.14
  57.1 3.1 %collective-permute-start.15 = (bf16[128,256]{1,0:T(8,128)(2,1)}, bf16[128,256]{1,0:T(8,128)(2,1)S(1)}, u32[]{:S(2)}, u32[]{:S(2)}) collective-permute-start(bf16[128,256]{1,0:T(8,128)(2,1)} %assemble.1), channel_id=1, source_target_pairs={{0,32},{1,129},{2,34},{3,131},{4,36},{5,133},{6,38},{7,135},{8,40}... | collective-permute-start | bytes 196616 | tf_op jit(solution)/shard_map/ppermute | solution.py:47
  60.2 0.2 collective-permute-start.16
  60.4 0.9 collective-permute-done.14
  61.3 1.5 %collective-permute-done.15 = bf16[128,256]{1,0:T(8,128)(2,1)S(1)} collective-permute-done((bf16[128,256]{1,0:T(8,128)(2,1)}, bf16[128,256]{1,0:T(8,128)(2,1)S(1)}, u32[]{:S(2)}, u32[]{:S(2)}) %collective-permute-start.15) | collective-permute-done | bytes 65568 | tf_op jit(solution)/shard_map/ppermute | solution.py:47
  62.8 0.8 collective-permute-done.16
  63.5 0.9 pad_maximum_fusion.refs_0_
  64.4 1.4 %collective-permute-start.17 = (bf16[4,128,256]{2,1,0:T(8,128)(2,1)S(1)}, bf16[4,128,256]{2,1,0:T(8,128)(2,1)S(1)}, u32[]{:S(2)}, u32[]{:S(2)}) collective-permute-start(bf16[4,128,256]{2,1,0:T(8,128)(2,1)S(1)} %pad_maximum_fusion.refs_0_), channel_id=1, source_target_pairs={{0,64},{1,17},{2,66},{3,19},{4,68},{5,21},{6,70},{7,23},{8,72},{9,... | collective-permute-start | bytes 786440 | tf_op jit(solution)/shard_map/ppermute | solution.py:47
  65.8 2.4 %collective-permute-start.19 = (bf16[4,128,256]{2,1,0:T(8,128)(2,1)S(1)}, bf16[4,128,256]{2,1,0:T(8,128)(2,1)S(1)}, u32[]{:S(2)}, u32[]{:S(2)}) collective-permute-start(bf16[4,128,256]{2,1,0:T(8,128)(2,1)S(1)} %pad_maximum_fusion.refs_0_), channel_id=1, source_target_pairs={{0,128},{1,33},{2,130},{3,35},{4,132},{5,37},{6,134},{7,39},{8,136... | collective-permute-start | bytes 786440 | tf_op jit(solution)/shard_map/ppermute | solution.py:47
  68.1 0.7 collective-permute-start.21
  68.9 0.7 pad_add_fusion.2.ids_ref
  69.5 5.3 %collective-permute-start.23 = (bf16[4,128,256]{2,1,0:T(8,128)(2,1)S(1)}, bf16[4,128,256]{2,1,0:T(8,128)(2,1)S(1)}, u32[]{:S(2)}, u32[]{:S(2)}) collective-permute-start(bf16[4,128,256]{2,1,0:T(8,128)(2,1)S(1)} %pad_maximum_fusion.refs_0_), channel_id=1, source_target_pairs={{0,1},{1,0},{2,3},{3,2},{4,5},{5,4},{6,7},{7,6},{8,9},{9,8},{10,11... | collective-permute-start | bytes 786440 | tf_op jit(solution)/shard_map/ppermute | solution.py:51
  74.9 0.6 pad_add_fusion.1.ids_ref
  75.5 1.8 %collective-permute-start.18 = (bf16[4,128,256]{2,1,0:T(8,128)(2,1)S(1)}, bf16[4,128,256]{2,1,0:T(8,128)(2,1)S(1)}, u32[]{:S(2)}, u32[]{:S(2)}) collective-permute-start(bf16[4,128,256]{2,1,0:T(8,128)(2,1)S(1)} %collective-permute-done.17.refs_0_), channel_id=1, source_target_pairs={{0,1},{1,0},{2,3},{3,2},{4,5},{5,4},{6,7},{7,6},{8,9},{9,8},{10,11... | collective-permute-start | bytes 786440 | tf_op jit(solution)/shard_map/ppermute | solution.py:51
  77.3 3.5 %collective-permute-start.20 = (bf16[4,128,256]{2,1,0:T(8,128)(2,1)S(1)}, bf16[4,128,256]{2,1,0:T(8,128)(2,1)S(1)}, u32[]{:S(2)}, u32[]{:S(2)}) collective-permute-start(bf16[4,128,256]{2,1,0:T(8,128)(2,1)S(1)} %collective-permute-done.19.refs_1_), channel_id=1, source_target_pairs={{0,1},{1,0},{2,3},{3,2},{4,5},{5,4},{6,7},{7,6},{8,9},{9,8},{10,11... | collective-permute-start | bytes 786440 | tf_op jit(solution)/shard_map/ppermute | solution.py:51
  80.8 0.2 collective-permute-start.22
  81.0 0.7 pad_add_fusion.ids_ref
  81.7 0.7 copy-done.8
  82.4 7.4 %couple.3.refs_5_ = bf16[32,16,64,128]{3,2,1,0:T(8,128)(2,1)} custom-call(s32[8]{0:T(128)} %pad_add_fusion.2.ids_ref, s32[32,16]{1,0:T(8,128)} %broadcast_and_fusion.slots_ref, bf16[4,128,256]{2,1,0:T(8,128)(2,1)} %copy-done, bf16[4,128,256]{2,1,0:T(8,128)(2,1)} %copy-done.8, f32[32,16,256]{2,1,0:T(8,128)} %refs_3_.5, bf16[8,64,256]{2,1,0:T(8,128)(2,1)} %refs_4_.3), custom_call_target="tpu_custom_call" | custom-call | flops 1073741824 | bytes 2097152 | tf_op jit(solution)/shard_map/couple/pallas_call | solution.py:234
  89.8 10.0 %couple.4.refs_5_ = bf16[32,16,64,128]{3,2,1,0:T(8,128)(2,1)} custom-call(s32[12]{0:T(128)} %pad_add_fusion.1.ids_ref, s32[32,16]{1,0:T(8,128)} %broadcast_and_fusion.slots_ref, bf16[4,128,256]{2,1,0:T(8,128)(2,1)} %copy-done.2, bf16[4,128,256]{2,1,0:T(8,128)(2,1)} %copy-done.3, bf16[4,128,256]{2,1,0:T(8,128)(2,1)} %copy-done.4, ...), custom_call_target="tpu_custom_call", output_to_operand_aliasing={{}: (7, {})} | custom-call | flops 1610612736 | bytes 3145728 | tf_op jit(solution)/shard_map/couple/pallas_call | solution.py:234
  99.8 2.4 %project.1 = f32[2,96,128]{2,1,0:T(8,128)} custom-call(bf16[2,96,1536]{2,1,0:T(8,128)(2,1)} %excitations.1, bf16[8,2,16,2048]{3,2,1,0:T(8,128)(2,1)} %bitcast.7), custom_call_target="tpu_custom_call" | custom-call | tf_op jit(solution)/shard_map/project/pallas_call | solution.py:263
  102.2 0.3 collective-permute-start.24
  102.6 0.7 copy-done.5
  103.2 0.1 copy-done.6
  103.3 0.7 copy-done.7
  104.0 10.0 %couple.5 = bf16[32,16,64,128]{3,2,1,0:T(8,128)(2,1)} custom-call(s32[12]{0:T(128)} %pad_add_fusion.ids_ref, s32[32,16]{1,0:T(8,128)} %broadcast_and_fusion.slots_ref, bf16[4,128,256]{2,1,0:T(8,128)(2,1)} %copy-done.5, bf16[4,128,256]{2,1,0:T(8,128)(2,1)} %copy-done.6, bf16[4,128,256]{2,1,0:T(8,128)(2,1)} %copy-done.7, ...), custom_call_target="tpu_custom_call", output_to_operand_aliasing={{}: (7, {})} | custom-call | flops 1610612736 | bytes 3145728 | tf_op jit(solution)/shard_map/couple/pallas_call | solution.py:234
  114.0 0.7 add.192
  (57 shorter events, 0.2 us)
Async XLA Ops:
  7.2 92.6 %all-gather.3.cloned.1.call-start = ((), (), s32[]{:S(2)}) async-start(), calls=%async_computation | async-start | bytes 1179648 | tf_op jit(solution)/shard_map/all_gather | solution.py:292
  10.3 6.4 %collective-permute-start = (bf16[3,16,1536]{2,1,0:T(8,128)(2,1)}, bf16[3,16,1536]{2,1,0:T(8,128)(2,1)S(1)}, u32[]{:S(2)}, u32[]{:S(2)}) collective-permute-start(bf16[3,16,1536]{2,1,0:T(8,128)(2,1)} %pick.1.a0), channel_id=1, source_target_pairs={{0,16},{1,65},{2,18},{3,67},{4,20},{5,69},{6,22},{7,71},{8,24},{9,... | collective-permute-start | bytes 442376 | tf_op jit(solution)/shard_map/ppermute | solution.py:47
  12.5 7.2 %collective-permute-start.1 = (bf16[3,16,1536]{2,1,0:T(8,128)(2,1)}, bf16[3,16,1536]{2,1,0:T(8,128)(2,1)S(1)}, u32[]{:S(2)}, u32[]{:S(2)}) collective-permute-start(bf16[3,16,1536]{2,1,0:T(8,128)(2,1)} %pick.1.a0), channel_id=1, source_target_pairs={{0,32},{1,129},{2,34},{3,131},{4,36},{5,133},{6,38},{7,135},{8,40}... | collective-permute-start | bytes 442376 | tf_op jit(solution)/shard_map/ppermute | solution.py:47
  15.1 4.6 %collective-permute-start.2 = (bf16[3,16,1536]{2,1,0:T(8,128)(2,1)}, bf16[3,16,1536]{2,1,0:T(8,128)(2,1)S(1)}, u32[]{:S(2)}, u32[]{:S(2)}) collective-permute-start(bf16[3,16,1536]{2,1,0:T(8,128)(2,1)} %pick.1.a0), channel_id=1, source_target_pairs={{0,48},{1,193},{2,50},{3,195},{4,52},{5,197},{6,54},{7,199},{8,56}... | collective-permute-start | bytes 442376 | tf_op jit(solution)/shard_map/ppermute | solution.py:47
  16.7 3.1 %copy-start.9 = (bf16[3,16,1536]{2,1,0:T(8,128)(2,1)}, bf16[3,16,1536]{2,1,0:T(8,128)(2,1)S(1)}, u32[]{:S(2)}) copy-start(bf16[3,16,1536]{2,1,0:T(8,128)(2,1)S(1)} %collective-permute-done.a1) | copy-start | bytes 442372
  19.7 0.7 copy-start.10
  20.4 0.7 copy-start.11
  23.3 4.9 %collective-permute-start.3 = (bf16[2,16,1536]{2,1,0:T(8,128)(2,1)}, bf16[2,16,1536]{2,1,0:T(8,128)(2,1)S(1)}, u32[]{:S(2)}, u32[]{:S(2)}) collective-permute-start(bf16[2,16,1536]{2,1,0:T(8,128)(2,1)} %get-tuple-element.9), channel_id=1, source_target_pairs={{0,64},{1,17},{2,66},{3,19},{4,68},{5,21},{6,70},{7,23},{8,72},{9,... | collective-permute-start | bytes 294920 | tf_op jit(solution)/shard_map/ppermute | solution.py:290
  24.2 6.0 %collective-permute-start.4 = (bf16[2,16,1536]{2,1,0:T(8,128)(2,1)}, bf16[2,16,1536]{2,1,0:T(8,128)(2,1)S(1)}, u32[]{:S(2)}, u32[]{:S(2)}) collective-permute-start(bf16[2,16,1536]{2,1,0:T(8,128)(2,1)} %get-tuple-element.10), channel_id=1, source_target_pairs={{0,128},{1,33},{2,130},{3,35},{4,132},{5,37},{6,134},{7,39},{8,136... | collective-permute-start | bytes 294920 | tf_op jit(solution)/shard_map/ppermute | solution.py:290
  27.0 4.0 %collective-permute-start.5 = (bf16[2,16,1536]{2,1,0:T(8,128)(2,1)}, bf16[2,16,1536]{2,1,0:T(8,128)(2,1)S(1)}, u32[]{:S(2)}, u32[]{:S(2)}) collective-permute-start(bf16[2,16,1536]{2,1,0:T(8,128)(2,1)} %get-tuple-element.11), channel_id=1, source_target_pairs={{0,192},{1,49},{2,194},{3,51},{4,196},{5,53},{6,198},{7,55},{8,200... | collective-permute-start | bytes 294920 | tf_op jit(solution)/shard_map/ppermute | solution.py:290
  28.2 2.8 %copy-start.13 = (bf16[2,16,1536]{2,1,0:T(8,128)(2,1)}, bf16[2,16,1536]{2,1,0:T(8,128)(2,1)S(1)}, u32[]{:S(2)}) copy-start(bf16[2,16,1536]{2,1,0:T(8,128)(2,1)S(1)} %collective-permute-done.3.a1) | copy-start | bytes 294916
  30.3 0.7 copy-start.14
  31.0 0.6 copy-start.15
  35.6 4.0 %collective-permute-start.6 = (f32[2,16,256]{2,1,0:T(8,128)}, f32[2,16,256]{2,1,0:T(8,128)S(1)}, u32[]{:S(2)}, u32[]{:S(2)}) collective-permute-start(f32[2,16,256]{2,1,0:T(8,128)} %get-tuple-element.12), channel_id=1, source_target_pairs={{0,1},{1,0},{2,3},{3,2},{4,5},{5,4},{6,7},{7,6},{8,9},{9,8},{10,11... | collective-permute-start | bytes 98312 | tf_op jit(solution)/shard_map/ppermute | solution.py:51
  40.3 13.7 %copy-start.12 = (bf16[2,16,256]{2,1,0:T(8,128)(2,1)}, bf16[2,16,256]{2,1,0:T(8,128)(2,1)S(1)}, u32[]{:S(2)}) copy-start(bf16[2,16,256]{2,1,0:T(8,128)(2,1)S(1)} %add_convert_fusion.own) | copy-start | bytes 49156
  40.3 11.8 %collective-permute-start.7 = (bf16[2,16,256]{2,1,0:T(8,128)(2,1)S(1)}, bf16[2,16,256]{2,1,0:T(8,128)(2,1)S(1)}, u32[]{:S(2)}, u32[]{:S(2)}) collective-permute-start(bf16[2,16,256]{2,1,0:T(8,128)(2,1)S(1)} %add_convert_fusion.own), channel_id=1, source_target_pairs={{0,2},{1,15},{2,4},{3,1},{4,6},{5,3},{6,8},{7,5},{8,10},{9,7},{10,... | collective-permute-start | bytes 49160 | tf_op jit(solution)/shard_map/ppermute | solution.py:296
  46.0 6.1 %collective-permute-start.8 = (bf16[2,16,256]{2,1,0:T(8,128)(2,1)S(1)}, bf16[2,16,256]{2,1,0:T(8,128)(2,1)S(1)}, u32[]{:S(2)}, u32[]{:S(2)}) collective-permute-start(bf16[2,16,256]{2,1,0:T(8,128)(2,1)S(1)} %add_convert_fusion.own), channel_id=1, source_target_pairs={{0,4},{1,13},{2,6},{3,15},{4,8},{5,1},{6,10},{7,3},{8,12},{9,5},{1... | collective-permute-start | bytes 49160 | tf_op jit(solution)/shard_map/ppermute | solution.py:296
  47.2 5.5 %collective-permute-start.9 = (bf16[2,16,256]{2,1,0:T(8,128)(2,1)S(1)}, bf16[2,16,256]{2,1,0:T(8,128)(2,1)S(1)}, u32[]{:S(2)}, u32[]{:S(2)}) collective-permute-start(bf16[2,16,256]{2,1,0:T(8,128)(2,1)S(1)} %add_convert_fusion.own), channel_id=1, source_target_pairs={{0,6},{1,11},{2,8},{3,13},{4,10},{5,15},{6,12},{7,1},{8,14},{9,3},... | collective-permute-start | bytes 49160 | tf_op jit(solution)/shard_map/ppermute | solution.py:296
  47.6 6.4 %collective-permute-start.13 = (bf16[16,256]{1,0:T(8,128)(2,1)S(1)}, bf16[16,256]{1,0:T(8,128)(2,1)S(1)}, u32[]{:S(2)}, u32[]{:S(2)}) collective-permute-start(bf16[16,256]{1,0:T(8,128)(2,1)S(1)} %dynamic-slice_bitcast_fusion), channel_id=1, source_target_pairs={{0,8},{1,9},{2,10},{3,11},{4,12},{5,13},{6,14},{7,15},{8,0},{9,1},... | collective-permute-start | bytes 24584 | tf_op jit(solution)/shard_map/ppermute | solution.py:297
  52.1 2.0 %copy-start.16 = (bf16[2,16,256]{2,1,0:T(8,128)(2,1)}, bf16[2,16,256]{2,1,0:T(8,128)(2,1)S(1)}, u32[]{:S(2)}) copy-start(bf16[2,16,256]{2,1,0:T(8,128)(2,1)S(1)} %collective-permute-done.7.r1) | copy-start | bytes 49156
  52.1 1.9 %collective-permute-start.10 = (bf16[2,16,256]{2,1,0:T(8,128)(2,1)S(1)}, bf16[2,16,256]{2,1,0:T(8,128)(2,1)S(1)}, u32[]{:S(2)}, u32[]{:S(2)}) collective-permute-start(bf16[2,16,256]{2,1,0:T(8,128)(2,1)S(1)} %collective-permute-done.7.r1), channel_id=1, source_target_pairs={{0,1},{1,0},{2,3},{3,2},{4,5},{5,4},{6,7},{7,6},{8,9},{9,8},{10,11... | collective-permute-start | bytes 49160 | tf_op jit(solution)/shard_map/ppermute | solution.py:51
  52.1 2.0 %copy-start.17 = (bf16[2,16,256]{2,1,0:T(8,128)(2,1)}, bf16[2,16,256]{2,1,0:T(8,128)(2,1)S(1)}, u32[]{:S(2)}) copy-start(bf16[2,16,256]{2,1,0:T(8,128)(2,1)S(1)} %collective-permute-done.8.r2) | copy-start | bytes 49156
  52.1 1.9 %collective-permute-start.11 = (bf16[2,16,256]{2,1,0:T(8,128)(2,1)S(1)}, bf16[2,16,256]{2,1,0:T(8,128)(2,1)S(1)}, u32[]{:S(2)}, u32[]{:S(2)}) collective-permute-start(bf16[2,16,256]{2,1,0:T(8,128)(2,1)S(1)} %collective-permute-done.8.r2), channel_id=1, source_target_pairs={{0,1},{1,0},{2,3},{3,2},{4,5},{5,4},{6,7},{7,6},{8,9},{9,8},{10,11... | collective-permute-start | bytes 49160 | tf_op jit(solution)/shard_map/ppermute | solution.py:51
  52.6 1.5 %copy-start.18 = (bf16[2,16,256]{2,1,0:T(8,128)(2,1)}, bf16[2,16,256]{2,1,0:T(8,128)(2,1)S(1)}, u32[]{:S(2)}) copy-start(bf16[2,16,256]{2,1,0:T(8,128)(2,1)S(1)} %collective-permute-done.9.r3) | copy-start | bytes 49156
  52.6 1.4 %collective-permute-start.12 = (bf16[2,16,256]{2,1,0:T(8,128)(2,1)S(1)}, bf16[2,16,256]{2,1,0:T(8,128)(2,1)S(1)}, u32[]{:S(2)}, u32[]{:S(2)}) collective-permute-start(bf16[2,16,256]{2,1,0:T(8,128)(2,1)S(1)} %collective-permute-done.9.r3), channel_id=1, source_target_pairs={{0,1},{1,0},{2,3},{3,2},{4,5},{5,4},{6,7},{7,6},{8,9},{9,8},{10,11... | collective-permute-start | bytes 49160 | tf_op jit(solution)/shard_map/ppermute | solution.py:51
  54.0 0.6 copy-start.22
  54.1 0.6 copy-start.19
  54.1 0.6 copy-start.20
  54.7 0.6 copy-start.21
  56.7 4.5 %collective-permute-start.14 = (bf16[128,256]{1,0:T(8,128)(2,1)}, bf16[128,256]{1,0:T(8,128)(2,1)S(1)}, u32[]{:S(2)}, u32[]{:S(2)}) collective-permute-start(bf16[128,256]{1,0:T(8,128)(2,1)} %assemble.1), channel_id=1, source_target_pairs={{0,16},{1,65},{2,18},{3,67},{4,20},{5,69},{6,22},{7,71},{8,24},{9,... | collective-permute-start | bytes 196616 | tf_op jit(solution)/shard_map/ppermute | solution.py:47
  57.1 5.6 %collective-permute-start.15 = (bf16[128,256]{1,0:T(8,128)(2,1)}, bf16[128,256]{1,0:T(8,128)(2,1)S(1)}, u32[]{:S(2)}, u32[]{:S(2)}) collective-permute-start(bf16[128,256]{1,0:T(8,128)(2,1)} %assemble.1), channel_id=1, source_target_pairs={{0,32},{1,129},{2,34},{3,131},{4,36},{5,133},{6,38},{7,135},{8,40}... | collective-permute-start | bytes 196616 | tf_op jit(solution)/shard_map/ppermute | solution.py:47
  60.2 3.3 %collective-permute-start.16 = (bf16[128,256]{1,0:T(8,128)(2,1)}, bf16[128,256]{1,0:T(8,128)(2,1)S(1)}, u32[]{:S(2)}, u32[]{:S(2)}) collective-permute-start(bf16[128,256]{1,0:T(8,128)(2,1)} %assemble.1), channel_id=1, source_target_pairs={{0,48},{1,193},{2,50},{3,195},{4,52},{5,197},{6,54},{7,199},{8,56}... | collective-permute-start | bytes 196616 | tf_op jit(solution)/shard_map/ppermute | solution.py:47
  64.4 17.3 %copy-start = (bf16[4,128,256]{2,1,0:T(8,128)(2,1)}, bf16[4,128,256]{2,1,0:T(8,128)(2,1)S(1)}, u32[]{:S(2)}) copy-start(bf16[4,128,256]{2,1,0:T(8,128)(2,1)S(1)} %pad_maximum_fusion.refs_0_) | copy-start | bytes 786436
  64.4 11.1 %collective-permute-start.17 = (bf16[4,128,256]{2,1,0:T(8,128)(2,1)S(1)}, bf16[4,128,256]{2,1,0:T(8,128)(2,1)S(1)}, u32[]{:S(2)}, u32[]{:S(2)}) collective-permute-start(bf16[4,128,256]{2,1,0:T(8,128)(2,1)S(1)} %pad_maximum_fusion.refs_0_), channel_id=1, source_target_pairs={{0,64},{1,17},{2,66},{3,19},{4,68},{5,21},{6,70},{7,23},{8,72},{9,... | collective-permute-start | bytes 786440 | tf_op jit(solution)/shard_map/ppermute | solution.py:47
  65.8 11.5 %collective-permute-start.19 = (bf16[4,128,256]{2,1,0:T(8,128)(2,1)S(1)}, bf16[4,128,256]{2,1,0:T(8,128)(2,1)S(1)}, u32[]{:S(2)}, u32[]{:S(2)}) collective-permute-start(bf16[4,128,256]{2,1,0:T(8,128)(2,1)S(1)} %pad_maximum_fusion.refs_0_), channel_id=1, source_target_pairs={{0,128},{1,33},{2,130},{3,35},{4,132},{5,37},{6,134},{7,39},{8,136... | collective-permute-start | bytes 786440 | tf_op jit(solution)/shard_map/ppermute | solution.py:47
  68.1 12.6 %collective-permute-start.21 = (bf16[4,128,256]{2,1,0:T(8,128)(2,1)S(1)}, bf16[4,128,256]{2,1,0:T(8,128)(2,1)S(1)}, u32[]{:S(2)}, u32[]{:S(2)}) collective-permute-start(bf16[4,128,256]{2,1,0:T(8,128)(2,1)S(1)} %pad_maximum_fusion.refs_0_), channel_id=1, source_target_pairs={{0,192},{1,49},{2,194},{3,51},{4,196},{5,53},{6,198},{7,55},{8,200... | collective-permute-start | bytes 786440 | tf_op jit(solution)/shard_map/ppermute | solution.py:47
  69.5 12.1 %collective-permute-start.23 = (bf16[4,128,256]{2,1,0:T(8,128)(2,1)S(1)}, bf16[4,128,256]{2,1,0:T(8,128)(2,1)S(1)}, u32[]{:S(2)}, u32[]{:S(2)}) collective-permute-start(bf16[4,128,256]{2,1,0:T(8,128)(2,1)S(1)} %pad_maximum_fusion.refs_0_), channel_id=1, source_target_pairs={{0,1},{1,0},{2,3},{3,2},{4,5},{5,4},{6,7},{7,6},{8,9},{9,8},{10,11... | collective-permute-start | bytes 786440 | tf_op jit(solution)/shard_map/ppermute | solution.py:51
  75.5 14.3 %copy-start.2 = (bf16[4,128,256]{2,1,0:T(8,128)(2,1)}, bf16[4,128,256]{2,1,0:T(8,128)(2,1)S(1)}, u32[]{:S(2)}) copy-start(bf16[4,128,256]{2,1,0:T(8,128)(2,1)S(1)} %collective-permute-done.17.refs_0_) | copy-start | bytes 786436
  75.5 27.0 %collective-permute-start.18 = (bf16[4,128,256]{2,1,0:T(8,128)(2,1)S(1)}, bf16[4,128,256]{2,1,0:T(8,128)(2,1)S(1)}, u32[]{:S(2)}, u32[]{:S(2)}) collective-permute-start(bf16[4,128,256]{2,1,0:T(8,128)(2,1)S(1)} %collective-permute-done.17.refs_0_), channel_id=1, source_target_pairs={{0,1},{1,0},{2,3},{3,2},{4,5},{5,4},{6,7},{7,6},{8,9},{9,8},{10,11... | collective-permute-start | bytes 786440 | tf_op jit(solution)/shard_map/ppermute | solution.py:51
  77.3 12.5 %copy-start.3 = (bf16[4,128,256]{2,1,0:T(8,128)(2,1)}, bf16[4,128,256]{2,1,0:T(8,128)(2,1)S(1)}, u32[]{:S(2)}) copy-start(bf16[4,128,256]{2,1,0:T(8,128)(2,1)S(1)} %collective-permute-done.19.refs_1_) | copy-start | bytes 786436
  77.3 25.2 %collective-permute-start.20 = (bf16[4,128,256]{2,1,0:T(8,128)(2,1)S(1)}, bf16[4,128,256]{2,1,0:T(8,128)(2,1)S(1)}, u32[]{:S(2)}, u32[]{:S(2)}) collective-permute-start(bf16[4,128,256]{2,1,0:T(8,128)(2,1)S(1)} %collective-permute-done.19.refs_1_), channel_id=1, source_target_pairs={{0,1},{1,0},{2,3},{3,2},{4,5},{5,4},{6,7},{7,6},{8,9},{9,8},{10,11... | collective-permute-start | bytes 786440 | tf_op jit(solution)/shard_map/ppermute | solution.py:51
  80.8 9.0 %copy-start.4 = (bf16[4,128,256]{2,1,0:T(8,128)(2,1)}, bf16[4,128,256]{2,1,0:T(8,128)(2,1)S(1)}, u32[]{:S(2)}) copy-start(bf16[4,128,256]{2,1,0:T(8,128)(2,1)S(1)} %collective-permute-done.21.refs_2_) | copy-start | bytes 786436
  80.8 21.8 %collective-permute-start.22 = (bf16[4,128,256]{2,1,0:T(8,128)(2,1)S(1)}, bf16[4,128,256]{2,1,0:T(8,128)(2,1)S(1)}, u32[]{:S(2)}, u32[]{:S(2)}) collective-permute-start(bf16[4,128,256]{2,1,0:T(8,128)(2,1)S(1)} %collective-permute-done.21.refs_2_), channel_id=1, source_target_pairs={{0,1},{1,0},{2,3},{3,2},{4,5},{5,4},{6,7},{7,6},{8,9},{9,8},{10,11... | collective-permute-start | bytes 786440 | tf_op jit(solution)/shard_map/ppermute | solution.py:51
  81.7 0.7 copy-start.8
  102.2 11.8 %copy-start.1 = (f32[2,96,128]{2,1,0:T(8,128)S(1)}, f32[2,96,128]{2,1,0:T(8,128)}, u32[]{:S(2)}) copy-start(f32[2,96,128]{2,1,0:T(8,128)} %project.1) | copy-start | bytes 294916
  102.2 11.8 %collective-permute-start.24 = (f32[2,96,128]{2,1,0:T(8,128)}, f32[2,96,128]{2,1,0:T(8,128)S(1)}, u32[]{:S(2)}, u32[]{:S(2)}) collective-permute-start(f32[2,96,128]{2,1,0:T(8,128)} %project.1), channel_id=1, source_target_pairs={{0,1},{1,0},{2,3},{3,2},{4,5},{5,4},{6,7},{7,6},{8,9},{9,8},{10,11... | collective-permute-start | bytes 294920 | tf_op jit(solution)/shard_map/ppermute | solution.py:51
  102.5 0.7 copy-start.5
  102.5 0.8 copy-start.6
  103.3 0.7 copy-start.7
Sparse Core Ops, SparseCore 0:
  34.3 38.5 all-gather.2

commit v2 on v1

v2 whole, which is shorter than its diff:
```python
import jax
import jax.numpy as jnp
from jax import lax
from jax.experimental import pallas as pl
from jax.experimental.pallas import tpu as pltpu
from jax.sharding import PartitionSpec as P

CAP = 3
SIDE = 4
DEPTH = 8
MOVED = 32
SLICES = 4
ORDER = (1, 3, 2)
MIB = 2**20
AXES = ("blk", "exc", "row")
NT = (((1,), (1,)), ((), ()))
SMEM = pl.BlockSpec(memory_space=pltpu.SMEM)
VMEM = pl.BlockSpec(memory_space=pltpu.VMEM)


def device_id(y, x, z, core):
    return ((y * SIDE + x) * DEPTH + z) * 2 + core


def plane_perm(shift, first):
    pairs = []
    for y in range(SIDE):
        for x in range(SIDE):
            for z in range(DEPTH):
                for core in range(2):
                    along_x = (core == 0) == first
                    y_to = y if along_x else (y + shift) % SIDE
                    x_to = (x + shift) % SIDE if along_x else x
                    pairs.append((device_id(y, x, z, core), device_id(y_to, x_to, z, core)))
    return pairs


def depth_perm(shift):
    pairs = []
    for y in range(SIDE):
        for x in range(SIDE):
            for z in range(DEPTH):
                for core in range(2):
                    pairs.append((device_id(y, x, z, core), device_id(y, x, (z + shift) % DEPTH, core)))
    return pairs


def plane_send(value, first):
    sent = {s: lax.ppermute(value, AXES, plane_perm(s, first)) for s in ORDER}
    return [sent[s] for s in range(1, SIDE)]


def depth_send(value):
    return [lax.ppermute(value, AXES, depth_perm(s)) for s in (1, -1, 2)]


def core_swap(value):
    return lax.ppermute(value, "row", [(0, 1), (1, 0)])


def limit(mib):
    return pltpu.CompilerParams(vmem_limit_bytes=mib * MIB)


def pick_kernel(moved, panels, *refs):
    staged = (len(refs) - 4) // 2
    sources, out, copies_to = refs[:staged], refs[staged], refs[staged + 1 : 2 * staged + 1]
    buf, sem, stage_sem = refs[-3:]
    me = lax.axis_index("blk")
    part = lax.axis_index("exc") & (SLICES - 1)
    slots = [jnp.int32(0)] * CAP
    count = jnp.int32(0)
    for i in range(MOVED):
        block = moved[i]
        mine = (block >> 3) == me
        slots = [jnp.where(mine & (count == s), block & 7, slots[s]) for s in range(CAP)]
        count = count + mine.astype(jnp.int32)
    copies = []
    for s in range(CAP):
        copy = pltpu.make_async_copy(panels.at[slots[s]], buf.at[s], sem.at[s])
        copy.start()
        copies.append(copy)
    stages = []
    for n in range(staged):
        copy = pltpu.make_async_copy(sources[n], copies_to[n], stage_sem.at[n])
        copy.start()
        stages.append(copy)
    width = buf.shape[2]
    share = out.shape[1]
    rows = lax.broadcasted_iota(jnp.int32, (share, width), 0)
    cols = lax.broadcasted_iota(jnp.int32, (share, width), 1)
    chosen = jnp.where(cols == rows + part * share, 1.0, 0.0).astype(jnp.bfloat16)
    for s in range(CAP):
        copies[s].wait()
        out[s] = lax.dot_general(chosen, buf[s], NT, preferred_element_type=jnp.float32).astype(jnp.bfloat16)
    for copy in stages:
        copy.wait()


def pick(moved_blocks, panels, *others):
    blocks, rows, width = panels.shape
    share = width // SLICES
    n = len(others)
    in_hbm = [pltpu.with_memory_space_constraint(value, pltpu.HBM) for value in (panels, *others)]
    picked = jax.ShapeDtypeStruct((CAP, share, rows), jnp.bfloat16)
    return pl.pallas_call(
        pick_kernel,
        out_shape=[picked] + [jax.ShapeDtypeStruct(value.shape, value.dtype) for value in others],
        in_specs=[SMEM] + [pl.BlockSpec(memory_space=pltpu.HBM)] * (1 + n),
        out_specs=[VMEM] * (1 + n),
        scratch_shapes=[
            pltpu.VMEM((CAP, rows, width), jnp.bfloat16),
            pltpu.SemaphoreType.DMA((CAP,)),
            pltpu.SemaphoreType.DMA((n,)),
        ],
        compiler_params=limit(12),
        name="pick",
    )(moved_blocks, *in_hbm)


def route_kernel(moved, a0, a1, a2, a3, o0, o1, o2, o3, count, rank):
    me = lax.axis_index("blk")
    core = lax.axis_index("row")
    y, x = me >> 2, me & 3
    on_x = core == 0
    here = jnp.where(on_x, x, y)
    across = jnp.where(on_x, y, x)
    for g in range(SIDE * SIDE):
        count[g] = 0
    for i in range(MOVED):
        owner = moved[i] >> 3
        seen = count[owner]
        rank[i] = seen
        count[owner] = seen + 1
    arrivals = (a0, a1, a2, a3)
    for t, out in enumerate((o0, o1, o2, o3)):
        target = (across + t) & 3
        block = jnp.where(on_x, target * SIDE + here, here * SIDE + target)
        for s in range(2):
            index = 2 * block + s
            owner = moved[index] >> 3
            slot = rank[index]
            owner_y, owner_x = owner >> 2, owner & 3
            found = jnp.where(on_x, owner_y, owner_x) == across
            source = (here - jnp.where(on_x, owner_x, owner_y)) & 3
            value = jnp.zeros(out.shape[1:], out.dtype)
            for k in range(SIDE):
                value = jnp.where(found & (source == k), arrivals[k][slot], value)
            out[s] = value


def route(moved_blocks, arrivals):
    _, share, rows = arrivals[0].shape
    return pl.pallas_call(
        route_kernel,
        out_shape=[jax.ShapeDtypeStruct((2, share, rows), jnp.bfloat16)] * SIDE,
        in_specs=[SMEM] + [VMEM] * SIDE,
        out_specs=[VMEM] * SIDE,
        scratch_shapes=[pltpu.SMEM((SIDE * SIDE,), jnp.int32), pltpu.SMEM((MOVED,), jnp.int32)],
        compiler_params=limit(6),
        name="route",
    )(moved_blocks, *arrivals)


def radiate_kernel(a0, a1, a2, a3, geometry, columns, keep, give):
    core = lax.axis_index("row")
    partial = []
    for s in range(2):
        panel = (a0[s] + a1[s]) + (a2[s] + a3[s])
        columns[s] = panel
        partial.append(jnp.dot(panel, geometry[s], preferred_element_type=jnp.float32))
    keep[...] = jnp.where(core == 0, partial[0], partial[1])
    give[...] = jnp.where(core == 0, partial[1], partial[0])


def radiate(arrivals, geometry):
    _, share, rows = arrivals[0].shape
    half = jax.ShapeDtypeStruct((share, geometry.shape[2]), jnp.float32)
    return pl.pallas_call(
        radiate_kernel,
        out_shape=[jax.ShapeDtypeStruct((2, share, rows), jnp.bfloat16), half, half],
        in_specs=[VMEM] * 5,
        out_specs=[VMEM] * 3,
        compiler_params=limit(8),
        name="radiate",
    )(*arrivals, geometry)


def assemble_kernel(own, up, down, far, out):
    z = lax.axis_index("exc")
    share = own.shape[0]
    for shift, value in ((0, own), (1, up), (-1, down), (2, far)):
        start = pl.multiple_of(((z - shift) & (SLICES - 1)) * share, share)
        out[pl.ds(start, share), :] = value[...]


def assemble(pieces):
    share, width = pieces[0].shape
    return pl.pallas_call(
        assemble_kernel,
        out_shape=jax.ShapeDtypeStruct((SLICES * share, width), jnp.bfloat16),
        in_specs=[VMEM] * 4,
        out_specs=VMEM,
        compiler_params=limit(4),
        name="assemble",
    )(*pieces)


def couple(pieces, partners, translation, patterns, so_far=None):
    n = len(pieces)
    moved, columns, width = translation.shape
    _, rows, _ = patterns.shape
    basis = pieces[0][2].shape[1]
    together = 4

    def kernel(partners_ref, trans, patt, *refs):
        piece_refs = refs[:n]
        out, buf, sem = refs[-3:]
        me = lax.axis_index("blk")
        core = lax.axis_index("row")
        y, x = me >> 2, me & 3
        copies = []
        for p, (leg, own, _) in enumerate(pieces):
            holder = core if own else 1 - core
            near = jnp.where(holder == 0, x, y)
            across = (jnp.where(holder == 0, y, x) - leg) & 3
            ids = []
            for k in range(SIDE):
                first = (near - k) & 3
                block = jnp.where(holder == 0, across * SIDE + first, first * SIDE + across)
                ids.append(2 * block + holder)
            rads = [piece_refs[p][k].T for k in range(SIDE)]
            for first in range(0, columns, together):
                for k in range(SIDE):
                    parts = []
                    for j in range(first, first + together):
                        pattern = patt[partners_ref[j, ids[k]] & 7].astype(jnp.float32)
                        parts.append((pattern * trans[ids[k], j : j + 1, :]).astype(jnp.bfloat16))
                    weighted = jnp.concatenate(parts, axis=0)
                    block = jnp.dot(weighted, rads[k], preferred_element_type=jnp.float32)
                    buf[p, k, first : first + together] = block.astype(jnp.bfloat16).reshape(together, rows, basis)
            for k in range(SIDE):
                copy = pltpu.make_async_copy(buf.at[p, k], out.at[ids[k]], sem.at[p, k])
                copy.start()
                copies.append(copy)
        for copy in copies:
            copy.wait()

    operands = [partners, translation, patterns, *[piece[2] for piece in pieces]]
    in_specs = [SMEM] + [VMEM] * (2 + n)
    aliases = {}
    if so_far is not None:
        in_specs.append(pl.BlockSpec(memory_space=pl.ANY))
        aliases = {len(operands): 0}
        operands.append(so_far)
    return pl.pallas_call(
        kernel,
        out_shape=jax.ShapeDtypeStruct((moved, columns, rows, basis), jnp.bfloat16),
        in_specs=in_specs,
        out_specs=pl.BlockSpec(memory_space=pl.ANY),
        scratch_shapes=[
            pltpu.VMEM((n, SIDE, columns, rows, basis), jnp.bfloat16),
            pltpu.SemaphoreType.DMA((n, SIDE)),
        ],
        input_output_aliases=aliases,
        compiler_params=limit(14),
        cost_estimate=pl.CostEstimate(
            flops=2 * n * SIDE * columns * rows * width * basis,
            bytes_accessed=n * SIDE * columns * rows * basis * 2,
            transcendentals=0,
        ),
        name="couple",
    )(*operands)


def project_kernel(excitations, own, up, down, far, out, panel):
    z = lax.axis_index("exc")
    share = own.shape[1]
    for shift, value in ((0, own), (1, up), (-1, down), (2, far)):
        start = pl.multiple_of(((z - shift) & (SLICES - 1)) * share, share)
        panel[:, pl.ds(start, share), :] = value[...]
    for s in range(2):
        out[s] = lax.dot_general(excitations[s], panel[s], NT, preferred_element_type=jnp.float32)


def project(excitations, pieces):
    moved, count, rows = excitations.shape
    basis = SLICES * pieces[0].shape[1]
    return pl.pallas_call(
        project_kernel,
        out_shape=jax.ShapeDtypeStruct((moved, count, basis), jnp.float32),
        in_specs=[VMEM] * 5,
        out_specs=VMEM,
        scratch_shapes=[pltpu.VMEM((2, basis, rows), jnp.bfloat16)],
        compiler_params=limit(6),
        name="project",
    )(excitations, *pieces)


def on_device(panels, patterns, geometry, excitations, moved_blocks, partners, translation):
    outgoing, geometry, translation, patterns, excitations, partners = pick(
        moved_blocks, panels, geometry, translation, patterns, excitations, partners.T
    )
    routed = route(moved_blocks, [outgoing, *plane_send(outgoing, True)])
    landed = {s: lax.ppermute(routed[s], AXES, plane_perm(s, False)) for s in ORDER}
    columns, keep, give = radiate([routed[0], *[landed[s] for s in range(1, SIDE)]], geometry)
    radiation = (keep + core_swap(give)).astype(jnp.bfloat16)
    columns, radiation = lax.optimization_barrier((columns, radiation))
    mine = assemble([radiation, *depth_send(radiation)])
    pieces = [columns, *depth_send(columns)]
    stack = jnp.stack([mine, *plane_send(mine, True)])
    arrived = plane_send(stack, False)
    couplings = couple([(0, True, stack)], partners, translation, patterns)
    couplings, *arrived = lax.optimization_barrier((couplings, *arrived))
    stack_other = core_swap(stack)
    arrived_other = [core_swap(value) for value in arrived]
    own = [(leg, True, arrived[leg - 1]) for leg in range(1, SIDE)]
    other = [(leg, False, arrived_other[leg - 1]) for leg in range(1, SIDE)]
    couplings = couple(own, partners, translation, patterns, couplings)
    couplings, *pieces = lax.optimization_barrier((couplings, *pieces))
    projected = project(excitations, pieces)
    couplings = couple([(0, False, stack_other), *other], partners, translation, patterns, couplings)
    projected = projected + core_swap(projected)
    return (couplings, projected)


def solution(mesh):
    placed = (
        P("blk", "row", None),
        P("blk", "row", None),
        P("blk", "row", None),
        P("blk", "exc", "row"),
        P(),
        P(None, ("blk", "exc")),
        P(None, ("blk", "exc"), None),
    )
    return jax.shard_map(
        on_device,
        mesh=mesh,
        in_specs=placed,
        out_specs=(P(None, ("blk", "exc"), "row", None), P("blk", "exc", None)),
        check_vma=False,
    )
```

time: 123 us -> 75.9 us (0.62); the launches traced: 122 us -> 75.8 us
  Pallas kernels: 39.2 us -> 14.9 us
  between operations: 14.2 us -> 0.88 us
  waiting for transfers between devices: 12.2 us -> 19.9 us
  starting transfers between devices: 45 us -> 38.8 us
  local copies, waits for them, and re-layouts: 6.08 us -> 0.65 us
  other arithmetic: 4.85 us -> 0.69 us
    pallas_call x3, Pallas kernels: 27.4 us -> 10.1 us  [couple(): pl.pallas_call(kernel, out_shape=jax.ShapeDtypeStruct((moved, columns, ro...]
    ppermute x13 -> x15, waiting for transfers between devices: 7.97 us -> 13.9 us  [the longest x9 9.14 us: plane_send(): sent = {s: lax.ppermute(value, AXES, plane_perm(s, first)) for s in ORDER}]
    unnamed x47 -> x2, local copies, waits for them, and re-layouts: 6.08 us -> 0.65 us
    ppermute x13 -> x15, starting transfers between devices: 25.8 us -> 22.2 us  [the longest x9 15.1 us: plane_send(): sent = {s: lax.ppermute(value, AXES, plane_perm(s, first)) for s in ORDER}]
    ppermute x9 -> x6, starting transfers between devices: 14.7 us -> 12 us  [core_swap(): return lax.ppermute(value, 'row', [(0, 1), (1, 0)])]
    pallas_call x1, Pallas kernels: 2.54 us -> 0.38 us  [radiate(): pl.pallas_call(radiate_kernel, out_shape=[jax.ShapeDtypeStruct((2, share,...]
    pallas_call x1, Pallas kernels: 2.43 us -> 0.43 us  [project(): pl.pallas_call(project_kernel, out_shape=jax.ShapeDtypeStruct((moved, cou...]
    concatenate x3 -> x0, other arithmetic: 1.91 us -> none  [the longest x1 0.67 us: on_device(): jnp.concatenate([piece_ids(y, x, core, 0), piece_ids(y, x, other, 0)])]
  transfers between devices with their start and end apart: 26 -> 24, of which waited for: 10 -> 12; matrix products, arithmetic and copies ran while one was open for 4% -> 1% of each run, Pallas kernels for 26% -> 8%
where the time goes in v2:
time: 75.9 us; the launch traced here: 75.8 us
  starting transfers between devices  38.8 us (51%)
  waiting for transfers between devices  19.9 us (26%)
  Pallas kernels  14.9 us (20%)
  between operations  0.88 us (1%)
    ppermute x9, starting transfers between devices, plane_send(): sent = {s: lax.ppermute(value, AXES, plane_perm(s, first)) for s in ORDER}  15.1 us
    ppermute x6, starting transfers between devices, core_swap(): return lax.ppermute(value, 'row', [(0, 1), (1, 0)])  12 us
    pallas_call x3, Pallas kernels, couple(): pl.pallas_call(kernel, out_shape=jax.ShapeDtypeStruct((moved, columns, ro...  10.1 us
    ppermute x9, waiting for transfers between devices, plane_send(): sent = {s: lax.ppermute(value, AXES, plane_perm(s, first)) for s in ORDER}  9.14 us
    ppermute x6, starting transfers between devices, depth_send(): return [lax.ppermute(value, AXES, depth_perm(s)) for s in (1, -1, 2)]  7.09 us
    ppermute x6, waiting for transfers between devices, depth_send(): return [lax.ppermute(value, AXES, depth_perm(s)) for s in (1, -1, 2)]  4.77 us
    ppermute x3, starting transfers between devices, on_device(): lax.ppermute(routed[s], AXES, plane_perm(s, False))  4.6 us
    ppermute x3, waiting for transfers between devices, on_device(): lax.ppermute(routed[s], AXES, plane_perm(s, False))  4.19 us
  transfers between devices with their start and end apart: 24, of which 12 were waited for; matrix products, arithmetic and copies ran while one was open for 1% of the time, Pallas kernels for 8%

profile of v2, /device:TPU:1, one launch (start us, length us, event | category | flops | bytes accessed | tf_op | source)
XLA Modules:
  0.0 75.8 jit_solution(11338069679525931031)
XLA Ops:
  0.6 0.0 copy-start
  0.6 0.6 copy-done
  1.3 3.1 %pick.1 = (bf16[3,32,1536]{2,1,0:T(8,128)(2,1)S(1)}, bf16[2,1536,256]{2,1,0:T(8,128)(2,1)S(1)}, f32[32,16,256]{2,1,0:T(8,128)S(1)}, bf16[8,64,256]{2,1,0:T(8,128...) custom-call(s32[32]{0:T(128)S(1)} %copy-done, bf16[8,1536,128]{2,1,0:T(8,128)(2,1)} %panels.1, ...), custom_call_target="tpu_custom_call" | custom-call | tf_op jit(solution)/shard_map/pick/pallas_call | solution.py:106
  4.4 2.2 %collective-permute-start = (bf16[3,32,1536]{2,1,0:T(8,128)(2,1)S(1)}, bf16[3,32,1536]{2,1,0:T(8,128)(2,1)S(1)}, u32[]{:S(2)}, u32[]{:S(2)}) collective-permute-start(bf16[3,32,1536]{2,1,0:T(8,128)(2,1)S(1)} %get-tuple-element.29.a0), channel_id=1, source_target_pairs={{0,16},{1,65},{2,18},{3,67},{4,20},{5,69},{6,22},{7,71},{8,24},{9,... | collective-permute-start | bytes 884744 | tf_op jit(solution)/shard_map/ppermute | solution.py:49
  6.6 2.6 %collective-permute-start.1 = (bf16[3,32,1536]{2,1,0:T(8,128)(2,1)S(1)}, bf16[3,32,1536]{2,1,0:T(8,128)(2,1)S(1)}, u32[]{:S(2)}, u32[]{:S(2)}) collective-permute-start(bf16[3,32,1536]{2,1,0:T(8,128)(2,1)S(1)} %get-tuple-element.29.a0), channel_id=1, source_target_pairs={{0,32},{1,129},{2,34},{3,131},{4,36},{5,133},{6,38},{7,135},{8,40}... | collective-permute-start | bytes 884744 | tf_op jit(solution)/shard_map/ppermute | solution.py:49
  9.3 1.1 %collective-permute-start.2 = (bf16[3,32,1536]{2,1,0:T(8,128)(2,1)S(1)}, bf16[3,32,1536]{2,1,0:T(8,128)(2,1)S(1)}, u32[]{:S(2)}, u32[]{:S(2)}) collective-permute-start(bf16[3,32,1536]{2,1,0:T(8,128)(2,1)S(1)} %get-tuple-element.29.a0), channel_id=1, source_target_pairs={{0,48},{1,193},{2,50},{3,195},{4,52},{5,197},{6,54},{7,199},{8,56}... | collective-permute-start | bytes 884744 | tf_op jit(solution)/shard_map/ppermute | solution.py:49
  10.3 2.2 %collective-permute-done.a1 = bf16[3,32,1536]{2,1,0:T(8,128)(2,1)S(1)} collective-permute-done((bf16[3,32,1536]{2,1,0:T(8,128)(2,1)S(1)}, bf16[3,32,1536]{2,1,0:T(8,128)(2,1)S(1)}, u32[]{:S(2)}, u32[]{:S(2)}) %collective-permute-start) | collective-permute-done | bytes 294944 | tf_op jit(solution)/shard_map/ppermute | solution.py:49
  12.5 4.3 %collective-permute-done.1.a2 = bf16[3,32,1536]{2,1,0:T(8,128)(2,1)S(1)} collective-permute-done((bf16[3,32,1536]{2,1,0:T(8,128)(2,1)S(1)}, bf16[3,32,1536]{2,1,0:T(8,128)(2,1)S(1)}, u32[]{:S(2)}, u32[]{:S(2)}) %collective-permute-start.1) | collective-permute-done | bytes 294944 | tf_op jit(solution)/shard_map/ppermute | solution.py:49
  16.8 0.0 collective-permute-done.2.a3
  16.8 0.9 %route.1 = (bf16[2,32,1536]{2,1,0:T(8,128)(2,1)S(1)}, bf16[2,32,1536]{2,1,0:T(8,128)(2,1)S(1)}, bf16[2,32,1536]{2,1,0:T(8,128)(2,1)S(1)}, bf16[2,32,1536]{2,1,0:T(8,128)(2,1)S(1)}) custom-call(s32[32]{0:T(128)S(1)} %copy-done, bf16[3,32,1536]{2,1,0:T(8,128)(2,1)S(1)} %get-tuple-element.29.a0, bf16[3,32,1536]{2,1,0:T(8,128)(2,1)S(1)} %collective-permute-done.a1, ...), custom_call_target="tpu_custom_call" | custom-call | tf_op jit(solution)/shard_map/route/pallas_call | solution.py:154
  17.7 1.0 %collective-permute-start.3 = (bf16[2,32,1536]{2,1,0:T(8,128)(2,1)S(1)}, bf16[2,32,1536]{2,1,0:T(8,128)(2,1)S(1)}, u32[]{:S(2)}, u32[]{:S(2)}) collective-permute-start(bf16[2,32,1536]{2,1,0:T(8,128)(2,1)S(1)} %get-tuple-element.31), channel_id=1, source_target_pairs={{0,64},{1,17},{2,66},{3,19},{4,68},{5,21},{6,70},{7,23},{8,72},{9,... | collective-permute-start | bytes 589832 | tf_op jit(solution)/shard_map/ppermute | solution.py:305
  18.7 2.5 %collective-permute-start.4 = (bf16[2,32,1536]{2,1,0:T(8,128)(2,1)S(1)}, bf16[2,32,1536]{2,1,0:T(8,128)(2,1)S(1)}, u32[]{:S(2)}, u32[]{:S(2)}) collective-permute-start(bf16[2,32,1536]{2,1,0:T(8,128)(2,1)S(1)} %get-tuple-element.32), channel_id=1, source_target_pairs={{0,128},{1,33},{2,130},{3,35},{4,132},{5,37},{6,134},{7,39},{8,136... | collective-permute-start | bytes 589832 | tf_op jit(solution)/shard_map/ppermute | solution.py:305
  21.2 1.1 %collective-permute-start.5 = (bf16[2,32,1536]{2,1,0:T(8,128)(2,1)S(1)}, bf16[2,32,1536]{2,1,0:T(8,128)(2,1)S(1)}, u32[]{:S(2)}, u32[]{:S(2)}) collective-permute-start(bf16[2,32,1536]{2,1,0:T(8,128)(2,1)S(1)} %get-tuple-element.33), channel_id=1, source_target_pairs={{0,192},{1,49},{2,194},{3,51},{4,196},{5,53},{6,198},{7,55},{8,200... | collective-permute-start | bytes 589832 | tf_op jit(solution)/shard_map/ppermute | solution.py:305
  22.3 1.2 %collective-permute-done.3.a1 = bf16[2,32,1536]{2,1,0:T(8,128)(2,1)S(1)} collective-permute-done((bf16[2,32,1536]{2,1,0:T(8,128)(2,1)S(1)}, bf16[2,32,1536]{2,1,0:T(8,128)(2,1)S(1)}, u32[]{:S(2)}, u32[]{:S(2)}) %collective-permute-start.3) | collective-permute-done | bytes 196640 | tf_op jit(solution)/shard_map/ppermute | solution.py:305
  23.5 2.8 %collective-permute-done.4.a2 = bf16[2,32,1536]{2,1,0:T(8,128)(2,1)S(1)} collective-permute-done((bf16[2,32,1536]{2,1,0:T(8,128)(2,1)S(1)}, bf16[2,32,1536]{2,1,0:T(8,128)(2,1)S(1)}, u32[]{:S(2)}, u32[]{:S(2)}) %collective-permute-start.4) | collective-permute-done | bytes 196640 | tf_op jit(solution)/shard_map/ppermute | solution.py:305
  26.3 0.2 collective-permute-done.5.a3
  26.5 0.4 radiate.1
  26.9 4.1 %collective-permute-start.6 = (f32[32,256]{1,0:T(8,128)S(1)}, f32[32,256]{1,0:T(8,128)S(1)}, u32[]{:S(2)}, u32[]{:S(2)}) collective-permute-start(f32[32,256]{1,0:T(8,128)S(1)} %get-tuple-element.37), channel_id=1, source_target_pairs={{0,1},{1,0},{2,3},{3,2},{4,5},{5,4},{6,7},{7,6},{8,9},{9,8},{10,11... | collective-permute-start | bytes 98312 | tf_op jit(solution)/shard_map/ppermute | solution.py:58
  30.9 0.9 %collective-permute-done.6 = f32[32,256]{1,0:T(8,128)S(1)} collective-permute-done((f32[32,256]{1,0:T(8,128)S(1)}, f32[32,256]{1,0:T(8,128)S(1)}, u32[]{:S(2)}, u32[]{:S(2)}) %collective-permute-start.6) | collective-permute-done | bytes 32800 | tf_op jit(solution)/shard_map/ppermute | solution.py:58
  31.8 0.4 collective-permute-start.7
  32.2 4.0 %collective-permute-start.8 = (bf16[32,256]{1,0:T(8,128)(2,1)S(1)}, bf16[32,256]{1,0:T(8,128)(2,1)S(1)}, u32[]{:S(2)}, u32[]{:S(2)}) collective-permute-start(bf16[32,256]{1,0:T(8,128)(2,1)S(1)} %add_convert_fusion.own), channel_id=1, source_target_pairs={{0,14},{1,15},{2,0},{3,1},{4,2},{5,3},{6,4},{7,5},{8,6},{9,7},{10,... | collective-permute-start | bytes 49160 | tf_op jit(solution)/shard_map/ppermute | solution.py:54
  36.2 0.0 collective-permute-start.9
  36.2 1.0 %collective-permute-done.7.up = bf16[32,256]{1,0:T(8,128)(2,1)S(1)} collective-permute-done((bf16[32,256]{1,0:T(8,128)(2,1)S(1)}, bf16[32,256]{1,0:T(8,128)(2,1)S(1)}, u32[]{:S(2)}, u32[]{:S(2)}) %collective-permute-start.7) | collective-permute-done | bytes 16416 | tf_op jit(solution)/shard_map/ppermute | solution.py:54
  37.3 0.0 collective-permute-done.8.down
  37.3 3.7 %collective-permute-done.9.far = bf16[32,256]{1,0:T(8,128)(2,1)S(1)} collective-permute-done((bf16[32,256]{1,0:T(8,128)(2,1)S(1)}, bf16[32,256]{1,0:T(8,128)(2,1)S(1)}, u32[]{:S(2)}, u32[]{:S(2)}) %collective-permute-start.9) | collective-permute-done | bytes 16416 | tf_op jit(solution)/shard_map/ppermute | solution.py:54
  41.0 1.4 %collective-permute-start.10 = (bf16[128,256]{1,0:T(8,128)(2,1)S(1)}, bf16[128,256]{1,0:T(8,128)(2,1)S(1)}, u32[]{:S(2)}, u32[]{:S(2)}) collective-permute-start(bf16[128,256]{1,0:T(8,128)(2,1)S(1)} %assemble.1), channel_id=1, source_target_pairs={{0,16},{1,65},{2,18},{3,67},{4,20},{5,69},{6,22},{7,71},{8,24},{9,... | collective-permute-start | bytes 196616 | tf_op jit(solution)/shard_map/ppermute | solution.py:49
  42.4 2.0 %collective-permute-start.11 = (bf16[128,256]{1,0:T(8,128)(2,1)S(1)}, bf16[128,256]{1,0:T(8,128)(2,1)S(1)}, u32[]{:S(2)}, u32[]{:S(2)}) collective-permute-start(bf16[128,256]{1,0:T(8,128)(2,1)S(1)} %assemble.1), channel_id=1, source_target_pairs={{0,32},{1,129},{2,34},{3,131},{4,36},{5,133},{6,38},{7,135},{8,40}... | collective-permute-start | bytes 196616 | tf_op jit(solution)/shard_map/ppermute | solution.py:49
  44.4 1.3 %collective-permute-start.12 = (bf16[128,256]{1,0:T(8,128)(2,1)S(1)}, bf16[128,256]{1,0:T(8,128)(2,1)S(1)}, u32[]{:S(2)}, u32[]{:S(2)}) collective-permute-start(bf16[128,256]{1,0:T(8,128)(2,1)S(1)} %assemble.1), channel_id=1, source_target_pairs={{0,48},{1,193},{2,50},{3,195},{4,52},{5,197},{6,54},{7,199},{8,56}... | collective-permute-start | bytes 196616 | tf_op jit(solution)/shard_map/ppermute | solution.py:49
  45.7 0.0 collective-permute-done.10
  45.7 1.3 %collective-permute-done.11 = bf16[128,256]{1,0:T(8,128)(2,1)S(1)} collective-permute-done((bf16[128,256]{1,0:T(8,128)(2,1)S(1)}, bf16[128,256]{1,0:T(8,128)(2,1)S(1)}, u32[]{:S(2)}, u32[]{:S(2)}) %collective-permute-start.11) | collective-permute-done | bytes 65568 | tf_op jit(solution)/shard_map/ppermute | solution.py:49
  47.0 0.8 %collective-permute-done.12 = bf16[128,256]{1,0:T(8,128)(2,1)S(1)} collective-permute-done((bf16[128,256]{1,0:T(8,128)(2,1)S(1)}, bf16[128,256]{1,0:T(8,128)(2,1)S(1)}, u32[]{:S(2)}, u32[]{:S(2)}) %collective-permute-start.12) | collective-permute-done | bytes 65568 | tf_op jit(solution)/shard_map/ppermute | solution.py:49
  47.9 1.4 %collective-permute-start.14 = (bf16[4,128,256]{2,1,0:T(8,128)(2,1)S(1)}, bf16[4,128,256]{2,1,0:T(8,128)(2,1)S(1)}, u32[]{:S(2)}, u32[]{:S(2)}) collective-permute-start(bf16[4,128,256]{2,1,0:T(8,128)(2,1)S(1)} %pad_maximum_fusion.refs_0_), channel_id=1, source_target_pairs={{0,64},{1,17},{2,66},{3,19},{4,68},{5,21},{6,70},{7,23},{8,72},{9,... | collective-permute-start | bytes 786440 | tf_op jit(solution)/shard_map/ppermute | solution.py:49
  49.3 2.1 %collective-permute-start.15 = (bf16[4,128,256]{2,1,0:T(8,128)(2,1)S(1)}, bf16[4,128,256]{2,1,0:T(8,128)(2,1)S(1)}, u32[]{:S(2)}, u32[]{:S(2)}) collective-permute-start(bf16[4,128,256]{2,1,0:T(8,128)(2,1)S(1)} %pad_maximum_fusion.refs_0_), channel_id=1, source_target_pairs={{0,128},{1,33},{2,130},{3,35},{4,132},{5,37},{6,134},{7,39},{8,136... | collective-permute-start | bytes 786440 | tf_op jit(solution)/shard_map/ppermute | solution.py:49
  51.4 1.0 %collective-permute-start.16 = (bf16[4,128,256]{2,1,0:T(8,128)(2,1)S(1)}, bf16[4,128,256]{2,1,0:T(8,128)(2,1)S(1)}, u32[]{:S(2)}, u32[]{:S(2)}) collective-permute-start(bf16[4,128,256]{2,1,0:T(8,128)(2,1)S(1)} %pad_maximum_fusion.refs_0_), channel_id=1, source_target_pairs={{0,192},{1,49},{2,194},{3,51},{4,196},{5,53},{6,198},{7,55},{8,200... | collective-permute-start | bytes 786440 | tf_op jit(solution)/shard_map/ppermute | solution.py:49
  52.4 0.0 collective-permute-start.20
  52.4 2.7 %collective-permute-start.21 = (bf16[2,32,1536]{2,1,0:T(8,128)(2,1)S(1)}, bf16[2,32,1536]{2,1,0:T(8,128)(2,1)S(1)}, u32[]{:S(2)}, u32[]{:S(2)}) collective-permute-start(bf16[2,32,1536]{2,1,0:T(8,128)(2,1)S(1)} %get-tuple-element.46.own), channel_id=1, source_target_pairs={{0,14},{1,15},{2,0},{3,1},{4,2},{5,3},{6,4},{7,5},{8,6},{9,7},{10,... | collective-permute-start | bytes 589832 | tf_op jit(solution)/shard_map/ppermute | solution.py:54
  55.1 0.0 collective-permute-done.14.refs_0_
  55.1 0.0 collective-permute-start.22
  55.1 2.4 %couple.3.refs_3_ = bf16[32,16,64,128]{3,2,1,0:T(8,128)(2,1)} custom-call(s32[16,32]{1,0:T(8,128)S(1)} %get-tuple-element.26.partners_ref, f32[32,16,256]{2,1,0:T(8,128)S(1)} %get-tuple-element.27.trans, bf16[8,64,256]{2,1,0:T(8,128)(2,1)S(1)} %get-tuple-element.28.patt, bf16[4,128,256]{2,1,0:T(8,128)(2,1)S(1)} %pad_maximum_fusion.refs_0_), custom_call_target="tpu_custom_call" | custom-call | flops 268435456 | bytes 1048576 | tf_op jit(solution)/shard_map/couple/pallas_call | solution.py:256
  57.5 0.5 collective-permute-done.15.refs_1_
  58.0 4.4 %collective-permute-start.13 = (bf16[4,128,256]{2,1,0:T(8,128)(2,1)S(1)}, bf16[4,128,256]{2,1,0:T(8,128)(2,1)S(1)}, u32[]{:S(2)}, u32[]{:S(2)}) collective-permute-start(bf16[4,128,256]{2,1,0:T(8,128)(2,1)S(1)} %pad_maximum_fusion.refs_0_), channel_id=1, source_target_pairs={{0,1},{1,0},{2,3},{3,2},{4,5},{5,4},{6,7},{7,6},{8,9},{9,8},{10,11... | collective-permute-start | bytes 786440 | tf_op jit(solution)/shard_map/ppermute | solution.py:58
  62.4 0.0 collective-permute-done.16.refs_2_
  62.4 0.1 collective-permute-start.17
  62.5 0.0 collective-permute-done.20.up
  62.5 2.8 %collective-permute-start.18 = (bf16[4,128,256]{2,1,0:T(8,128)(2,1)S(1)}, bf16[4,128,256]{2,1,0:T(8,128)(2,1)S(1)}, u32[]{:S(2)}, u32[]{:S(2)}) collective-permute-start(bf16[4,128,256]{2,1,0:T(8,128)(2,1)S(1)} %collective-permute-done.15.refs_1_), channel_id=1, source_target_pairs={{0,1},{1,0},{2,3},{3,2},{4,5},{5,4},{6,7},{7,6},{8,9},{9,8},{10,11... | collective-permute-start | bytes 786440 | tf_op jit(solution)/shard_map/ppermute | solution.py:58
  65.3 0.0 collective-permute-done.21.down
  65.3 0.0 collective-permute-start.19
  65.3 3.6 %couple.4.refs_4_ = bf16[32,16,64,128]{3,2,1,0:T(8,128)(2,1)} custom-call(s32[16,32]{1,0:T(8,128)S(1)} %get-tuple-element.26.partners_ref, f32[32,16,256]{2,1,0:T(8,128)S(1)} %get-tuple-element.27.trans, bf16[8,64,256]{2,1,0:T(8,128)(2,1)S(1)} %get-tuple-element.28.patt, ...), custom_call_target="tpu_custom_call", output_to_operand_aliasing={{}: (6, {})} | custom-call | flops 805306368 | bytes 3145728 | tf_op jit(solution)/shard_map/couple/pallas_call | solution.py:256
  68.8 0.0 collective-permute-done.22.far
  68.9 0.4 project.1
  69.3 0.6 collective-permute-start.23
  69.9 0.9 %collective-permute-done.23 = f32[2,96,128]{2,1,0:T(8,128)S(1)} collective-permute-done((f32[2,96,128]{2,1,0:T(8,128)S(1)}, f32[2,96,128]{2,1,0:T(8,128)S(1)}, u32[]{:S(2)}, u32[]{:S(2)}) %collective-permute-start.23) | collective-permute-done | bytes 98336 | tf_op jit(solution)/shard_map/ppermute | solution.py:58
  70.8 0.7 add.7
  71.5 0.0 collective-permute-done.13.refs_0_
  71.5 0.0 collective-permute-done.17.refs_1_
  71.5 0.0 collective-permute-done.18.refs_2_
  71.5 0.0 collective-permute-done.19.refs_3_
  71.5 4.2 %couple.5 = bf16[32,16,64,128]{3,2,1,0:T(8,128)(2,1)} custom-call(s32[16,32]{1,0:T(8,128)S(1)} %get-tuple-element.26.partners_ref, f32[32,16,256]{2,1,0:T(8,128)S(1)} %get-tuple-element.27.trans, bf16[8,64,256]{2,1,0:T(8,128)(2,1)S(1)} %get-tuple-element.28.patt, ...), custom_call_target="tpu_custom_call", output_to_operand_aliasing={{}: (7, {})} | custom-call | flops 1073741824 | bytes 4194304 | tf_op jit(solution)/shard_map/couple/pallas_call | solution.py:256
  (3 shorter events, 0.1 us)
Async XLA Ops:
  0.6 0.7 copy-start
  4.4 8.0 %collective-permute-start = (bf16[3,32,1536]{2,1,0:T(8,128)(2,1)S(1)}, bf16[3,32,1536]{2,1,0:T(8,128)(2,1)S(1)}, u32[]{:S(2)}, u32[]{:S(2)}) collective-permute-start(bf16[3,32,1536]{2,1,0:T(8,128)(2,1)S(1)} %get-tuple-element.29.a0), channel_id=1, source_target_pairs={{0,16},{1,65},{2,18},{3,67},{4,20},{5,69},{6,22},{7,71},{8,24},{9,... | collective-permute-start | bytes 884744 | tf_op jit(solution)/shard_map/ppermute | solution.py:49
  6.6 10.2 %collective-permute-start.1 = (bf16[3,32,1536]{2,1,0:T(8,128)(2,1)S(1)}, bf16[3,32,1536]{2,1,0:T(8,128)(2,1)S(1)}, u32[]{:S(2)}, u32[]{:S(2)}) collective-permute-start(bf16[3,32,1536]{2,1,0:T(8,128)(2,1)S(1)} %get-tuple-element.29.a0), channel_id=1, source_target_pairs={{0,32},{1,129},{2,34},{3,131},{4,36},{5,133},{6,38},{7,135},{8,40}... | collective-permute-start | bytes 884744 | tf_op jit(solution)/shard_map/ppermute | solution.py:49
  9.3 7.6 %collective-permute-start.2 = (bf16[3,32,1536]{2,1,0:T(8,128)(2,1)S(1)}, bf16[3,32,1536]{2,1,0:T(8,128)(2,1)S(1)}, u32[]{:S(2)}, u32[]{:S(2)}) collective-permute-start(bf16[3,32,1536]{2,1,0:T(8,128)(2,1)S(1)} %get-tuple-element.29.a0), channel_id=1, source_target_pairs={{0,48},{1,193},{2,50},{3,195},{4,52},{5,197},{6,54},{7,199},{8,56}... | collective-permute-start | bytes 884744 | tf_op jit(solution)/shard_map/ppermute | solution.py:49
  17.7 5.8 %collective-permute-start.3 = (bf16[2,32,1536]{2,1,0:T(8,128)(2,1)S(1)}, bf16[2,32,1536]{2,1,0:T(8,128)(2,1)S(1)}, u32[]{:S(2)}, u32[]{:S(2)}) collective-permute-start(bf16[2,32,1536]{2,1,0:T(8,128)(2,1)S(1)} %get-tuple-element.31), channel_id=1, source_target_pairs={{0,64},{1,17},{2,66},{3,19},{4,68},{5,21},{6,70},{7,23},{8,72},{9,... | collective-permute-start | bytes 589832 | tf_op jit(solution)/shard_map/ppermute | solution.py:305
  18.7 7.6 %collective-permute-start.4 = (bf16[2,32,1536]{2,1,0:T(8,128)(2,1)S(1)}, bf16[2,32,1536]{2,1,0:T(8,128)(2,1)S(1)}, u32[]{:S(2)}, u32[]{:S(2)}) collective-permute-start(bf16[2,32,1536]{2,1,0:T(8,128)(2,1)S(1)} %get-tuple-element.32), channel_id=1, source_target_pairs={{0,128},{1,33},{2,130},{3,35},{4,132},{5,37},{6,134},{7,39},{8,136... | collective-permute-start | bytes 589832 | tf_op jit(solution)/shard_map/ppermute | solution.py:305
  21.2 5.3 %collective-permute-start.5 = (bf16[2,32,1536]{2,1,0:T(8,128)(2,1)S(1)}, bf16[2,32,1536]{2,1,0:T(8,128)(2,1)S(1)}, u32[]{:S(2)}, u32[]{:S(2)}) collective-permute-start(bf16[2,32,1536]{2,1,0:T(8,128)(2,1)S(1)} %get-tuple-element.33), channel_id=1, source_target_pairs={{0,192},{1,49},{2,194},{3,51},{4,196},{5,53},{6,198},{7,55},{8,200... | collective-permute-start | bytes 589832 | tf_op jit(solution)/shard_map/ppermute | solution.py:305
  26.9 4.9 %collective-permute-start.6 = (f32[32,256]{1,0:T(8,128)S(1)}, f32[32,256]{1,0:T(8,128)S(1)}, u32[]{:S(2)}, u32[]{:S(2)}) collective-permute-start(f32[32,256]{1,0:T(8,128)S(1)} %get-tuple-element.37), channel_id=1, source_target_pairs={{0,1},{1,0},{2,3},{3,2},{4,5},{5,4},{6,7},{7,6},{8,9},{9,8},{10,11... | collective-permute-start | bytes 98312 | tf_op jit(solution)/shard_map/ppermute | solution.py:58
  31.8 5.5 %collective-permute-start.7 = (bf16[32,256]{1,0:T(8,128)(2,1)S(1)}, bf16[32,256]{1,0:T(8,128)(2,1)S(1)}, u32[]{:S(2)}, u32[]{:S(2)}) collective-permute-start(bf16[32,256]{1,0:T(8,128)(2,1)S(1)} %add_convert_fusion.own), channel_id=1, source_target_pairs={{0,2},{1,3},{2,4},{3,5},{4,6},{5,7},{6,8},{7,9},{8,10},{9,11},{10,... | collective-permute-start | bytes 49160 | tf_op jit(solution)/shard_map/ppermute | solution.py:54
  32.2 5.1 %collective-permute-start.8 = (bf16[32,256]{1,0:T(8,128)(2,1)S(1)}, bf16[32,256]{1,0:T(8,128)(2,1)S(1)}, u32[]{:S(2)}, u32[]{:S(2)}) collective-permute-start(bf16[32,256]{1,0:T(8,128)(2,1)S(1)} %add_convert_fusion.own), channel_id=1, source_target_pairs={{0,14},{1,15},{2,0},{3,1},{4,2},{5,3},{6,4},{7,5},{8,6},{9,7},{10,... | collective-permute-start | bytes 49160 | tf_op jit(solution)/shard_map/ppermute | solution.py:54
  36.2 4.8 %collective-permute-start.9 = (bf16[32,256]{1,0:T(8,128)(2,1)S(1)}, bf16[32,256]{1,0:T(8,128)(2,1)S(1)}, u32[]{:S(2)}, u32[]{:S(2)}) collective-permute-start(bf16[32,256]{1,0:T(8,128)(2,1)S(1)} %add_convert_fusion.own), channel_id=1, source_target_pairs={{0,4},{1,5},{2,6},{3,7},{4,8},{5,9},{6,10},{7,11},{8,12},{9,13},{1... | collective-permute-start | bytes 49160 | tf_op jit(solution)/shard_map/ppermute | solution.py:54
  41.0 4.7 %collective-permute-start.10 = (bf16[128,256]{1,0:T(8,128)(2,1)S(1)}, bf16[128,256]{1,0:T(8,128)(2,1)S(1)}, u32[]{:S(2)}, u32[]{:S(2)}) collective-permute-start(bf16[128,256]{1,0:T(8,128)(2,1)S(1)} %assemble.1), channel_id=1, source_target_pairs={{0,16},{1,65},{2,18},{3,67},{4,20},{5,69},{6,22},{7,71},{8,24},{9,... | collective-permute-start | bytes 196616 | tf_op jit(solution)/shard_map/ppermute | solution.py:49
  42.4 4.6 %collective-permute-start.11 = (bf16[128,256]{1,0:T(8,128)(2,1)S(1)}, bf16[128,256]{1,0:T(8,128)(2,1)S(1)}, u32[]{:S(2)}, u32[]{:S(2)}) collective-permute-start(bf16[128,256]{1,0:T(8,128)(2,1)S(1)} %assemble.1), channel_id=1, source_target_pairs={{0,32},{1,129},{2,34},{3,131},{4,36},{5,133},{6,38},{7,135},{8,40}... | collective-permute-start | bytes 196616 | tf_op jit(solution)/shard_map/ppermute | solution.py:49
  44.4 3.4 %collective-permute-start.12 = (bf16[128,256]{1,0:T(8,128)(2,1)S(1)}, bf16[128,256]{1,0:T(8,128)(2,1)S(1)}, u32[]{:S(2)}, u32[]{:S(2)}) collective-permute-start(bf16[128,256]{1,0:T(8,128)(2,1)S(1)} %assemble.1), channel_id=1, source_target_pairs={{0,48},{1,193},{2,50},{3,195},{4,52},{5,197},{6,54},{7,199},{8,56}... | collective-permute-start | bytes 196616 | tf_op jit(solution)/shard_map/ppermute | solution.py:49
  47.9 7.2 %collective-permute-start.14 = (bf16[4,128,256]{2,1,0:T(8,128)(2,1)S(1)}, bf16[4,128,256]{2,1,0:T(8,128)(2,1)S(1)}, u32[]{:S(2)}, u32[]{:S(2)}) collective-permute-start(bf16[4,128,256]{2,1,0:T(8,128)(2,1)S(1)} %pad_maximum_fusion.refs_0_), channel_id=1, source_target_pairs={{0,64},{1,17},{2,66},{3,19},{4,68},{5,21},{6,70},{7,23},{8,72},{9,... | collective-permute-start | bytes 786440 | tf_op jit(solution)/shard_map/ppermute | solution.py:49
  49.3 8.7 %collective-permute-start.15 = (bf16[4,128,256]{2,1,0:T(8,128)(2,1)S(1)}, bf16[4,128,256]{2,1,0:T(8,128)(2,1)S(1)}, u32[]{:S(2)}, u32[]{:S(2)}) collective-permute-start(bf16[4,128,256]{2,1,0:T(8,128)(2,1)S(1)} %pad_maximum_fusion.refs_0_), channel_id=1, source_target_pairs={{0,128},{1,33},{2,130},{3,35},{4,132},{5,37},{6,134},{7,39},{8,136... | collective-permute-start | bytes 786440 | tf_op jit(solution)/shard_map/ppermute | solution.py:49
  51.4 11.0 %collective-permute-start.16 = (bf16[4,128,256]{2,1,0:T(8,128)(2,1)S(1)}, bf16[4,128,256]{2,1,0:T(8,128)(2,1)S(1)}, u32[]{:S(2)}, u32[]{:S(2)}) collective-permute-start(bf16[4,128,256]{2,1,0:T(8,128)(2,1)S(1)} %pad_maximum_fusion.refs_0_), channel_id=1, source_target_pairs={{0,192},{1,49},{2,194},{3,51},{4,196},{5,53},{6,198},{7,55},{8,200... | collective-permute-start | bytes 786440 | tf_op jit(solution)/shard_map/ppermute | solution.py:49
  52.4 10.1 %collective-permute-start.20 = (bf16[2,32,1536]{2,1,0:T(8,128)(2,1)S(1)}, bf16[2,32,1536]{2,1,0:T(8,128)(2,1)S(1)}, u32[]{:S(2)}, u32[]{:S(2)}) collective-permute-start(bf16[2,32,1536]{2,1,0:T(8,128)(2,1)S(1)} %get-tuple-element.46.own), channel_id=1, source_target_pairs={{0,2},{1,3},{2,4},{3,5},{4,6},{5,7},{6,8},{7,9},{8,10},{9,11},{10,... | collective-permute-start | bytes 589832 | tf_op jit(solution)/shard_map/ppermute | solution.py:54
  52.4 12.9 %collective-permute-start.21 = (bf16[2,32,1536]{2,1,0:T(8,128)(2,1)S(1)}, bf16[2,32,1536]{2,1,0:T(8,128)(2,1)S(1)}, u32[]{:S(2)}, u32[]{:S(2)}) collective-permute-start(bf16[2,32,1536]{2,1,0:T(8,128)(2,1)S(1)} %get-tuple-element.46.own), channel_id=1, source_target_pairs={{0,14},{1,15},{2,0},{3,1},{4,2},{5,3},{6,4},{7,5},{8,6},{9,7},{10,... | collective-permute-start | bytes 589832 | tf_op jit(solution)/shard_map/ppermute | solution.py:54
  55.1 13.8 %collective-permute-start.22 = (bf16[2,32,1536]{2,1,0:T(8,128)(2,1)S(1)}, bf16[2,32,1536]{2,1,0:T(8,128)(2,1)S(1)}, u32[]{:S(2)}, u32[]{:S(2)}) collective-permute-start(bf16[2,32,1536]{2,1,0:T(8,128)(2,1)S(1)} %get-tuple-element.46.own), channel_id=1, source_target_pairs={{0,4},{1,5},{2,6},{3,7},{4,8},{5,9},{6,10},{7,11},{8,12},{9,13},{1... | collective-permute-start | bytes 589832 | tf_op jit(solution)/shard_map/ppermute | solution.py:54
  58.0 13.5 %collective-permute-start.13 = (bf16[4,128,256]{2,1,0:T(8,128)(2,1)S(1)}, bf16[4,128,256]{2,1,0:T(8,128)(2,1)S(1)}, u32[]{:S(2)}, u32[]{:S(2)}) collective-permute-start(bf16[4,128,256]{2,1,0:T(8,128)(2,1)S(1)} %pad_maximum_fusion.refs_0_), channel_id=1, source_target_pairs={{0,1},{1,0},{2,3},{3,2},{4,5},{5,4},{6,7},{7,6},{8,9},{9,8},{10,11... | collective-permute-start | bytes 786440 | tf_op jit(solution)/shard_map/ppermute | solution.py:58
  62.4 9.1 %collective-permute-start.17 = (bf16[4,128,256]{2,1,0:T(8,128)(2,1)S(1)}, bf16[4,128,256]{2,1,0:T(8,128)(2,1)S(1)}, u32[]{:S(2)}, u32[]{:S(2)}) collective-permute-start(bf16[4,128,256]{2,1,0:T(8,128)(2,1)S(1)} %collective-permute-done.14.refs_0_), channel_id=1, source_target_pairs={{0,1},{1,0},{2,3},{3,2},{4,5},{5,4},{6,7},{7,6},{8,9},{9,8},{10,11... | collective-permute-start | bytes 786440 | tf_op jit(solution)/shard_map/ppermute | solution.py:58
  62.5 9.0 %collective-permute-start.18 = (bf16[4,128,256]{2,1,0:T(8,128)(2,1)S(1)}, bf16[4,128,256]{2,1,0:T(8,128)(2,1)S(1)}, u32[]{:S(2)}, u32[]{:S(2)}) collective-permute-start(bf16[4,128,256]{2,1,0:T(8,128)(2,1)S(1)} %collective-permute-done.15.refs_1_), channel_id=1, source_target_pairs={{0,1},{1,0},{2,3},{3,2},{4,5},{5,4},{6,7},{7,6},{8,9},{9,8},{10,11... | collective-permute-start | bytes 786440 | tf_op jit(solution)/shard_map/ppermute | solution.py:58
  65.3 6.2 %collective-permute-start.19 = (bf16[4,128,256]{2,1,0:T(8,128)(2,1)S(1)}, bf16[4,128,256]{2,1,0:T(8,128)(2,1)S(1)}, u32[]{:S(2)}, u32[]{:S(2)}) collective-permute-start(bf16[4,128,256]{2,1,0:T(8,128)(2,1)S(1)} %collective-permute-done.16.refs_2_), channel_id=1, source_target_pairs={{0,1},{1,0},{2,3},{3,2},{4,5},{5,4},{6,7},{7,6},{8,9},{9,8},{10,11... | collective-permute-start | bytes 786440 | tf_op jit(solution)/shard_map/ppermute | solution.py:58
  69.3 1.5 %collective-permute-start.23 = (f32[2,96,128]{2,1,0:T(8,128)S(1)}, f32[2,96,128]{2,1,0:T(8,128)S(1)}, u32[]{:S(2)}, u32[]{:S(2)}) collective-permute-start(f32[2,96,128]{2,1,0:T(8,128)S(1)} %project.1), channel_id=1, source_target_pairs={{0,1},{1,0},{2,3},{3,2},{4,5},{5,4},{6,7},{7,6},{8,9},{9,8},{10,11... | collective-permute-start | bytes 294920 | tf_op jit(solution)/shard_map/ppermute | solution.py:58

commit v3 on v2

v3 whole, which is shorter than its diff:
```python
import jax
import jax.numpy as jnp
from jax import lax
from jax.experimental import pallas as pl
from jax.experimental.pallas import tpu as pltpu
from jax.sharding import PartitionSpec as P

CAP = 3
SIDE = 4
DEPTH = 8
MOVED = 32
SLICES = 4
ORDER = (1, 3, 2)
MIB = 2**20
AXES = ("blk", "exc", "row")
NT = (((1,), (1,)), ((), ()))
SMEM = pl.BlockSpec(memory_space=pltpu.SMEM)
VMEM = pl.BlockSpec(memory_space=pltpu.VMEM)
HBM = pl.BlockSpec(memory_space=pltpu.HBM)


def device_id(y, x, z, core):
    return ((y * SIDE + x) * DEPTH + z) * 2 + core


def plane_perm(shift, first):
    pairs = []
    for y in range(SIDE):
        for x in range(SIDE):
            for z in range(DEPTH):
                for core in range(2):
                    along_x = (core == 0) == first
                    y_to = y if along_x else (y + shift) % SIDE
                    x_to = (x + shift) % SIDE if along_x else x
                    pairs.append((device_id(y, x, z, core), device_id(y_to, x_to, z, core)))
    return pairs


def depth_perm(shift):
    pairs = []
    for y in range(SIDE):
        for x in range(SIDE):
            for z in range(DEPTH):
                for core in range(2):
                    step = -shift if core and shift == 2 else shift
                    pairs.append((device_id(y, x, z, core), device_id(y, x, (z + step) % DEPTH, core)))
    return pairs


def plane_send(value, first):
    sent = {s: lax.ppermute(value, AXES, plane_perm(s, first)) for s in ORDER}
    return [sent[s] for s in range(1, SIDE)]


def depth_send(value, shift):
    return lax.ppermute(value, AXES, depth_perm(shift))


def core_swap(value):
    return lax.ppermute(value, "row", [(0, 1), (1, 0)])


def limit(mib):
    return pltpu.CompilerParams(vmem_limit_bytes=mib * MIB)


def pick_kernel(moved_hbm, panels, out, moved, buf, sem):
    index_copy = pltpu.make_async_copy(moved_hbm, moved, sem.at[CAP])
    index_copy.start()
    me = lax.axis_index("blk")
    part = lax.axis_index("exc") & (SLICES - 1)
    slots = [jnp.int32(0)] * CAP
    count = jnp.int32(0)
    index_copy.wait()
    for i in range(MOVED):
        block = moved[i]
        mine = (block >> 3) == me
        slots = [jnp.where(mine & (count == s), block & 7, slots[s]) for s in range(CAP)]
        count = count + mine.astype(jnp.int32)
    copies = []
    for s in range(CAP):
        copy = pltpu.make_async_copy(panels.at[slots[s]], buf.at[s], sem.at[s])
        copy.start()
        copies.append(copy)
    width = buf.shape[2]
    share = out.shape[1]
    rows = lax.broadcasted_iota(jnp.int32, (share, width), 0)
    cols = lax.broadcasted_iota(jnp.int32, (share, width), 1)
    chosen = jnp.where(cols == rows + part * share, 1.0, 0.0).astype(jnp.bfloat16)
    for s in range(CAP):
        copies[s].wait()
        out[s] = lax.dot_general(chosen, buf[s], NT, preferred_element_type=jnp.float32).astype(jnp.bfloat16)


def in_hbm(value):
    return pltpu.with_memory_space_constraint(value, pltpu.HBM)


def pick(moved_blocks, panels):
    blocks, rows, width = panels.shape
    return pl.pallas_call(
        pick_kernel,
        out_shape=jax.ShapeDtypeStruct((CAP, width // SLICES, rows), jnp.bfloat16),
        in_specs=[HBM] * 2,
        out_specs=VMEM,
        scratch_shapes=[
            pltpu.SMEM((MOVED,), jnp.int32),
            pltpu.VMEM((CAP, rows, width), jnp.bfloat16),
            pltpu.SemaphoreType.DMA((CAP + 1,)),
        ],
        compiler_params=limit(6),
        name="pick",
    )(in_hbm(moved_blocks), in_hbm(panels))


def stage_kernel(after, moved_hbm, *refs):
    n = (len(refs) - 5) // 2
    table = refs[n]
    moved, count, rank, sem = refs[-4:]
    copies = [pltpu.make_async_copy(refs[k], refs[n + 1 + k], sem.at[k]) for k in range(n)]
    index_copy = pltpu.make_async_copy(moved_hbm, moved, sem.at[n])
    index_copy.start()
    for copy in copies:
        copy.start()
    me = lax.axis_index("blk")
    core = lax.axis_index("row")
    y, x = me >> 2, me & 3
    on_x = core == 0
    here = jnp.where(on_x, x, y)
    across = jnp.where(on_x, y, x)
    for g in range(SIDE * SIDE):
        count[g] = 0
    index_copy.wait()
    for i in range(MOVED):
        owner = moved[i] >> 3
        seen = count[owner]
        rank[i] = seen
        count[owner] = seen + 1
    for t in range(SIDE):
        target = (across + t) & 3
        block = jnp.where(on_x, target * SIDE + here, here * SIDE + target)
        for s in range(2):
            index = 2 * block + s
            owner = moved[index] >> 3
            owner_y, owner_x = owner >> 2, owner & 3
            found = jnp.where(on_x, owner_y, owner_x) == across
            source = (here - jnp.where(on_x, owner_x, owner_y)) & 3
            table[2 * t + s] = jnp.where(found, source * 4 + rank[index], -1)
    for copy in copies:
        copy.wait()


def stage(after, moved_blocks, values):
    n = len(values)
    table, *staged = pl.pallas_call(
        stage_kernel,
        out_shape=[jax.ShapeDtypeStruct((2 * SIDE,), jnp.int32)]
        + [jax.ShapeDtypeStruct(value.shape, value.dtype) for value in values],
        in_specs=[pl.BlockSpec(memory_space=pl.ANY)] + [HBM] * (1 + n),
        out_specs=[SMEM] + [VMEM] * n,
        scratch_shapes=[
            pltpu.SMEM((MOVED,), jnp.int32),
            pltpu.SMEM((SIDE * SIDE,), jnp.int32),
            pltpu.SMEM((MOVED,), jnp.int32),
            pltpu.SemaphoreType.DMA((n + 1,)),
        ],
        compiler_params=limit(6),
        name="stage",
    )(after, *[in_hbm(value) for value in (moved_blocks, *values)])
    return table, staged


def route_kernel(table, a0, a1, a2, a3, o0, o1, o2, o3):
    arrivals = (a0, a1, a2, a3)
    for t, out in enumerate((o0, o1, o2, o3)):
        for s in range(2):
            entry = table[2 * t + s]
            slot = jnp.maximum(entry, 0) & 3
            value = jnp.zeros(out.shape[1:], out.dtype)
            for k in range(SIDE):
                value = jnp.where((entry >> 2) == k, arrivals[k][slot], value)
            out[s] = value


def route(table, arrivals):
    _, share, rows = arrivals[0].shape
    return pl.pallas_call(
        route_kernel,
        out_shape=[jax.ShapeDtypeStruct((2, share, rows), jnp.bfloat16)] * SIDE,
        in_specs=[SMEM] + [VMEM] * SIDE,
        out_specs=[VMEM] * SIDE,
        compiler_params=limit(6),
        name="route",
    )(table, *arrivals)


def radiate_kernel(a0, a1, a2, a3, geometry, columns, keep, give):
    core = lax.axis_index("row")
    partial = []
    for s in range(2):
        panel = (a0[s] + a1[s]) + (a2[s] + a3[s])
        columns[s] = panel
        partial.append(jnp.dot(panel, geometry[s], preferred_element_type=jnp.float32))
    keep[...] = jnp.where(core == 0, partial[0], partial[1])
    give[...] = jnp.where(core == 0, partial[1], partial[0])


def radiate(arrivals, geometry):
    _, share, rows = arrivals[0].shape
    half = jax.ShapeDtypeStruct((share, geometry.shape[2]), jnp.float32)
    return pl.pallas_call(
        radiate_kernel,
        out_shape=[jax.ShapeDtypeStruct((2, share, rows), jnp.bfloat16), half, half],
        in_specs=[VMEM] * 5,
        out_specs=[VMEM] * 3,
        compiler_params=limit(8),
        name="radiate",
    )(*arrivals, geometry)


def first_row(shift, share):
    part = (lax.axis_index("exc") - shift) & (SLICES - 1)
    return pl.multiple_of(part * share, share)


def assemble_kernel(own, up, down, far, out):
    share = own.shape[0]
    for shift, value in ((0, own), (1, up), (-1, down), (2, far)):
        out[pl.ds(first_row(shift, share), share), :] = value[...]


def assemble(pieces):
    share, width = pieces[0].shape
    return pl.pallas_call(
        assemble_kernel,
        out_shape=jax.ShapeDtypeStruct((SLICES * share, width), jnp.bfloat16),
        in_specs=[VMEM] * 4,
        out_specs=VMEM,
        compiler_params=limit(4),
        name="assemble",
    )(*pieces)


def weigh_kernel(partners, trans, patt, after, out):
    columns = trans.shape[1]
    rows = patt.shape[1]

    def body(i, carry):
        for j in range(columns):
            pattern = patt[partners[j, i] & 7].astype(jnp.float32)
            out[i, j * rows : (j + 1) * rows, :] = (pattern * trans[i, j : j + 1, :]).astype(jnp.bfloat16)
        return carry

    lax.fori_loop(0, trans.shape[0], body, 0)


def weigh(partners, translation, patterns, after):
    moved, columns, width = translation.shape
    return pl.pallas_call(
        weigh_kernel,
        out_shape=pltpu.VMEM((moved, columns * patterns.shape[1], width), jnp.bfloat16),
        in_specs=[SMEM, VMEM, VMEM, pl.BlockSpec(memory_space=pl.ANY)],
        out_specs=VMEM,
        compiler_params=limit(4),
        name="weigh",
    )(partners, translation, patterns, after)


def couple(pieces, weighted, columns, so_far=None, addends=None):
    n = len(pieces)
    moved, tall, width = weighted.shape
    rows = tall // columns
    basis = pieces[0][2].shape[1]
    together = 4

    def kernel(weights, *refs):
        piece_refs = refs[:n]
        copies = []
        if addends is None:
            out, buf, sem = refs[-3:]
        else:
            left, right = refs[n : n + 2]
            out, total_out, buf, sem, total, total_sem = refs[-6:]
            total[...] = left[...] + right[...]
            copies.append(pltpu.make_async_copy(total, total_out, total_sem))
            copies[0].start()
        me = lax.axis_index("blk")
        core = lax.axis_index("row")
        y, x = me >> 2, me & 3
        for p, (leg, own, _) in enumerate(pieces):
            holder = core if own else 1 - core
            near = jnp.where(holder == 0, x, y)
            across = (jnp.where(holder == 0, y, x) - leg) & 3
            ids = []
            for k in range(SIDE):
                first = (near - k) & 3
                block = jnp.where(holder == 0, across * SIDE + first, first * SIDE + across)
                ids.append(2 * block + holder)
            halves = 2 if p == n - 1 else 1
            for part in range(halves):
                some = range(part * SIDE // halves, (part + 1) * SIDE // halves)
                rads = {k: piece_refs[p][k].T for k in some}
                for first in range(0, columns, together):
                    for k in some:
                        some_rows = weights[ids[k], first * rows : (first + together) * rows, :]
                        block = jnp.dot(some_rows, rads[k], preferred_element_type=jnp.float32)
                        buf[p, k, first : first + together] = block.astype(jnp.bfloat16).reshape(together, rows, basis)
                for k in some:
                    copy = pltpu.make_async_copy(buf.at[p, k], out.at[ids[k]], sem.at[p, k])
                    copy.start()
                    copies.append(copy)
        for copy in copies:
            copy.wait()

    operands = [weighted, *[piece[2] for piece in pieces], *(addends or ())]
    in_specs = [VMEM] * len(operands)
    aliases = {}
    if so_far is not None:
        in_specs.append(pl.BlockSpec(memory_space=pl.ANY))
        aliases = {len(operands): 0}
        operands.append(so_far)
    shapes = [jax.ShapeDtypeStruct((moved, columns, rows, basis), jnp.bfloat16)]
    scratch = [pltpu.VMEM((n, SIDE, columns, rows, basis), jnp.bfloat16), pltpu.SemaphoreType.DMA((n, SIDE))]
    if addends is not None:
        shapes.append(jax.ShapeDtypeStruct(addends[0].shape, addends[0].dtype))
        scratch += [pltpu.VMEM(addends[0].shape, addends[0].dtype), pltpu.SemaphoreType.DMA]
    results = pl.pallas_call(
        kernel,
        out_shape=shapes,
        in_specs=in_specs,
        out_specs=[pl.BlockSpec(memory_space=pl.ANY)] * len(shapes),
        scratch_shapes=scratch,
        input_output_aliases=aliases,
        compiler_params=limit(8),
        cost_estimate=pl.CostEstimate(
            flops=2 * n * SIDE * tall * width * basis,
            bytes_accessed=n * SIDE * tall * basis * 2,
            transcendentals=0,
        ),
        name="couple",
    )(*operands)
    return results[0] if addends is None else results


def hold_kernel(value, after, out):
    pass


def hold(value, after):
    return pl.pallas_call(
        hold_kernel,
        out_shape=jax.ShapeDtypeStruct(value.shape, value.dtype),
        in_specs=[pl.BlockSpec(memory_space=pl.ANY)] * 2,
        out_specs=pl.BlockSpec(memory_space=pl.ANY),
        input_output_aliases={0: 0},
        compiler_params=limit(1),
        name="hold",
    )(value, after)


def project_kernel(excitations, own, up, down, far, out, panel):
    share = own.shape[1]
    for shift, value in ((0, own), (1, up), (-1, down), (2, far)):
        panel[:, pl.ds(first_row(shift, share), share), :] = value[...]
    for s in range(2):
        out[s] = lax.dot_general(excitations[s], panel[s], NT, preferred_element_type=jnp.float32)


def project(excitations, pieces):
    moved, count, rows = excitations.shape
    basis = SLICES * pieces[0].shape[1]
    return pl.pallas_call(
        project_kernel,
        out_shape=jax.ShapeDtypeStruct((moved, count, basis), jnp.float32),
        in_specs=[VMEM] * 5,
        out_specs=VMEM,
        scratch_shapes=[pltpu.VMEM((2, basis, rows), jnp.bfloat16)],
        compiler_params=limit(6),
        name="project",
    )(excitations, *pieces)


def on_device(panels, patterns, geometry, excitations, moved_blocks, partners, translation):
    outgoing = pick(moved_blocks, panels)
    arrivals = plane_send(outgoing, True)
    table, (geometry, translation, patterns, excitations, partners) = stage(
        outgoing, moved_blocks, [geometry, translation, patterns, excitations, partners.T]
    )
    table, *arrivals = lax.optimization_barrier((table, *arrivals))
    routed = route(table, [outgoing, *arrivals])
    landed = [lax.ppermute(routed[s], AXES, plane_perm(s, False)) for s in range(1, SIDE)]
    weighted = weigh(partners, translation, patterns, routed[0])
    weighted, *landed = lax.optimization_barrier((weighted, *landed))
    columns, keep, give = radiate([routed[0], *landed], geometry)
    radiation = (keep + core_swap(give)).astype(jnp.bfloat16)
    mine = assemble([radiation, *[depth_send(radiation, s) for s in (1, -1, 2)]])

    seen = plane_send(mine, True)
    columns = hold(columns, mine)
    columns_far = depth_send(columns, 2)
    stack = jnp.stack([mine, *seen])
    arrived = plane_send(stack, False)
    columns_up, columns_down = depth_send(columns, 1), depth_send(columns, -1)
    columns_far, stack = lax.optimization_barrier((columns_far, stack))
    depth = weighted, translation.shape[1]
    couplings = couple([(0, True, stack)], *depth)
    couplings, stack, columns_up, columns_down, *arrived = lax.optimization_barrier(
        (couplings, stack, columns_up, columns_down, *arrived)
    )
    other = [(leg, False, core_swap(value)) for leg, value in enumerate([stack, *arrived])]
    projected = project(excitations, [columns, columns_up, columns_down, columns_far])
    came = core_swap(projected)
    couplings = couple([(leg, True, arrived[leg - 1]) for leg in range(1, SIDE)], *depth, couplings)
    couplings, projected = couple(other, *depth, couplings, (projected, came))
    return (couplings, projected)


def solution(mesh):
    placed = (
        P("blk", "row", None),
        P("blk", "row", None),
        P("blk", "row", None),
        P("blk", "exc", "row"),
        P(),
        P(None, ("blk", "exc")),
        P(None, ("blk", "exc"), None),
    )
    return jax.shard_map(
        on_device,
        mesh=mesh,
        in_specs=placed,
        out_specs=(P(None, ("blk", "exc"), "row", None), P("blk", "exc", None)),
        check_vma=False,
    )
```

time: 75.9 us -> 71 us (0.935)
  starting transfers between devices: 38.8 us -> 29.7 us
  Pallas kernels: 14.9 us -> 17.6 us
  waiting for transfers between devices: 19.9 us -> 22.5 us
    ppermute x9, starting transfers between devices: 15.1 us -> 9.74 us  [plane_send(): sent = {s: lax.ppermute(value, AXES, plane_perm(s, first)) for s in ORDER}]
    ppermute x6, starting transfers between devices: 12 us -> 7.33 us  [core_swap(): return lax.ppermute(value, 'row', [(0, 1), (1, 0)])]
    ppermute x3, waiting for transfers between devices: 4.19 us -> 0.4 us  [on_device(): lax.ppermute(routed[s], AXES, plane_perm(s, False))]
    ppermute x9, waiting for transfers between devices: 9.14 us -> 12.9 us  [plane_send(): sent = {s: lax.ppermute(value, AXES, plane_perm(s, first)) for s in ORDER}]
    ppermute x6, waiting for transfers between devices: 4.77 us -> 8.4 us  [depth_send(): return lax.ppermute(value, AXES, depth_perm(shift))]
    pallas_call x4 -> x7, Pallas kernels: 13.3 us -> 16.1 us  [the longest x3 7.52 us: couple(): pl.pallas_call(kernel, out_shape=shapes, in_specs=in_specs, out_specs=[pl...]
    ppermute x6, waiting for transfers between devices: 1.81 us -> 0.87 us  [core_swap(): return lax.ppermute(value, 'row', [(0, 1), (1, 0)])]
    ppermute x6, starting transfers between devices: 7.09 us -> 8.03 us  [depth_send(): return lax.ppermute(value, AXES, depth_perm(shift))]
  transfers between devices with their start and end apart: 24 -> 24, of which waited for: 12 -> 14; matrix products, arithmetic and copies ran while one was open for 1% -> 0% of each run, Pallas kernels for 8% -> 15%
where the time goes in v3:
time: 71 us; the launch traced here: 70.8 us
  starting transfers between devices  29.7 us (42%)
  waiting for transfers between devices  22.5 us (32%)
  Pallas kernels  17.6 us (25%)
  between operations  0.91 us (1%)
    ppermute x9, waiting for transfers between devices, plane_send(): sent = {s: lax.ppermute(value, AXES, plane_perm(s, first)) for s in ORDER}  12.9 us
    ppermute x9, starting transfers between devices, plane_send(): sent = {s: lax.ppermute(value, AXES, plane_perm(s, first)) for s in ORDER}  9.74 us
    ppermute x6, waiting for transfers between devices, depth_send(): return lax.ppermute(value, AXES, depth_perm(shift))  8.4 us
    ppermute x6, starting transfers between devices, depth_send(): return lax.ppermute(value, AXES, depth_perm(shift))  8.03 us
    pallas_call x3, Pallas kernels, couple(): pl.pallas_call(kernel, out_shape=shapes, in_specs=in_specs, out_specs=[pl...  7.52 us
    ppermute x6, starting transfers between devices, core_swap(): return lax.ppermute(value, 'row', [(0, 1), (1, 0)])  7.33 us
    ppermute x3, starting transfers between devices, on_device(): lax.ppermute(routed[s], AXES, plane_perm(s, False))  4.6 us
    pallas_call x1, Pallas kernels, weigh(): pl.pallas_call(weigh_kernel, out_shape=pltpu.VMEM((moved, columns * patte...  3.6 us
  transfers between devices with their start and end apart: 24, of which 14 were waited for; matrix products, arithmetic and copies ran while one was open for 0% of the time, Pallas kernels for 15%

profile of v3, /device:TPU:1, one launch (start us, length us, event | category | flops | bytes accessed | tf_op | source)
XLA Modules:
  0.0 70.8 jit_solution(4601237078269401440)
XLA Ops:
  0.6 2.6 %pick.1.after.a0 = bf16[3,32,1536]{2,1,0:T(8,128)(2,1)S(1)} custom-call(s32[32]{0:T(128)} %moved_hbm.3, bf16[8,1536,128]{2,1,0:T(8,128)(2,1)} %panels.1), custom_call_target="tpu_custom_call" | custom-call | tf_op jit(solution)/shard_map/pick/pallas_call | solution.py:101
  3.2 3.6 %collective-permute-start.2 = (bf16[3,32,1536]{2,1,0:T(8,128)(2,1)S(1)}, bf16[3,32,1536]{2,1,0:T(8,128)(2,1)S(1)}, u32[]{:S(2)}, u32[]{:S(2)}) collective-permute-start(bf16[3,32,1536]{2,1,0:T(8,128)(2,1)S(1)} %pick.1.after.a0), channel_id=1, source_target_pairs={{0,48},{1,193},{2,50},{3,195},{4,52},{5,197},{6,54},{7,199},{8,56}... | collective-permute-start | bytes 884744 | tf_op jit(solution)/shard_map/ppermute | solution.py:51
  6.8 0.3 collective-permute-start.1
  7.2 0.7 collective-permute-start
  7.9 2.4 %stage.1 = (s32[8]{0:T(128)S(1)}, bf16[2,1536,256]{2,1,0:T(8,128)(2,1)S(1)}, f32[32,16,256]{2,1,0:T(8,128)S(1)}, bf16[8,64,256]{2,1,0:T(8,128)(2,1)S(1)}, bf16[2...) custom-call(bf16[3,32,1536]{2,1,0:T(8,128)(2,1)S(1)} %pick.1.after.a0, s32[32]{0:T(128)} %moved_hbm.3, ...), custom_call_target="tpu_custom_call" | custom-call | tf_op jit(solution)/shard_map/stage/pallas_call | solution.py:155
  10.3 3.4 %collective-permute-done.2.a3 = bf16[3,32,1536]{2,1,0:T(8,128)(2,1)S(1)} collective-permute-done((bf16[3,32,1536]{2,1,0:T(8,128)(2,1)S(1)}, bf16[3,32,1536]{2,1,0:T(8,128)(2,1)S(1)}, u32[]{:S(2)}, u32[]{:S(2)}) %collective-permute-start.2) | collective-permute-done | bytes 294944 | tf_op jit(solution)/shard_map/ppermute | solution.py:51
  13.7 0.6 collective-permute-done.1.a2
  14.3 3.1 %collective-permute-done.a1 = bf16[3,32,1536]{2,1,0:T(8,128)(2,1)S(1)} collective-permute-done((bf16[3,32,1536]{2,1,0:T(8,128)(2,1)S(1)}, bf16[3,32,1536]{2,1,0:T(8,128)(2,1)S(1)}, u32[]{:S(2)}, u32[]{:S(2)}) %collective-permute-start) | collective-permute-done | bytes 294944 | tf_op jit(solution)/shard_map/ppermute | solution.py:51
  17.4 0.7 %route.1 = (bf16[2,32,1536]{2,1,0:T(8,128)(2,1)S(1)}, bf16[2,32,1536]{2,1,0:T(8,128)(2,1)S(1)}, bf16[2,32,1536]{2,1,0:T(8,128)(2,1)S(1)}, bf16[2,32,1536]{2,1,0:T(8,128)(2,1)S(1)}) custom-call(s32[8]{0:T(128)S(1)} %get-tuple-element.36.table, bf16[3,32,1536]{2,1,0:T(8,128)(2,1)S(1)} %pick.1.after.a0, bf16[3,32,1536]{2,1,0:T(8,128)(2,1)S(1)} %collective-permute-done.a1, ...), custom_call_target="tpu_custom_call" | custom-call | tf_op jit(solution)/shard_map/route/pallas_call | solution.py:187
  18.1 1.0 %collective-permute-start.3 = (bf16[2,32,1536]{2,1,0:T(8,128)(2,1)S(1)}, bf16[2,32,1536]{2,1,0:T(8,128)(2,1)S(1)}, u32[]{:S(2)}, u32[]{:S(2)}) collective-permute-start(bf16[2,32,1536]{2,1,0:T(8,128)(2,1)S(1)} %get-tuple-element.41), channel_id=1, source_target_pairs={{0,64},{1,17},{2,66},{3,19},{4,68},{5,21},{6,70},{7,23},{8,72},{9,... | collective-permute-start | bytes 589832 | tf_op jit(solution)/shard_map/ppermute | solution.py:391
  19.1 2.5 %collective-permute-start.4 = (bf16[2,32,1536]{2,1,0:T(8,128)(2,1)S(1)}, bf16[2,32,1536]{2,1,0:T(8,128)(2,1)S(1)}, u32[]{:S(2)}, u32[]{:S(2)}) collective-permute-start(bf16[2,32,1536]{2,1,0:T(8,128)(2,1)S(1)} %get-tuple-element.42), channel_id=1, source_target_pairs={{0,128},{1,33},{2,130},{3,35},{4,132},{5,37},{6,134},{7,39},{8,136... | collective-permute-start | bytes 589832 | tf_op jit(solution)/shard_map/ppermute | solution.py:391
  21.6 1.1 %collective-permute-start.5 = (bf16[2,32,1536]{2,1,0:T(8,128)(2,1)S(1)}, bf16[2,32,1536]{2,1,0:T(8,128)(2,1)S(1)}, u32[]{:S(2)}, u32[]{:S(2)}) collective-permute-start(bf16[2,32,1536]{2,1,0:T(8,128)(2,1)S(1)} %get-tuple-element.43), channel_id=1, source_target_pairs={{0,192},{1,49},{2,194},{3,51},{4,196},{5,53},{6,198},{7,55},{8,200... | collective-permute-start | bytes 589832 | tf_op jit(solution)/shard_map/ppermute | solution.py:391
  22.7 3.6 %weigh.1.weights = bf16[32,1024,256]{2,1,0:T(8,128)(2,1)S(1)} custom-call(s32[16,32]{1,0:T(8,128)S(1)} %get-tuple-element.32.partners, f32[32,16,256]{2,1,0:T(8,128)S(1)} %get-tuple-element.33.trans, bf16[8,64,256]{2,1,0:T(8,128)(2,1)S(1)} %get-tuple-element.34.patt, bf16[2,32,1536]{2,1,0:T(8,128)(2,1)S(1)} %get-tuple-element.40.after.a0), custom_call_target="tpu_custom_call" | custom-call | tf_op jit(solution)/shard_map/weigh/pallas_call | solution.py:259
  26.3 0.0 collective-permute-done.3.a1
  26.3 0.4 collective-permute-done.4.a2
  26.7 0.0 collective-permute-done.5.a3
  26.7 0.4 radiate.1
  27.1 3.3 %collective-permute-start.6 = (f32[32,256]{1,0:T(8,128)S(1)}, f32[32,256]{1,0:T(8,128)S(1)}, u32[]{:S(2)}, u32[]{:S(2)}) collective-permute-start(f32[32,256]{1,0:T(8,128)S(1)} %get-tuple-element.51), channel_id=1, source_target_pairs={{0,1},{1,0},{2,3},{3,2},{4,5},{5,4},{6,7},{7,6},{8,9},{9,8},{10,11... | collective-permute-start | bytes 98312 | tf_op jit(solution)/shard_map/ppermute | solution.py:60
  30.4 0.9 %collective-permute-done.6 = f32[32,256]{1,0:T(8,128)S(1)} collective-permute-done((f32[32,256]{1,0:T(8,128)S(1)}, f32[32,256]{1,0:T(8,128)S(1)}, u32[]{:S(2)}, u32[]{:S(2)}) %collective-permute-start.6) | collective-permute-done | bytes 32800 | tf_op jit(solution)/shard_map/ppermute | solution.py:60
  31.2 6.0 %collective-permute-start.9 = (bf16[32,256]{1,0:T(8,128)(2,1)S(1)}, bf16[32,256]{1,0:T(8,128)(2,1)S(1)}, u32[]{:S(2)}, u32[]{:S(2)}) collective-permute-start(bf16[32,256]{1,0:T(8,128)(2,1)S(1)} %add_convert_fusion.own), channel_id=1, source_target_pairs={{0,4},{1,13},{2,6},{3,15},{4,8},{5,1},{6,10},{7,3},{8,12},{9,5},{1... | collective-permute-start | bytes 49160 | tf_op jit(solution)/shard_map/ppermute | solution.py:56
  37.2 0.7 %collective-permute-start.8 = (bf16[32,256]{1,0:T(8,128)(2,1)S(1)}, bf16[32,256]{1,0:T(8,128)(2,1)S(1)}, u32[]{:S(2)}, u32[]{:S(2)}) collective-permute-start(bf16[32,256]{1,0:T(8,128)(2,1)S(1)} %add_convert_fusion.own), channel_id=1, source_target_pairs={{0,14},{1,15},{2,0},{3,1},{4,2},{5,3},{6,4},{7,5},{8,6},{9,7},{10,... | collective-permute-start | bytes 49160 | tf_op jit(solution)/shard_map/ppermute | solution.py:56
  38.0 0.7 %collective-permute-start.7 = (bf16[32,256]{1,0:T(8,128)(2,1)S(1)}, bf16[32,256]{1,0:T(8,128)(2,1)S(1)}, u32[]{:S(2)}, u32[]{:S(2)}) collective-permute-start(bf16[32,256]{1,0:T(8,128)(2,1)S(1)} %add_convert_fusion.own), channel_id=1, source_target_pairs={{0,2},{1,3},{2,4},{3,5},{4,6},{5,7},{6,8},{7,9},{8,10},{9,11},{10,... | collective-permute-start | bytes 49160 | tf_op jit(solution)/shard_map/ppermute | solution.py:56
  38.7 0.0 collective-permute-done.9.far
  38.7 1.1 %collective-permute-done.8.down = bf16[32,256]{1,0:T(8,128)(2,1)S(1)} collective-permute-done((bf16[32,256]{1,0:T(8,128)(2,1)S(1)}, bf16[32,256]{1,0:T(8,128)(2,1)S(1)}, u32[]{:S(2)}, u32[]{:S(2)}) %collective-permute-start.8) | collective-permute-done | bytes 16416 | tf_op jit(solution)/shard_map/ppermute | solution.py:56
  39.8 2.4 %collective-permute-done.7.up = bf16[32,256]{1,0:T(8,128)(2,1)S(1)} collective-permute-done((bf16[32,256]{1,0:T(8,128)(2,1)S(1)}, bf16[32,256]{1,0:T(8,128)(2,1)S(1)}, u32[]{:S(2)}, u32[]{:S(2)}) %collective-permute-start.7) | collective-permute-done | bytes 16416 | tf_op jit(solution)/shard_map/ppermute | solution.py:56
  42.2 2.3 %collective-permute-start.13 = (bf16[128,256]{1,0:T(8,128)(2,1)S(1)}, bf16[128,256]{1,0:T(8,128)(2,1)S(1)}, u32[]{:S(2)}, u32[]{:S(2)}) collective-permute-start(bf16[128,256]{1,0:T(8,128)(2,1)S(1)} %assemble.1.after), channel_id=1, source_target_pairs={{0,48},{1,193},{2,50},{3,195},{4,52},{5,197},{6,54},{7,199},{8,56}... | collective-permute-start | bytes 196616 | tf_op jit(solution)/shard_map/ppermute | solution.py:51
  44.5 1.0 %collective-permute-start.12 = (bf16[128,256]{1,0:T(8,128)(2,1)S(1)}, bf16[128,256]{1,0:T(8,128)(2,1)S(1)}, u32[]{:S(2)}, u32[]{:S(2)}) collective-permute-start(bf16[128,256]{1,0:T(8,128)(2,1)S(1)} %assemble.1.after), channel_id=1, source_target_pairs={{0,32},{1,129},{2,34},{3,131},{4,36},{5,133},{6,38},{7,135},{8,40}... | collective-permute-start | bytes 196616 | tf_op jit(solution)/shard_map/ppermute | solution.py:51
  45.5 0.3 collective-permute-start.11
  45.8 0.0 collective-permute-start.10
  45.8 0.1 collective-permute-done.13
  45.8 3.3 %collective-permute-done.12 = bf16[128,256]{1,0:T(8,128)(2,1)S(1)} collective-permute-done((bf16[128,256]{1,0:T(8,128)(2,1)S(1)}, bf16[128,256]{1,0:T(8,128)(2,1)S(1)}, u32[]{:S(2)}, u32[]{:S(2)}) %collective-permute-start.12) | collective-permute-done | bytes 65568 | tf_op jit(solution)/shard_map/ppermute | solution.py:51
  49.1 0.7 collective-permute-done.11
  49.9 0.4 collective-permute-start.18
  50.3 0.5 collective-permute-start.17
  50.8 0.6 collective-permute-start.16
  51.4 0.0 collective-permute-start.15
  51.4 0.9 %collective-permute-done.10.far = bf16[2,32,1536]{2,1,0:T(8,128)(2,1)S(1)} collective-permute-done((bf16[2,32,1536]{2,1,0:T(8,128)(2,1)S(1)}, bf16[2,32,1536]{2,1,0:T(8,128)(2,1)S(1)}, u32[]{:S(2)}, u32[]{:S(2)}) %collective-permute-start.10) | collective-permute-done | bytes 196640 | tf_op jit(solution)/shard_map/ppermute | solution.py:56
  52.4 0.5 collective-permute-start.14
  52.9 1.5 %couple.3.refs_3_ = bf16[32,16,64,128]{3,2,1,0:T(8,128)(2,1)} custom-call(bf16[32,1024,256]{2,1,0:T(8,128)(2,1)S(1)} %weigh.1.weights, bf16[4,128,256]{2,1,0:T(8,128)(2,1)S(1)} %pad_maximum_fusion.refs_0_), custom_call_target="tpu_custom_call" | custom-call | flops 268435456 | bytes 1048576 | tf_op jit(solution)/shard_map/couple/pallas_call | solution.py:327
  54.4 1.5 %collective-permute-done.15.down = bf16[2,32,1536]{2,1,0:T(8,128)(2,1)S(1)} collective-permute-done((bf16[2,32,1536]{2,1,0:T(8,128)(2,1)S(1)}, bf16[2,32,1536]{2,1,0:T(8,128)(2,1)S(1)}, u32[]{:S(2)}, u32[]{:S(2)}) %collective-permute-start.15) | collective-permute-done | bytes 196640 | tf_op jit(solution)/shard_map/ppermute | solution.py:56
  55.9 2.4 %collective-permute-done.14.up = bf16[2,32,1536]{2,1,0:T(8,128)(2,1)S(1)} collective-permute-done((bf16[2,32,1536]{2,1,0:T(8,128)(2,1)S(1)}, bf16[2,32,1536]{2,1,0:T(8,128)(2,1)S(1)}, u32[]{:S(2)}, u32[]{:S(2)}) %collective-permute-start.14) | collective-permute-done | bytes 196640 | tf_op jit(solution)/shard_map/ppermute | solution.py:56
  58.4 0.0 collective-permute-done.18.refs_2_
  58.4 0.0 collective-permute-done.17.refs_1_
  58.4 1.7 %collective-permute-done.16.refs_0_ = bf16[4,128,256]{2,1,0:T(8,128)(2,1)S(1)} collective-permute-done((bf16[4,128,256]{2,1,0:T(8,128)(2,1)S(1)}, bf16[4,128,256]{2,1,0:T(8,128)(2,1)S(1)}, u32[]{:S(2)}, u32[]{:S(2)}) %collective-permute-start.16) | collective-permute-done | bytes 262176 | tf_op jit(solution)/shard_map/ppermute | solution.py:51
  60.1 3.0 %collective-permute-start.19 = (bf16[4,128,256]{2,1,0:T(8,128)(2,1)S(1)}, bf16[4,128,256]{2,1,0:T(8,128)(2,1)S(1)}, u32[]{:S(2)}, u32[]{:S(2)}) collective-permute-start(bf16[4,128,256]{2,1,0:T(8,128)(2,1)S(1)} %pad_maximum_fusion.refs_0_), channel_id=1, source_target_pairs={{0,1},{1,0},{2,3},{3,2},{4,5},{5,4},{6,7},{7,6},{8,9},{9,8},{10,11... | collective-permute-start | bytes 786440 | tf_op jit(solution)/shard_map/ppermute | solution.py:60
  63.1 0.0 collective-permute-start.20
  63.1 0.5 collective-permute-start.21
  63.6 0.0 collective-permute-start.22
  63.6 0.4 project.1.refs_4_
  64.0 0.6 collective-permute-start.23
  64.6 2.7 %couple.4.refs_6_ = bf16[32,16,64,128]{3,2,1,0:T(8,128)(2,1)} custom-call(bf16[32,1024,256]{2,1,0:T(8,128)(2,1)S(1)} %weigh.1.weights, bf16[4,128,256]{2,1,0:T(8,128)(2,1)S(1)} %collective-permute-done.16.refs_0_, bf16[4,128,256]{2,1,0:T(8,128)(2,1)S(1)} %collective-permute-done.17.refs_1_, ...), custom_call_target="tpu_custom_call", output_to_operand_aliasing={{}: (4, {})} | custom-call | flops 805306368 | bytes 3145728 | tf_op jit(solution)/shard_map/couple/pallas_call | solution.py:327
  67.3 0.0 collective-permute-done.23.refs_5_
  67.3 0.0 collective-permute-done.19.refs_0_
  67.3 0.0 collective-permute-done.20.refs_1_
  67.4 0.0 collective-permute-done.21.refs_2_
  67.4 0.0 collective-permute-done.22.refs_3_
  67.4 3.3 %couple.5 = (bf16[32,16,64,128]{3,2,1,0:T(8,128)(2,1)}, f32[2,96,128]{2,1,0:T(8,128)}) custom-call(bf16[32,1024,256]{2,1,0:T(8,128)(2,1)S(1)} %weigh.1.weights, bf16[4,128,256]{2,1,0:T(8,128)(2,1)S(1)} %collective-permute-done.19.refs_0_, bf16[4,128,256]{2,1,0:T(8,128)(2,1)S(1)} %collective-permute-done.20.refs_1_, ...), custom_call_target="tpu_custom_call", output_to_operand_aliasing={{0}: (7, {})} | custom-call | flops 1073741824 | bytes 4194304 | tf_op jit(solution)/shard_map/couple/pallas_call | solution.py:327
  (4 shorter events, 0.0 us)
Async XLA Ops:
  3.2 10.5 %collective-permute-start.2 = (bf16[3,32,1536]{2,1,0:T(8,128)(2,1)S(1)}, bf16[3,32,1536]{2,1,0:T(8,128)(2,1)S(1)}, u32[]{:S(2)}, u32[]{:S(2)}) collective-permute-start(bf16[3,32,1536]{2,1,0:T(8,128)(2,1)S(1)} %pick.1.after.a0), channel_id=1, source_target_pairs={{0,48},{1,193},{2,50},{3,195},{4,52},{5,197},{6,54},{7,199},{8,56}... | collective-permute-start | bytes 884744 | tf_op jit(solution)/shard_map/ppermute | solution.py:51
  6.8 7.4 %collective-permute-start.1 = (bf16[3,32,1536]{2,1,0:T(8,128)(2,1)S(1)}, bf16[3,32,1536]{2,1,0:T(8,128)(2,1)S(1)}, u32[]{:S(2)}, u32[]{:S(2)}) collective-permute-start(bf16[3,32,1536]{2,1,0:T(8,128)(2,1)S(1)} %pick.1.after.a0), channel_id=1, source_target_pairs={{0,32},{1,129},{2,34},{3,131},{4,36},{5,133},{6,38},{7,135},{8,40}... | collective-permute-start | bytes 884744 | tf_op jit(solution)/shard_map/ppermute | solution.py:51
  7.2 10.2 %collective-permute-start = (bf16[3,32,1536]{2,1,0:T(8,128)(2,1)S(1)}, bf16[3,32,1536]{2,1,0:T(8,128)(2,1)S(1)}, u32[]{:S(2)}, u32[]{:S(2)}) collective-permute-start(bf16[3,32,1536]{2,1,0:T(8,128)(2,1)S(1)} %pick.1.after.a0), channel_id=1, source_target_pairs={{0,16},{1,65},{2,18},{3,67},{4,20},{5,69},{6,22},{7,71},{8,24},{9,... | collective-permute-start | bytes 884744 | tf_op jit(solution)/shard_map/ppermute | solution.py:51
  18.1 8.2 %collective-permute-start.3 = (bf16[2,32,1536]{2,1,0:T(8,128)(2,1)S(1)}, bf16[2,32,1536]{2,1,0:T(8,128)(2,1)S(1)}, u32[]{:S(2)}, u32[]{:S(2)}) collective-permute-start(bf16[2,32,1536]{2,1,0:T(8,128)(2,1)S(1)} %get-tuple-element.41), channel_id=1, source_target_pairs={{0,64},{1,17},{2,66},{3,19},{4,68},{5,21},{6,70},{7,23},{8,72},{9,... | collective-permute-start | bytes 589832 | tf_op jit(solution)/shard_map/ppermute | solution.py:391
  19.1 7.6 %collective-permute-start.4 = (bf16[2,32,1536]{2,1,0:T(8,128)(2,1)S(1)}, bf16[2,32,1536]{2,1,0:T(8,128)(2,1)S(1)}, u32[]{:S(2)}, u32[]{:S(2)}) collective-permute-start(bf16[2,32,1536]{2,1,0:T(8,128)(2,1)S(1)} %get-tuple-element.42), channel_id=1, source_target_pairs={{0,128},{1,33},{2,130},{3,35},{4,132},{5,37},{6,134},{7,39},{8,136... | collective-permute-start | bytes 589832 | tf_op jit(solution)/shard_map/ppermute | solution.py:391
  21.6 5.2 %collective-permute-start.5 = (bf16[2,32,1536]{2,1,0:T(8,128)(2,1)S(1)}, bf16[2,32,1536]{2,1,0:T(8,128)(2,1)S(1)}, u32[]{:S(2)}, u32[]{:S(2)}) collective-permute-start(bf16[2,32,1536]{2,1,0:T(8,128)(2,1)S(1)} %get-tuple-element.43), channel_id=1, source_target_pairs={{0,192},{1,49},{2,194},{3,51},{4,196},{5,53},{6,198},{7,55},{8,200... | collective-permute-start | bytes 589832 | tf_op jit(solution)/shard_map/ppermute | solution.py:391
  27.1 4.1 %collective-permute-start.6 = (f32[32,256]{1,0:T(8,128)S(1)}, f32[32,256]{1,0:T(8,128)S(1)}, u32[]{:S(2)}, u32[]{:S(2)}) collective-permute-start(f32[32,256]{1,0:T(8,128)S(1)} %get-tuple-element.51), channel_id=1, source_target_pairs={{0,1},{1,0},{2,3},{3,2},{4,5},{5,4},{6,7},{7,6},{8,9},{9,8},{10,11... | collective-permute-start | bytes 98312 | tf_op jit(solution)/shard_map/ppermute | solution.py:60
  31.2 7.5 %collective-permute-start.9 = (bf16[32,256]{1,0:T(8,128)(2,1)S(1)}, bf16[32,256]{1,0:T(8,128)(2,1)S(1)}, u32[]{:S(2)}, u32[]{:S(2)}) collective-permute-start(bf16[32,256]{1,0:T(8,128)(2,1)S(1)} %add_convert_fusion.own), channel_id=1, source_target_pairs={{0,4},{1,13},{2,6},{3,15},{4,8},{5,1},{6,10},{7,3},{8,12},{9,5},{1... | collective-permute-start | bytes 49160 | tf_op jit(solution)/shard_map/ppermute | solution.py:56
  37.2 2.6 %collective-permute-start.8 = (bf16[32,256]{1,0:T(8,128)(2,1)S(1)}, bf16[32,256]{1,0:T(8,128)(2,1)S(1)}, u32[]{:S(2)}, u32[]{:S(2)}) collective-permute-start(bf16[32,256]{1,0:T(8,128)(2,1)S(1)} %add_convert_fusion.own), channel_id=1, source_target_pairs={{0,14},{1,15},{2,0},{3,1},{4,2},{5,3},{6,4},{7,5},{8,6},{9,7},{10,... | collective-permute-start | bytes 49160 | tf_op jit(solution)/shard_map/ppermute | solution.py:56
  38.0 4.3 %collective-permute-start.7 = (bf16[32,256]{1,0:T(8,128)(2,1)S(1)}, bf16[32,256]{1,0:T(8,128)(2,1)S(1)}, u32[]{:S(2)}, u32[]{:S(2)}) collective-permute-start(bf16[32,256]{1,0:T(8,128)(2,1)S(1)} %add_convert_fusion.own), channel_id=1, source_target_pairs={{0,2},{1,3},{2,4},{3,5},{4,6},{5,7},{6,8},{7,9},{8,10},{9,11},{10,... | collective-permute-start | bytes 49160 | tf_op jit(solution)/shard_map/ppermute | solution.py:56
  42.2 3.6 %collective-permute-start.13 = (bf16[128,256]{1,0:T(8,128)(2,1)S(1)}, bf16[128,256]{1,0:T(8,128)(2,1)S(1)}, u32[]{:S(2)}, u32[]{:S(2)}) collective-permute-start(bf16[128,256]{1,0:T(8,128)(2,1)S(1)} %assemble.1.after), channel_id=1, source_target_pairs={{0,48},{1,193},{2,50},{3,195},{4,52},{5,197},{6,54},{7,199},{8,56}... | collective-permute-start | bytes 196616 | tf_op jit(solution)/shard_map/ppermute | solution.py:51
  44.5 4.6 %collective-permute-start.12 = (bf16[128,256]{1,0:T(8,128)(2,1)S(1)}, bf16[128,256]{1,0:T(8,128)(2,1)S(1)}, u32[]{:S(2)}, u32[]{:S(2)}) collective-permute-start(bf16[128,256]{1,0:T(8,128)(2,1)S(1)} %assemble.1.after), channel_id=1, source_target_pairs={{0,32},{1,129},{2,34},{3,131},{4,36},{5,133},{6,38},{7,135},{8,40}... | collective-permute-start | bytes 196616 | tf_op jit(solution)/shard_map/ppermute | solution.py:51
  45.5 4.4 %collective-permute-start.11 = (bf16[128,256]{1,0:T(8,128)(2,1)S(1)}, bf16[128,256]{1,0:T(8,128)(2,1)S(1)}, u32[]{:S(2)}, u32[]{:S(2)}) collective-permute-start(bf16[128,256]{1,0:T(8,128)(2,1)S(1)} %assemble.1.after), channel_id=1, source_target_pairs={{0,16},{1,65},{2,18},{3,67},{4,20},{5,69},{6,22},{7,71},{8,24},{9,... | collective-permute-start | bytes 196616 | tf_op jit(solution)/shard_map/ppermute | solution.py:51
  45.8 6.6 %collective-permute-start.10 = (bf16[2,32,1536]{2,1,0:T(8,128)(2,1)S(1)}, bf16[2,32,1536]{2,1,0:T(8,128)(2,1)S(1)}, u32[]{:S(2)}, u32[]{:S(2)}) collective-permute-start(bf16[2,32,1536]{2,1,0:T(8,128)(2,1)S(1)} %hold.1.own), channel_id=1, source_target_pairs={{0,4},{1,13},{2,6},{3,15},{4,8},{5,1},{6,10},{7,3},{8,12},{9,5},{1... | collective-permute-start | bytes 589832 | tf_op jit(solution)/shard_map/ppermute | solution.py:56
  49.9 8.5 %collective-permute-start.18 = (bf16[4,128,256]{2,1,0:T(8,128)(2,1)S(1)}, bf16[4,128,256]{2,1,0:T(8,128)(2,1)S(1)}, u32[]{:S(2)}, u32[]{:S(2)}) collective-permute-start(bf16[4,128,256]{2,1,0:T(8,128)(2,1)S(1)} %pad_maximum_fusion.refs_0_), channel_id=1, source_target_pairs={{0,192},{1,49},{2,194},{3,51},{4,196},{5,53},{6,198},{7,55},{8,200... | collective-permute-start | bytes 786440 | tf_op jit(solution)/shard_map/ppermute | solution.py:51
  50.3 8.1 %collective-permute-start.17 = (bf16[4,128,256]{2,1,0:T(8,128)(2,1)S(1)}, bf16[4,128,256]{2,1,0:T(8,128)(2,1)S(1)}, u32[]{:S(2)}, u32[]{:S(2)}) collective-permute-start(bf16[4,128,256]{2,1,0:T(8,128)(2,1)S(1)} %pad_maximum_fusion.refs_0_), channel_id=1, source_target_pairs={{0,128},{1,33},{2,130},{3,35},{4,132},{5,37},{6,134},{7,39},{8,136... | collective-permute-start | bytes 786440 | tf_op jit(solution)/shard_map/ppermute | solution.py:51
  50.8 9.3 %collective-permute-start.16 = (bf16[4,128,256]{2,1,0:T(8,128)(2,1)S(1)}, bf16[4,128,256]{2,1,0:T(8,128)(2,1)S(1)}, u32[]{:S(2)}, u32[]{:S(2)}) collective-permute-start(bf16[4,128,256]{2,1,0:T(8,128)(2,1)S(1)} %pad_maximum_fusion.refs_0_), channel_id=1, source_target_pairs={{0,64},{1,17},{2,66},{3,19},{4,68},{5,21},{6,70},{7,23},{8,72},{9,... | collective-permute-start | bytes 786440 | tf_op jit(solution)/shard_map/ppermute | solution.py:51
  51.4 4.5 %collective-permute-start.15 = (bf16[2,32,1536]{2,1,0:T(8,128)(2,1)S(1)}, bf16[2,32,1536]{2,1,0:T(8,128)(2,1)S(1)}, u32[]{:S(2)}, u32[]{:S(2)}) collective-permute-start(bf16[2,32,1536]{2,1,0:T(8,128)(2,1)S(1)} %hold.1.own), channel_id=1, source_target_pairs={{0,14},{1,15},{2,0},{3,1},{4,2},{5,3},{6,4},{7,5},{8,6},{9,7},{10,... | collective-permute-start | bytes 589832 | tf_op jit(solution)/shard_map/ppermute | solution.py:56
  52.4 6.0 %collective-permute-start.14 = (bf16[2,32,1536]{2,1,0:T(8,128)(2,1)S(1)}, bf16[2,32,1536]{2,1,0:T(8,128)(2,1)S(1)}, u32[]{:S(2)}, u32[]{:S(2)}) collective-permute-start(bf16[2,32,1536]{2,1,0:T(8,128)(2,1)S(1)} %hold.1.own), channel_id=1, source_target_pairs={{0,2},{1,3},{2,4},{3,5},{4,6},{5,7},{6,8},{7,9},{8,10},{9,11},{10,... | collective-permute-start | bytes 589832 | tf_op jit(solution)/shard_map/ppermute | solution.py:56
  60.1 7.2 %collective-permute-start.19 = (bf16[4,128,256]{2,1,0:T(8,128)(2,1)S(1)}, bf16[4,128,256]{2,1,0:T(8,128)(2,1)S(1)}, u32[]{:S(2)}, u32[]{:S(2)}) collective-permute-start(bf16[4,128,256]{2,1,0:T(8,128)(2,1)S(1)} %pad_maximum_fusion.refs_0_), channel_id=1, source_target_pairs={{0,1},{1,0},{2,3},{3,2},{4,5},{5,4},{6,7},{7,6},{8,9},{9,8},{10,11... | collective-permute-start | bytes 786440 | tf_op jit(solution)/shard_map/ppermute | solution.py:60
  63.1 4.3 %collective-permute-start.20 = (bf16[4,128,256]{2,1,0:T(8,128)(2,1)S(1)}, bf16[4,128,256]{2,1,0:T(8,128)(2,1)S(1)}, u32[]{:S(2)}, u32[]{:S(2)}) collective-permute-start(bf16[4,128,256]{2,1,0:T(8,128)(2,1)S(1)} %collective-permute-done.16.refs_0_), channel_id=1, source_target_pairs={{0,1},{1,0},{2,3},{3,2},{4,5},{5,4},{6,7},{7,6},{8,9},{9,8},{10,11... | collective-permute-start | bytes 786440 | tf_op jit(solution)/shard_map/ppermute | solution.py:60
  63.1 4.3 %collective-permute-start.21 = (bf16[4,128,256]{2,1,0:T(8,128)(2,1)S(1)}, bf16[4,128,256]{2,1,0:T(8,128)(2,1)S(1)}, u32[]{:S(2)}, u32[]{:S(2)}) collective-permute-start(bf16[4,128,256]{2,1,0:T(8,128)(2,1)S(1)} %collective-permute-done.17.refs_1_), channel_id=1, source_target_pairs={{0,1},{1,0},{2,3},{3,2},{4,5},{5,4},{6,7},{7,6},{8,9},{9,8},{10,11... | collective-permute-start | bytes 786440 | tf_op jit(solution)/shard_map/ppermute | solution.py:60
  63.6 3.8 %collective-permute-start.22 = (bf16[4,128,256]{2,1,0:T(8,128)(2,1)S(1)}, bf16[4,128,256]{2,1,0:T(8,128)(2,1)S(1)}, u32[]{:S(2)}, u32[]{:S(2)}) collective-permute-start(bf16[4,128,256]{2,1,0:T(8,128)(2,1)S(1)} %collective-permute-done.18.refs_2_), channel_id=1, source_target_pairs={{0,1},{1,0},{2,3},{3,2},{4,5},{5,4},{6,7},{7,6},{8,9},{9,8},{10,11... | collective-permute-start | bytes 786440 | tf_op jit(solution)/shard_map/ppermute | solution.py:60
  64.0 3.3 %collective-permute-start.23 = (f32[2,96,128]{2,1,0:T(8,128)S(1)}, f32[2,96,128]{2,1,0:T(8,128)S(1)}, u32[]{:S(2)}, u32[]{:S(2)}) collective-permute-start(f32[2,96,128]{2,1,0:T(8,128)S(1)} %project.1.refs_4_), channel_id=1, source_target_pairs={{0,1},{1,0},{2,3},{3,2},{4,5},{5,4},{6,7},{7,6},{8,9},{9,8},{10,11... | collective-permute-start | bytes 294920 | tf_op jit(solution)/shard_map/ppermute | solution.py:60

commit v4 on v3

--- a/solution.py
+++ b/solution.py
@@ -404,11 +404,10 @@
     columns_far, stack = lax.optimization_barrier((columns_far, stack))
     depth = weighted, translation.shape[1]
     couplings = couple([(0, True, stack)], *depth)
-    couplings, stack, columns_up, columns_down, *arrived = lax.optimization_barrier(
-        (couplings, stack, columns_up, columns_down, *arrived)
-    )
+    couplings, columns_up, columns_down = lax.optimization_barrier((couplings, columns_up, columns_down))
+    projected = project(excitations, [columns, columns_up, columns_down, columns_far])
+    couplings, projected, stack, *arrived = lax.optimization_barrier((couplings, projected, stack, *arrived))
     other = [(leg, False, core_swap(value)) for leg, value in enumerate([stack, *arrived])]
-    projected = project(excitations, [columns, columns_up, columns_down, columns_far])
     came = core_swap(projected)
     couplings = couple([(leg, True, arrived[leg - 1]) for leg in range(1, SIDE)], *depth, couplings)
     couplings, projected = couple(other, *depth, couplings, (projected, came))

time: 71 us -> 70.8 us (level)
  waiting for transfers between devices: 22.5 us -> 8.63 us
  starting transfers between devices: 29.7 us -> 43.3 us
    ppermute x9, waiting for transfers between devices: 12.9 us -> 4.08 us  [plane_send(): sent = {s: lax.ppermute(value, AXES, plane_perm(s, first)) for s in ORDER}]
    ppermute x9, starting transfers between devices: 9.74 us -> 15.4 us  [plane_send(): sent = {s: lax.ppermute(value, AXES, plane_perm(s, first)) for s in ORDER}]
    ppermute x6, waiting for transfers between devices: 8.4 us -> 3.17 us  [depth_send(): return lax.ppermute(value, AXES, depth_perm(shift))]
    ppermute x6, starting transfers between devices: 8.03 us -> 12.2 us  [depth_send(): return lax.ppermute(value, AXES, depth_perm(shift))]
    ppermute x6, starting transfers between devices: 7.33 us -> 11 us  [core_swap(): return lax.ppermute(value, 'row', [(0, 1), (1, 0)])]
  transfers between devices with their start and end apart: 24 -> 24, of which waited for: 14 -> 6; matrix products, arithmetic and copies ran while one was open for 0% -> 0% of each run, Pallas kernels for 15% -> 15%
where the time goes in v4:
time: 70.8 us; the launch traced here: 70.6 us
  starting transfers between devices  43.3 us (61%)
  Pallas kernels  17.8 us (25%)
  waiting for transfers between devices  8.63 us (12%)
  between operations  0.94 us (1%)
    ppermute x9, starting transfers between devices, plane_send(): sent = {s: lax.ppermute(value, AXES, plane_perm(s, first)) for s in ORDER}  15.4 us
    ppermute x6, starting transfers between devices, depth_send(): return lax.ppermute(value, AXES, depth_perm(shift))  12.2 us
    ppermute x6, starting transfers between devices, core_swap(): return lax.ppermute(value, 'row', [(0, 1), (1, 0)])  11 us
    pallas_call x3, Pallas kernels, couple(): pl.pallas_call(kernel, out_shape=shapes, in_specs=in_specs, out_specs=[pl...  7.52 us
    ppermute x3, starting transfers between devices, on_device(): lax.ppermute(routed[s], AXES, plane_perm(s, False))  4.6 us
    ppermute x9, waiting for transfers between devices, plane_send(): sent = {s: lax.ppermute(value, AXES, plane_perm(s, first)) for s in ORDER}  4.08 us
    pallas_call x1, Pallas kernels, weigh(): pl.pallas_call(weigh_kernel, out_shape=pltpu.VMEM((moved, columns * patte...  3.67 us
    ppermute x6, waiting for transfers between devices, depth_send(): return lax.ppermute(value, AXES, depth_perm(shift))  3.17 us
  transfers between devices with their start and end apart: 24, of which 6 were waited for; matrix products, arithmetic and copies ran while one was open for 0% of the time, Pallas kernels for 15%

profile of v4, /device:TPU:1, one launch (start us, length us, event | category | flops | bytes accessed | tf_op | source)
XLA Modules:
  0.0 70.6 jit_solution(12741621760678189674)
XLA Ops:
  0.6 2.6 %pick.1.after.a0 = bf16[3,32,1536]{2,1,0:T(8,128)(2,1)S(1)} custom-call(s32[32]{0:T(128)} %moved_hbm.3, bf16[8,1536,128]{2,1,0:T(8,128)(2,1)} %panels.1), custom_call_target="tpu_custom_call" | custom-call | tf_op jit(solution)/shard_map/pick/pallas_call | solution.py:101
  3.2 2.2 %collective-permute-start = (bf16[3,32,1536]{2,1,0:T(8,128)(2,1)S(1)}, bf16[3,32,1536]{2,1,0:T(8,128)(2,1)S(1)}, u32[]{:S(2)}, u32[]{:S(2)}) collective-permute-start(bf16[3,32,1536]{2,1,0:T(8,128)(2,1)S(1)} %pick.1.after.a0), channel_id=1, source_target_pairs={{0,16},{1,65},{2,18},{3,67},{4,20},{5,69},{6,22},{7,71},{8,24},{9,... | collective-permute-start | bytes 884744 | tf_op jit(solution)/shard_map/ppermute | solution.py:51
  5.4 2.6 %collective-permute-start.1 = (bf16[3,32,1536]{2,1,0:T(8,128)(2,1)S(1)}, bf16[3,32,1536]{2,1,0:T(8,128)(2,1)S(1)}, u32[]{:S(2)}, u32[]{:S(2)}) collective-permute-start(bf16[3,32,1536]{2,1,0:T(8,128)(2,1)S(1)} %pick.1.after.a0), channel_id=1, source_target_pairs={{0,32},{1,129},{2,34},{3,131},{4,36},{5,133},{6,38},{7,135},{8,40}... | collective-permute-start | bytes 884744 | tf_op jit(solution)/shard_map/ppermute | solution.py:51
  8.0 1.1 %collective-permute-start.2 = (bf16[3,32,1536]{2,1,0:T(8,128)(2,1)S(1)}, bf16[3,32,1536]{2,1,0:T(8,128)(2,1)S(1)}, u32[]{:S(2)}, u32[]{:S(2)}) collective-permute-start(bf16[3,32,1536]{2,1,0:T(8,128)(2,1)S(1)} %pick.1.after.a0), channel_id=1, source_target_pairs={{0,48},{1,193},{2,50},{3,195},{4,52},{5,197},{6,54},{7,199},{8,56}... | collective-permute-start | bytes 884744 | tf_op jit(solution)/shard_map/ppermute | solution.py:51
  9.1 2.4 %stage.1 = (s32[8]{0:T(128)S(1)}, bf16[2,1536,256]{2,1,0:T(8,128)(2,1)S(1)}, f32[32,16,256]{2,1,0:T(8,128)S(1)}, bf16[8,64,256]{2,1,0:T(8,128)(2,1)S(1)}, bf16[2...) custom-call(bf16[3,32,1536]{2,1,0:T(8,128)(2,1)S(1)} %pick.1.after.a0, s32[32]{0:T(128)} %moved_hbm.3, ...), custom_call_target="tpu_custom_call" | custom-call | tf_op jit(solution)/shard_map/stage/pallas_call | solution.py:155
  11.5 0.0 collective-permute-done.a1
  11.5 4.1 %collective-permute-done.1.a2 = bf16[3,32,1536]{2,1,0:T(8,128)(2,1)S(1)} collective-permute-done((bf16[3,32,1536]{2,1,0:T(8,128)(2,1)S(1)}, bf16[3,32,1536]{2,1,0:T(8,128)(2,1)S(1)}, u32[]{:S(2)}, u32[]{:S(2)}) %collective-permute-start.1) | collective-permute-done | bytes 294944 | tf_op jit(solution)/shard_map/ppermute | solution.py:51
  15.6 0.0 collective-permute-done.2.a3
  15.6 0.8 %route.1 = (bf16[2,32,1536]{2,1,0:T(8,128)(2,1)S(1)}, bf16[2,32,1536]{2,1,0:T(8,128)(2,1)S(1)}, bf16[2,32,1536]{2,1,0:T(8,128)(2,1)S(1)}, bf16[2,32,1536]{2,1,0:T(8,128)(2,1)S(1)}) custom-call(s32[8]{0:T(128)S(1)} %get-tuple-element.38.table, bf16[3,32,1536]{2,1,0:T(8,128)(2,1)S(1)} %pick.1.after.a0, bf16[3,32,1536]{2,1,0:T(8,128)(2,1)S(1)} %collective-permute-done.a1, ...), custom_call_target="tpu_custom_call" | custom-call | tf_op jit(solution)/shard_map/route/pallas_call | solution.py:187
  16.4 1.0 %collective-permute-start.3 = (bf16[2,32,1536]{2,1,0:T(8,128)(2,1)S(1)}, bf16[2,32,1536]{2,1,0:T(8,128)(2,1)S(1)}, u32[]{:S(2)}, u32[]{:S(2)}) collective-permute-start(bf16[2,32,1536]{2,1,0:T(8,128)(2,1)S(1)} %get-tuple-element.43), channel_id=1, source_target_pairs={{0,64},{1,17},{2,66},{3,19},{4,68},{5,21},{6,70},{7,23},{8,72},{9,... | collective-permute-start | bytes 589832 | tf_op jit(solution)/shard_map/ppermute | solution.py:391
  17.3 2.5 %collective-permute-start.4 = (bf16[2,32,1536]{2,1,0:T(8,128)(2,1)S(1)}, bf16[2,32,1536]{2,1,0:T(8,128)(2,1)S(1)}, u32[]{:S(2)}, u32[]{:S(2)}) collective-permute-start(bf16[2,32,1536]{2,1,0:T(8,128)(2,1)S(1)} %get-tuple-element.44), channel_id=1, source_target_pairs={{0,128},{1,33},{2,130},{3,35},{4,132},{5,37},{6,134},{7,39},{8,136... | collective-permute-start | bytes 589832 | tf_op jit(solution)/shard_map/ppermute | solution.py:391
  19.8 1.2 %collective-permute-start.5 = (bf16[2,32,1536]{2,1,0:T(8,128)(2,1)S(1)}, bf16[2,32,1536]{2,1,0:T(8,128)(2,1)S(1)}, u32[]{:S(2)}, u32[]{:S(2)}) collective-permute-start(bf16[2,32,1536]{2,1,0:T(8,128)(2,1)S(1)} %get-tuple-element.45), channel_id=1, source_target_pairs={{0,192},{1,49},{2,194},{3,51},{4,196},{5,53},{6,198},{7,55},{8,200... | collective-permute-start | bytes 589832 | tf_op jit(solution)/shard_map/ppermute | solution.py:391
  21.0 3.7 %weigh.1.weights = bf16[32,1024,256]{2,1,0:T(8,128)(2,1)S(1)} custom-call(s32[16,32]{1,0:T(8,128)S(1)} %get-tuple-element.34.partners, f32[32,16,256]{2,1,0:T(8,128)S(1)} %get-tuple-element.35.trans, bf16[8,64,256]{2,1,0:T(8,128)(2,1)S(1)} %get-tuple-element.36.patt, bf16[2,32,1536]{2,1,0:T(8,128)(2,1)S(1)} %get-tuple-element.42.after.a0), custom_call_target="tpu_custom_call" | custom-call | tf_op jit(solution)/shard_map/weigh/pallas_call | solution.py:259
  24.6 0.0 collective-permute-done.3.a1
  24.6 0.3 collective-permute-done.4.a2
  25.0 0.2 collective-permute-done.5.a3
  25.1 0.4 radiate.1
  25.5 4.1 %collective-permute-start.6 = (f32[32,256]{1,0:T(8,128)S(1)}, f32[32,256]{1,0:T(8,128)S(1)}, u32[]{:S(2)}, u32[]{:S(2)}) collective-permute-start(f32[32,256]{1,0:T(8,128)S(1)} %get-tuple-element.53), channel_id=1, source_target_pairs={{0,1},{1,0},{2,3},{3,2},{4,5},{5,4},{6,7},{7,6},{8,9},{9,8},{10,11... | collective-permute-start | bytes 98312 | tf_op jit(solution)/shard_map/ppermute | solution.py:60
  29.6 0.9 %collective-permute-done.6 = f32[32,256]{1,0:T(8,128)S(1)} collective-permute-done((f32[32,256]{1,0:T(8,128)S(1)}, f32[32,256]{1,0:T(8,128)S(1)}, u32[]{:S(2)}, u32[]{:S(2)}) %collective-permute-start.6) | collective-permute-done | bytes 32800 | tf_op jit(solution)/shard_map/ppermute | solution.py:60
  30.5 0.4 collective-permute-start.7
  30.8 4.0 %collective-permute-start.8 = (bf16[32,256]{1,0:T(8,128)(2,1)S(1)}, bf16[32,256]{1,0:T(8,128)(2,1)S(1)}, u32[]{:S(2)}, u32[]{:S(2)}) collective-permute-start(bf16[32,256]{1,0:T(8,128)(2,1)S(1)} %add_convert_fusion.own), channel_id=1, source_target_pairs={{0,14},{1,15},{2,0},{3,1},{4,2},{5,3},{6,4},{7,5},{8,6},{9,7},{10,... | collective-permute-start | bytes 49160 | tf_op jit(solution)/shard_map/ppermute | solution.py:56
  34.9 1.8 %collective-permute-start.9 = (bf16[32,256]{1,0:T(8,128)(2,1)S(1)}, bf16[32,256]{1,0:T(8,128)(2,1)S(1)}, u32[]{:S(2)}, u32[]{:S(2)}) collective-permute-start(bf16[32,256]{1,0:T(8,128)(2,1)S(1)} %add_convert_fusion.own), channel_id=1, source_target_pairs={{0,4},{1,13},{2,6},{3,15},{4,8},{5,1},{6,10},{7,3},{8,12},{9,5},{1... | collective-permute-start | bytes 49160 | tf_op jit(solution)/shard_map/ppermute | solution.py:56
  36.7 0.0 collective-permute-done.7.up
  36.7 0.0 collective-permute-done.8.down
  36.7 1.7 %collective-permute-done.9.far = bf16[32,256]{1,0:T(8,128)(2,1)S(1)} collective-permute-done((bf16[32,256]{1,0:T(8,128)(2,1)S(1)}, bf16[32,256]{1,0:T(8,128)(2,1)S(1)}, u32[]{:S(2)}, u32[]{:S(2)}) %collective-permute-start.9) | collective-permute-done | bytes 16416 | tf_op jit(solution)/shard_map/ppermute | solution.py:56
  38.4 1.4 %collective-permute-start.11 = (bf16[128,256]{1,0:T(8,128)(2,1)S(1)}, bf16[128,256]{1,0:T(8,128)(2,1)S(1)}, u32[]{:S(2)}, u32[]{:S(2)}) collective-permute-start(bf16[128,256]{1,0:T(8,128)(2,1)S(1)} %assemble.1.after), channel_id=1, source_target_pairs={{0,16},{1,65},{2,18},{3,67},{4,20},{5,69},{6,22},{7,71},{8,24},{9,... | collective-permute-start | bytes 196616 | tf_op jit(solution)/shard_map/ppermute | solution.py:51
  39.8 2.0 %collective-permute-start.12 = (bf16[128,256]{1,0:T(8,128)(2,1)S(1)}, bf16[128,256]{1,0:T(8,128)(2,1)S(1)}, u32[]{:S(2)}, u32[]{:S(2)}) collective-permute-start(bf16[128,256]{1,0:T(8,128)(2,1)S(1)} %assemble.1.after), channel_id=1, source_target_pairs={{0,32},{1,129},{2,34},{3,131},{4,36},{5,133},{6,38},{7,135},{8,40}... | collective-permute-start | bytes 196616 | tf_op jit(solution)/shard_map/ppermute | solution.py:51
  41.8 1.3 %collective-permute-start.13 = (bf16[128,256]{1,0:T(8,128)(2,1)S(1)}, bf16[128,256]{1,0:T(8,128)(2,1)S(1)}, u32[]{:S(2)}, u32[]{:S(2)}) collective-permute-start(bf16[128,256]{1,0:T(8,128)(2,1)S(1)} %assemble.1.after), channel_id=1, source_target_pairs={{0,48},{1,193},{2,50},{3,195},{4,52},{5,197},{6,54},{7,199},{8,56}... | collective-permute-start | bytes 196616 | tf_op jit(solution)/shard_map/ppermute | solution.py:51
  43.1 3.0 %collective-permute-start.10 = (bf16[2,32,1536]{2,1,0:T(8,128)(2,1)S(1)}, bf16[2,32,1536]{2,1,0:T(8,128)(2,1)S(1)}, u32[]{:S(2)}, u32[]{:S(2)}) collective-permute-start(bf16[2,32,1536]{2,1,0:T(8,128)(2,1)S(1)} %hold.1.own), channel_id=1, source_target_pairs={{0,4},{1,13},{2,6},{3,15},{4,8},{5,1},{6,10},{7,3},{8,12},{9,5},{1... | collective-permute-start | bytes 589832 | tf_op jit(solution)/shard_map/ppermute | solution.py:56
  46.1 0.0 collective-permute-done.11
  46.1 0.0 collective-permute-done.12
  46.1 0.0 collective-permute-done.13
  46.2 1.7 %collective-permute-start.16 = (bf16[4,128,256]{2,1,0:T(8,128)(2,1)S(1)}, bf16[4,128,256]{2,1,0:T(8,128)(2,1)S(1)}, u32[]{:S(2)}, u32[]{:S(2)}) collective-permute-start(bf16[4,128,256]{2,1,0:T(8,128)(2,1)S(1)} %pad_maximum_fusion.refs_0_), channel_id=1, source_target_pairs={{0,64},{1,17},{2,66},{3,19},{4,68},{5,21},{6,70},{7,23},{8,72},{9,... | collective-permute-start | bytes 786440 | tf_op jit(solution)/shard_map/ppermute | solution.py:51
  47.9 1.8 %collective-permute-start.17 = (bf16[4,128,256]{2,1,0:T(8,128)(2,1)S(1)}, bf16[4,128,256]{2,1,0:T(8,128)(2,1)S(1)}, u32[]{:S(2)}, u32[]{:S(2)}) collective-permute-start(bf16[4,128,256]{2,1,0:T(8,128)(2,1)S(1)} %pad_maximum_fusion.refs_0_), channel_id=1, source_target_pairs={{0,128},{1,33},{2,130},{3,35},{4,132},{5,37},{6,134},{7,39},{8,136... | collective-permute-start | bytes 786440 | tf_op jit(solution)/shard_map/ppermute | solution.py:51
  49.7 1.3 %collective-permute-start.18 = (bf16[4,128,256]{2,1,0:T(8,128)(2,1)S(1)}, bf16[4,128,256]{2,1,0:T(8,128)(2,1)S(1)}, u32[]{:S(2)}, u32[]{:S(2)}) collective-permute-start(bf16[4,128,256]{2,1,0:T(8,128)(2,1)S(1)} %pad_maximum_fusion.refs_0_), channel_id=1, source_target_pairs={{0,192},{1,49},{2,194},{3,51},{4,196},{5,53},{6,198},{7,55},{8,200... | collective-permute-start | bytes 786440 | tf_op jit(solution)/shard_map/ppermute | solution.py:51
  51.0 0.7 %collective-permute-start.14 = (bf16[2,32,1536]{2,1,0:T(8,128)(2,1)S(1)}, bf16[2,32,1536]{2,1,0:T(8,128)(2,1)S(1)}, u32[]{:S(2)}, u32[]{:S(2)}) collective-permute-start(bf16[2,32,1536]{2,1,0:T(8,128)(2,1)S(1)} %hold.1.own), channel_id=1, source_target_pairs={{0,2},{1,3},{2,4},{3,5},{4,6},{5,7},{6,8},{7,9},{8,10},{9,11},{10,... | collective-permute-start | bytes 589832 | tf_op jit(solution)/shard_map/ppermute | solution.py:56
  51.7 0.0 collective-permute-done.10.far
  51.7 2.2 %collective-permute-start.15 = (bf16[2,32,1536]{2,1,0:T(8,128)(2,1)S(1)}, bf16[2,32,1536]{2,1,0:T(8,128)(2,1)S(1)}, u32[]{:S(2)}, u32[]{:S(2)}) collective-permute-start(bf16[2,32,1536]{2,1,0:T(8,128)(2,1)S(1)} %hold.1.own), channel_id=1, source_target_pairs={{0,14},{1,15},{2,0},{3,1},{4,2},{5,3},{6,4},{7,5},{8,6},{9,7},{10,... | collective-permute-start | bytes 589832 | tf_op jit(solution)/shard_map/ppermute | solution.py:56
  54.0 1.5 %couple.3.refs_3_ = bf16[32,16,64,128]{3,2,1,0:T(8,128)(2,1)} custom-call(bf16[32,1024,256]{2,1,0:T(8,128)(2,1)S(1)} %weigh.1.weights, bf16[4,128,256]{2,1,0:T(8,128)(2,1)S(1)} %pad_maximum_fusion.refs_0_), custom_call_target="tpu_custom_call" | custom-call | flops 268435456 | bytes 1048576 | tf_op jit(solution)/shard_map/couple/pallas_call | solution.py:327
  55.5 1.5 %collective-permute-done.14.up = bf16[2,32,1536]{2,1,0:T(8,128)(2,1)S(1)} collective-permute-done((bf16[2,32,1536]{2,1,0:T(8,128)(2,1)S(1)}, bf16[2,32,1536]{2,1,0:T(8,128)(2,1)S(1)}, u32[]{:S(2)}, u32[]{:S(2)}) %collective-permute-start.14) | collective-permute-done | bytes 196640 | tf_op jit(solution)/shard_map/ppermute | solution.py:56
  57.0 0.0 collective-permute-done.15.down
  57.0 0.4 project.1.refs_4_
  57.4 0.0 collective-permute-done.16.refs_0_
  57.5 0.0 collective-permute-done.17.refs_1_
  57.5 0.0 collective-permute-done.18.refs_2_
  57.5 5.9 %collective-permute-start.19 = (bf16[4,128,256]{2,1,0:T(8,128)(2,1)S(1)}, bf16[4,128,256]{2,1,0:T(8,128)(2,1)S(1)}, u32[]{:S(2)}, u32[]{:S(2)}) collective-permute-start(bf16[4,128,256]{2,1,0:T(8,128)(2,1)S(1)} %pad_maximum_fusion.refs_0_), channel_id=1, source_target_pairs={{0,1},{1,0},{2,3},{3,2},{4,5},{5,4},{6,7},{7,6},{8,9},{9,8},{10,11... | collective-permute-start | bytes 786440 | tf_op jit(solution)/shard_map/ppermute | solution.py:60
  63.4 0.1 collective-permute-start.20
  63.5 0.4 collective-permute-start.21
  63.9 0.1 collective-permute-start.22
  64.0 0.4 collective-permute-start.23
  64.4 2.7 %couple.4.refs_6_ = bf16[32,16,64,128]{3,2,1,0:T(8,128)(2,1)} custom-call(bf16[32,1024,256]{2,1,0:T(8,128)(2,1)S(1)} %weigh.1.weights, bf16[4,128,256]{2,1,0:T(8,128)(2,1)S(1)} %collective-permute-done.16.refs_0_, bf16[4,128,256]{2,1,0:T(8,128)(2,1)S(1)} %collective-permute-done.17.refs_1_, ...), custom_call_target="tpu_custom_call", output_to_operand_aliasing={{}: (4, {})} | custom-call | flops 805306368 | bytes 3145728 | tf_op jit(solution)/shard_map/couple/pallas_call | solution.py:327
  67.1 0.0 collective-permute-done.23.refs_5_
  67.1 0.0 collective-permute-done.19.refs_0_
  67.1 0.0 collective-permute-done.20.refs_1_
  67.2 0.0 collective-permute-done.21.refs_2_
  67.2 0.0 collective-permute-done.22.refs_3_
  67.2 3.3 %couple.5 = (bf16[32,16,64,128]{3,2,1,0:T(8,128)(2,1)}, f32[2,96,128]{2,1,0:T(8,128)}) custom-call(bf16[32,1024,256]{2,1,0:T(8,128)(2,1)S(1)} %weigh.1.weights, bf16[4,128,256]{2,1,0:T(8,128)(2,1)S(1)} %collective-permute-done.19.refs_0_, bf16[4,128,256]{2,1,0:T(8,128)(2,1)S(1)} %collective-permute-done.20.refs_1_, ...), custom_call_target="tpu_custom_call", output_to_operand_aliasing={{0}: (7, {})} | custom-call | flops 1073741824 | bytes 4194304 | tf_op jit(solution)/shard_map/couple/pallas_call | solution.py:327
  (4 shorter events, 0.1 us)
Async XLA Ops:
  3.2 8.3 %collective-permute-start = (bf16[3,32,1536]{2,1,0:T(8,128)(2,1)S(1)}, bf16[3,32,1536]{2,1,0:T(8,128)(2,1)S(1)}, u32[]{:S(2)}, u32[]{:S(2)}) collective-permute-start(bf16[3,32,1536]{2,1,0:T(8,128)(2,1)S(1)} %pick.1.after.a0), channel_id=1, source_target_pairs={{0,16},{1,65},{2,18},{3,67},{4,20},{5,69},{6,22},{7,71},{8,24},{9,... | collective-permute-start | bytes 884744 | tf_op jit(solution)/shard_map/ppermute | solution.py:51
  5.4 10.2 %collective-permute-start.1 = (bf16[3,32,1536]{2,1,0:T(8,128)(2,1)S(1)}, bf16[3,32,1536]{2,1,0:T(8,128)(2,1)S(1)}, u32[]{:S(2)}, u32[]{:S(2)}) collective-permute-start(bf16[3,32,1536]{2,1,0:T(8,128)(2,1)S(1)} %pick.1.after.a0), channel_id=1, source_target_pairs={{0,32},{1,129},{2,34},{3,131},{4,36},{5,133},{6,38},{7,135},{8,40}... | collective-permute-start | bytes 884744 | tf_op jit(solution)/shard_map/ppermute | solution.py:51
  8.0 7.6 %collective-permute-start.2 = (bf16[3,32,1536]{2,1,0:T(8,128)(2,1)S(1)}, bf16[3,32,1536]{2,1,0:T(8,128)(2,1)S(1)}, u32[]{:S(2)}, u32[]{:S(2)}) collective-permute-start(bf16[3,32,1536]{2,1,0:T(8,128)(2,1)S(1)} %pick.1.after.a0), channel_id=1, source_target_pairs={{0,48},{1,193},{2,50},{3,195},{4,52},{5,197},{6,54},{7,199},{8,56}... | collective-permute-start | bytes 884744 | tf_op jit(solution)/shard_map/ppermute | solution.py:51
  16.4 8.3 %collective-permute-start.3 = (bf16[2,32,1536]{2,1,0:T(8,128)(2,1)S(1)}, bf16[2,32,1536]{2,1,0:T(8,128)(2,1)S(1)}, u32[]{:S(2)}, u32[]{:S(2)}) collective-permute-start(bf16[2,32,1536]{2,1,0:T(8,128)(2,1)S(1)} %get-tuple-element.43), channel_id=1, source_target_pairs={{0,64},{1,17},{2,66},{3,19},{4,68},{5,21},{6,70},{7,23},{8,72},{9,... | collective-permute-start | bytes 589832 | tf_op jit(solution)/shard_map/ppermute | solution.py:391
  17.3 7.6 %collective-permute-start.4 = (bf16[2,32,1536]{2,1,0:T(8,128)(2,1)S(1)}, bf16[2,32,1536]{2,1,0:T(8,128)(2,1)S(1)}, u32[]{:S(2)}, u32[]{:S(2)}) collective-permute-start(bf16[2,32,1536]{2,1,0:T(8,128)(2,1)S(1)} %get-tuple-element.44), channel_id=1, source_target_pairs={{0,128},{1,33},{2,130},{3,35},{4,132},{5,37},{6,134},{7,39},{8,136... | collective-permute-start | bytes 589832 | tf_op jit(solution)/shard_map/ppermute | solution.py:391
  19.8 5.3 %collective-permute-start.5 = (bf16[2,32,1536]{2,1,0:T(8,128)(2,1)S(1)}, bf16[2,32,1536]{2,1,0:T(8,128)(2,1)S(1)}, u32[]{:S(2)}, u32[]{:S(2)}) collective-permute-start(bf16[2,32,1536]{2,1,0:T(8,128)(2,1)S(1)} %get-tuple-element.45), channel_id=1, source_target_pairs={{0,192},{1,49},{2,194},{3,51},{4,196},{5,53},{6,198},{7,55},{8,200... | collective-permute-start | bytes 589832 | tf_op jit(solution)/shard_map/ppermute | solution.py:391
  25.5 4.9 %collective-permute-start.6 = (f32[32,256]{1,0:T(8,128)S(1)}, f32[32,256]{1,0:T(8,128)S(1)}, u32[]{:S(2)}, u32[]{:S(2)}) collective-permute-start(f32[32,256]{1,0:T(8,128)S(1)} %get-tuple-element.53), channel_id=1, source_target_pairs={{0,1},{1,0},{2,3},{3,2},{4,5},{5,4},{6,7},{7,6},{8,9},{9,8},{10,11... | collective-permute-start | bytes 98312 | tf_op jit(solution)/shard_map/ppermute | solution.py:60
  30.5 6.2 %collective-permute-start.7 = (bf16[32,256]{1,0:T(8,128)(2,1)S(1)}, bf16[32,256]{1,0:T(8,128)(2,1)S(1)}, u32[]{:S(2)}, u32[]{:S(2)}) collective-permute-start(bf16[32,256]{1,0:T(8,128)(2,1)S(1)} %add_convert_fusion.own), channel_id=1, source_target_pairs={{0,2},{1,3},{2,4},{3,5},{4,6},{5,7},{6,8},{7,9},{8,10},{9,11},{10,... | collective-permute-start | bytes 49160 | tf_op jit(solution)/shard_map/ppermute | solution.py:56
  30.8 5.9 %collective-permute-start.8 = (bf16[32,256]{1,0:T(8,128)(2,1)S(1)}, bf16[32,256]{1,0:T(8,128)(2,1)S(1)}, u32[]{:S(2)}, u32[]{:S(2)}) collective-permute-start(bf16[32,256]{1,0:T(8,128)(2,1)S(1)} %add_convert_fusion.own), channel_id=1, source_target_pairs={{0,14},{1,15},{2,0},{3,1},{4,2},{5,3},{6,4},{7,5},{8,6},{9,7},{10,... | collective-permute-start | bytes 49160 | tf_op jit(solution)/shard_map/ppermute | solution.py:56
  34.9 3.5 %collective-permute-start.9 = (bf16[32,256]{1,0:T(8,128)(2,1)S(1)}, bf16[32,256]{1,0:T(8,128)(2,1)S(1)}, u32[]{:S(2)}, u32[]{:S(2)}) collective-permute-start(bf16[32,256]{1,0:T(8,128)(2,1)S(1)} %add_convert_fusion.own), channel_id=1, source_target_pairs={{0,4},{1,13},{2,6},{3,15},{4,8},{5,1},{6,10},{7,3},{8,12},{9,5},{1... | collective-permute-start | bytes 49160 | tf_op jit(solution)/shard_map/ppermute | solution.py:56
  38.4 7.8 %collective-permute-start.11 = (bf16[128,256]{1,0:T(8,128)(2,1)S(1)}, bf16[128,256]{1,0:T(8,128)(2,1)S(1)}, u32[]{:S(2)}, u32[]{:S(2)}) collective-permute-start(bf16[128,256]{1,0:T(8,128)(2,1)S(1)} %assemble.1.after), channel_id=1, source_target_pairs={{0,16},{1,65},{2,18},{3,67},{4,20},{5,69},{6,22},{7,71},{8,24},{9,... | collective-permute-start | bytes 196616 | tf_op jit(solution)/shard_map/ppermute | solution.py:51
  39.8 6.3 %collective-permute-start.12 = (bf16[128,256]{1,0:T(8,128)(2,1)S(1)}, bf16[128,256]{1,0:T(8,128)(2,1)S(1)}, u32[]{:S(2)}, u32[]{:S(2)}) collective-permute-start(bf16[128,256]{1,0:T(8,128)(2,1)S(1)} %assemble.1.after), channel_id=1, source_target_pairs={{0,32},{1,129},{2,34},{3,131},{4,36},{5,133},{6,38},{7,135},{8,40}... | collective-permute-start | bytes 196616 | tf_op jit(solution)/shard_map/ppermute | solution.py:51
  41.8 4.3 %collective-permute-start.13 = (bf16[128,256]{1,0:T(8,128)(2,1)S(1)}, bf16[128,256]{1,0:T(8,128)(2,1)S(1)}, u32[]{:S(2)}, u32[]{:S(2)}) collective-permute-start(bf16[128,256]{1,0:T(8,128)(2,1)S(1)} %assemble.1.after), channel_id=1, source_target_pairs={{0,48},{1,193},{2,50},{3,195},{4,52},{5,197},{6,54},{7,199},{8,56}... | collective-permute-start | bytes 196616 | tf_op jit(solution)/shard_map/ppermute | solution.py:51
  43.1 8.6 %collective-permute-start.10 = (bf16[2,32,1536]{2,1,0:T(8,128)(2,1)S(1)}, bf16[2,32,1536]{2,1,0:T(8,128)(2,1)S(1)}, u32[]{:S(2)}, u32[]{:S(2)}) collective-permute-start(bf16[2,32,1536]{2,1,0:T(8,128)(2,1)S(1)} %hold.1.own), channel_id=1, source_target_pairs={{0,4},{1,13},{2,6},{3,15},{4,8},{5,1},{6,10},{7,3},{8,12},{9,5},{1... | collective-permute-start | bytes 589832 | tf_op jit(solution)/shard_map/ppermute | solution.py:56
  46.2 11.3 %collective-permute-start.16 = (bf16[4,128,256]{2,1,0:T(8,128)(2,1)S(1)}, bf16[4,128,256]{2,1,0:T(8,128)(2,1)S(1)}, u32[]{:S(2)}, u32[]{:S(2)}) collective-permute-start(bf16[4,128,256]{2,1,0:T(8,128)(2,1)S(1)} %pad_maximum_fusion.refs_0_), channel_id=1, source_target_pairs={{0,64},{1,17},{2,66},{3,19},{4,68},{5,21},{6,70},{7,23},{8,72},{9,... | collective-permute-start | bytes 786440 | tf_op jit(solution)/shard_map/ppermute | solution.py:51
  47.9 9.6 %collective-permute-start.17 = (bf16[4,128,256]{2,1,0:T(8,128)(2,1)S(1)}, bf16[4,128,256]{2,1,0:T(8,128)(2,1)S(1)}, u32[]{:S(2)}, u32[]{:S(2)}) collective-permute-start(bf16[4,128,256]{2,1,0:T(8,128)(2,1)S(1)} %pad_maximum_fusion.refs_0_), channel_id=1, source_target_pairs={{0,128},{1,33},{2,130},{3,35},{4,132},{5,37},{6,134},{7,39},{8,136... | collective-permute-start | bytes 786440 | tf_op jit(solution)/shard_map/ppermute | solution.py:51
  49.7 7.8 %collective-permute-start.18 = (bf16[4,128,256]{2,1,0:T(8,128)(2,1)S(1)}, bf16[4,128,256]{2,1,0:T(8,128)(2,1)S(1)}, u32[]{:S(2)}, u32[]{:S(2)}) collective-permute-start(bf16[4,128,256]{2,1,0:T(8,128)(2,1)S(1)} %pad_maximum_fusion.refs_0_), channel_id=1, source_target_pairs={{0,192},{1,49},{2,194},{3,51},{4,196},{5,53},{6,198},{7,55},{8,200... | collective-permute-start | bytes 786440 | tf_op jit(solution)/shard_map/ppermute | solution.py:51
  51.0 6.0 %collective-permute-start.14 = (bf16[2,32,1536]{2,1,0:T(8,128)(2,1)S(1)}, bf16[2,32,1536]{2,1,0:T(8,128)(2,1)S(1)}, u32[]{:S(2)}, u32[]{:S(2)}) collective-permute-start(bf16[2,32,1536]{2,1,0:T(8,128)(2,1)S(1)} %hold.1.own), channel_id=1, source_target_pairs={{0,2},{1,3},{2,4},{3,5},{4,6},{5,7},{6,8},{7,9},{8,10},{9,11},{10,... | collective-permute-start | bytes 589832 | tf_op jit(solution)/shard_map/ppermute | solution.py:56
  51.7 5.3 %collective-permute-start.15 = (bf16[2,32,1536]{2,1,0:T(8,128)(2,1)S(1)}, bf16[2,32,1536]{2,1,0:T(8,128)(2,1)S(1)}, u32[]{:S(2)}, u32[]{:S(2)}) collective-permute-start(bf16[2,32,1536]{2,1,0:T(8,128)(2,1)S(1)} %hold.1.own), channel_id=1, source_target_pairs={{0,14},{1,15},{2,0},{3,1},{4,2},{5,3},{6,4},{7,5},{8,6},{9,7},{10,... | collective-permute-start | bytes 589832 | tf_op jit(solution)/shard_map/ppermute | solution.py:56
  57.5 9.7 %collective-permute-start.19 = (bf16[4,128,256]{2,1,0:T(8,128)(2,1)S(1)}, bf16[4,128,256]{2,1,0:T(8,128)(2,1)S(1)}, u32[]{:S(2)}, u32[]{:S(2)}) collective-permute-start(bf16[4,128,256]{2,1,0:T(8,128)(2,1)S(1)} %pad_maximum_fusion.refs_0_), channel_id=1, source_target_pairs={{0,1},{1,0},{2,3},{3,2},{4,5},{5,4},{6,7},{7,6},{8,9},{9,8},{10,11... | collective-permute-start | bytes 786440 | tf_op jit(solution)/shard_map/ppermute | solution.py:60
  63.4 3.7 %collective-permute-start.20 = (bf16[4,128,256]{2,1,0:T(8,128)(2,1)S(1)}, bf16[4,128,256]{2,1,0:T(8,128)(2,1)S(1)}, u32[]{:S(2)}, u32[]{:S(2)}) collective-permute-start(bf16[4,128,256]{2,1,0:T(8,128)(2,1)S(1)} %collective-permute-done.16.refs_0_), channel_id=1, source_target_pairs={{0,1},{1,0},{2,3},{3,2},{4,5},{5,4},{6,7},{7,6},{8,9},{9,8},{10,11... | collective-permute-start | bytes 786440 | tf_op jit(solution)/shard_map/ppermute | solution.py:60
  63.5 3.7 %collective-permute-start.21 = (bf16[4,128,256]{2,1,0:T(8,128)(2,1)S(1)}, bf16[4,128,256]{2,1,0:T(8,128)(2,1)S(1)}, u32[]{:S(2)}, u32[]{:S(2)}) collective-permute-start(bf16[4,128,256]{2,1,0:T(8,128)(2,1)S(1)} %collective-permute-done.17.refs_1_), channel_id=1, source_target_pairs={{0,1},{1,0},{2,3},{3,2},{4,5},{5,4},{6,7},{7,6},{8,9},{9,8},{10,11... | collective-permute-start | bytes 786440 | tf_op jit(solution)/shard_map/ppermute | solution.py:60
  63.9 3.3 %collective-permute-start.22 = (bf16[4,128,256]{2,1,0:T(8,128)(2,1)S(1)}, bf16[4,128,256]{2,1,0:T(8,128)(2,1)S(1)}, u32[]{:S(2)}, u32[]{:S(2)}) collective-permute-start(bf16[4,128,256]{2,1,0:T(8,128)(2,1)S(1)} %collective-permute-done.18.refs_2_), channel_id=1, source_target_pairs={{0,1},{1,0},{2,3},{3,2},{4,5},{5,4},{6,7},{7,6},{8,9},{9,8},{10,11... | collective-permute-start | bytes 786440 | tf_op jit(solution)/shard_map/ppermute | solution.py:60
  64.0 3.1 %collective-permute-start.23 = (f32[2,96,128]{2,1,0:T(8,128)S(1)}, f32[2,96,128]{2,1,0:T(8,128)S(1)}, u32[]{:S(2)}, u32[]{:S(2)}) collective-permute-start(f32[2,96,128]{2,1,0:T(8,128)S(1)} %project.1.refs_4_), channel_id=1, source_target_pairs={{0,1},{1,0},{2,3},{3,2},{4,5},{5,4},{6,7},{7,6},{8,9},{9,8},{10,11... | collective-permute-start | bytes 294920 | tf_op jit(solution)/shard_map/ppermute | solution.py:60
